TPU v7x, 32 devices: a whole 2x2x4 slice. The times are simulated.
32 devices in a mesh: dp: 16 (over z, x, core), fsdp: 2 (over y).
Axes of the slice: x: 2, y: 2, z: 4, core: 2. Of those that a mesh axis runs over, the one named last changes fastest.
Arguments:
- tokens: bfloat16 [32768, 1024], P(('dp', 'fsdp')), may hold values from -6 to 6
- doc_split: int32 [32], P(('dp', 'fsdp')), may hold values from 512 to 1024, as said below
- head_scale: float32 [16], replicated, may hold values from 0.5 to 1.5
- query_key_value_weight: bfloat16 [1024, 3072], P(('dp', 'fsdp')), may hold values from -0.25 to 0.25
- output_weight: bfloat16 [1024, 1024], P(('dp', 'fsdp')), may hold values from -0.1875 to 0.1875
- first_weight: bfloat16 [1024, 4096], P(('dp', 'fsdp')), may hold values from -0.1875 to 0.1875
- second_weight: bfloat16 [4096, 1024], P(('dp', 'fsdp')), may hold values from -0.09375 to 0.09375
- model_vectors: bfloat16 [10, 1024], P(None, ('dp', 'fsdp')), may hold values from -0.59375 to 1.5, as said below
- hidden_vectors: bfloat16 [3, 4096], P(None, ('dp', 'fsdp')), may hold values from -0.59375 to 1.5, as said below
- cotangent: bfloat16 [32768, 1024], P(('dp', 'fsdp')), may hold values from -6 to 6
Outputs:
- output: bfloat16 [32768, 1024], P(('dp', 'fsdp'))
- grad_tokens: float32 [32768, 1024], P(('dp', 'fsdp'))
- grad_head_scale: float32 [16], replicated
- grad_w_qkv: float32 [1024, 3072], P(('dp', 'fsdp'))
- grad_w_out: float32 [1024, 1024], P(('dp', 'fsdp'))
- grad_w_fc1: float32 [1024, 4096], P(('dp', 'fsdp'))
- grad_w_fc2: float32 [4096, 1024], P(('dp', 'fsdp'))
- grad_vec_d: float32 [10, 1024], P(None, ('dp', 'fsdp'))
- grad_vec_ff: float32 [3, 4096], P(None, ('dp', 'fsdp'))
Inputs may be any that keep to these rules, and one draw needn't show every extreme that they name: Every row holds one or two documents; some row has doc_split 1024 (one document) and some 1024 // 2. `model_vectors`: gains and biases. `hidden_vectors`: gains and biases.
All inputs are finite; a program needn't handle non-finite values.
Results may differ from a plain program's by a relative error of at most 0.015.
Values may be sent and summed in bfloat16 or wider, within the bound.
No kernel may reach another device: no remote copies, remote signals or barrier semaphores. Data moves between devices by JAX's collectives and lax.ppermute only.
A program may use at most 256 MiB of HBM per device.

v0:
```python
import functools

import jax
import jax.numpy as jnp
from jax import lax
from jax.experimental import pallas as pl
from jax.experimental.pallas import tpu as pltpu
from jax.sharding import PartitionSpec as P

epsilon = 1e-05
AXES = ("dp", "fsdp")
f32 = jnp.float32
bf16 = jnp.bfloat16
NEG = -1e30
VMEM_LIMIT = 56 << 20
ROWS_LIMIT = 62 << 20


def launch(
    kernel, args, *, in_specs, out_specs, out_shape, name, after=(), grid=(), scratch_shapes=(),
    prefetch=0, limit=VMEM_LIMIT, aliases=None, cover=False, cost=(1, 1, 0),
):
    after, count = list(after), len(args)

    def body(*refs):
        kernel(*refs[:count], *refs[count + len(after) :])

    return pl.pallas_call(
        body,
        grid_spec=pltpu.PrefetchScalarGridSpec(
            num_scalar_prefetch=prefetch,
            grid=grid,
            in_specs=[*in_specs] + [pl.BlockSpec(memory_space=pltpu.HBM)] * len(after),
            out_specs=out_specs,
            scratch_shapes=scratch_shapes,
        ),
        out_shape=out_shape,
        input_output_aliases=aliases or {},
        compiler_params=pltpu.CompilerParams(vmem_limit_bytes=limit),
        cost_estimate=pl.CostEstimate(
            flops=10**12 if cover else cost[0], bytes_accessed=cost[1], transcendentals=cost[2]
        ),
        name=name,
    )(*args, *after)


def relay(values, after):
    anywhere = pl.BlockSpec(memory_space=pl.ANY)
    return list(
        launch(
            lambda *refs: None,
            values,
            after=after,
            in_specs=[anywhere] * len(values),
            out_specs=[anywhere] * len(values),
            out_shape=[jax.ShapeDtypeStruct(v.shape, v.dtype) for v in values],
            aliases={k: k for k in range(len(values))},
            name="relay",
        )
    )


def in_vmem(value):
    return pltpu.with_memory_space_constraint(value, pltpu.VMEM)


class Plan:
    def __init__(self, mesh):
        n_dp, n_fs = mesh.shape["dp"], mesh.shape["fsdp"]
        self.count = n_dp * n_fs
        self.ways = min(self.count, 32)
        self.low = self.count // self.ways
        self.core = max(1, n_fs // self.low)
        self.dims = [1 << b for b in range(self.ways.bit_length() - 1) if 1 << b != self.core]
        self.half = self.ways // 2
        self.steps = len(self.dims)

    def order(self, core_bit, part, gathers):
        near, far = self.dims[:-1], self.dims[-1:]
        shift = (core_bit + part if part != 1 else 2) % len(near)
        near = near[shift:] + near[:shift]
        return far + near if gathers else near + far

    def pairs(self, part, step, gathers):
        out = []
        for i in range(self.count):
            group = i // self.low
            mask = self.order(int(bool(group & self.core)), part, gathers)[step]
            out.append((i, i ^ (mask * self.low)))
        return out

    def core_pairs(self):
        return [(i, i ^ (self.core * self.low)) for i in range(self.count)]

    def low_groups(self):
        return [[g * self.low + i for i in range(self.low)] for g in range(self.ways)]

    def table(self, part, gathers):
        me = (lax.axis_index("dp") * lax.axis_size("fsdp") + lax.axis_index("fsdp")) // self.low
        rows = []
        for core_bit in (0, 1):
            row = []
            for other in (0, 1):
                masks = self.order(core_bit ^ other, part, gathers)
                for r in range(self.half):
                    x = self.core if other else 0
                    for k in range(self.steps):
                        bit = k if gathers else self.steps - 1 - k
                        if (r >> bit) & 1:
                            x ^= masks[k]
                    row.append(x)
            rows.append(row)
        mine = ((me & self.core) != 0).astype(jnp.int32)
        masks = jnp.where(mine == 1, jnp.array(rows[1], jnp.int32), jnp.array(rows[0], jnp.int32))
        return jnp.bitwise_xor(me.astype(jnp.int32), masks)


class Gather:
    def __init__(self, plan, pieces):
        self.plan = plan
        self.held = [piece[None] for piece in pieces]
        self.fresh = None
        self.at = 0

    def join(self):
        if self.fresh is not None:
            self.held = [jnp.concatenate(pair, 0) for pair in zip(self.held, self.fresh)]
            self.fresh = None

    def step(self):
        self.join()
        self.fresh = [
            lax.ppermute(h, AXES, self.plan.pairs(part, self.at, True)) for part, h in enumerate(self.held)
        ]
        self.at += 1

    def cross_held(self):
        self.far_held = [lax.ppermute(h, AXES, self.plan.core_pairs()) for h in self.held]

    def cross_fresh(self):
        self.far_fresh = [lax.ppermute(h, AXES, self.plan.core_pairs()) for h in self.fresh]

    def blocks(self):
        return [list(b) for b in zip(self.held, self.fresh, self.far_held, self.far_fresh)]


def join_kernel(*refs, count):
    for n in range(count):
        out = refs[2 * count + n]
        half = out.shape[0] // 2
        out[:half] = refs[2 * n][...]
        out[half:] = refs[2 * n + 1][...]


def join_after(gathers, after):
    args = [
        a
        for one in gathers
        for held, fresh in zip(one.held, one.fresh)
        for a in (held, in_vmem(fresh))
    ]
    shapes = [(2 * h.shape[0], *h.shape[1:]) for one in gathers for h in one.held]
    vmem = pl.BlockSpec(memory_space=pltpu.VMEM)
    outs = launch(
        functools.partial(join_kernel, count=len(shapes)),
        args,
        after=after,
        in_specs=[vmem] * len(args),
        out_specs=[vmem] * len(shapes),
        out_shape=[jax.ShapeDtypeStruct(shape, bf16) for shape in shapes],
        name="join",
    )
    for n, one in enumerate(gathers):
        one.held = list(outs[2 * n : 2 * n + 2])
        one.fresh = None


def join_low(plan, piece, axis=0):
    if plan.low == 1:
        return piece
    return lax.all_gather(piece, AXES, axis=axis, tiled=True, axis_index_groups=plan.low_groups())


def fetch(action, table_ref, sources, lines, sem):
    for number, part, column, width, place in lines:
        for b in range(4):
            source = sources[4 * part + b]
            count = source.shape[0]

            def one(r, _, source=source, number=number, part=part, b=b, count=count):
                at = b * count + r
                copy = pltpu.make_async_copy(
                    source.at[r, :, pl.ds(column, width)],
                    place(table_ref[part, at]),
                    sem.at[number, at],
                )
                getattr(copy, action)()
                return _

            lax.fori_loop(0, count, one, 0)


def block_operands(plan, gathered):
    blocks = gathered.blocks()
    table = jnp.stack([plan.table(part, True) for part in range(len(blocks))])
    flat = [b for part in blocks for b in part]
    specs = [pl.BlockSpec(memory_space=pltpu.SMEM)] + [pl.BlockSpec(memory_space=pltpu.HBM)] * len(flat)
    return [table, *flat], specs


def plus(a, b):
    return a.astype(f32) + b.astype(f32)


class Scatter:
    def __init__(self, plan, part, keep, got):
        self.plan, self.part, self.at = plan, part, 0
        self.keep, self.got = keep, got

    @classmethod
    def begun(cls, plan, part, going, keep):
        one = cls(plan, part, None, None)
        one.send(going, keep)
        return one

    def send(self, going, keep):
        self.keep = keep
        self.got = lax.ppermute(going, AXES, self.plan.pairs(self.part, self.at, False))
        self.at += 1

    def total(self):
        return plus(self.keep[0], self.got[0])


def halve_kernel(*refs, count):
    for n in range(count):
        keep_ref, got_ref = refs[2 * n], refs[2 * n + 1]
        going_ref, kept_ref = refs[2 * (count + n)], refs[2 * (count + n) + 1]
        half = keep_ref.shape[0] // 2
        for out, part in ((going_ref, slice(half, 2 * half)), (kept_ref, slice(0, half))):
            out[...] = plus(keep_ref[part], got_ref[part]).astype(out.dtype)


def step_all(scatters, after=(), cover=False):
    args = [
        a
        for one in scatters
        for a in (one.keep, in_vmem(one.got))
    ]
    shapes = [
        jax.ShapeDtypeStruct((one.keep.shape[0] // 2, *one.keep.shape[1:]), one.keep.dtype)
        for one in scatters
        for _ in range(2)
    ]
    outs = launch(
        functools.partial(halve_kernel, count=len(scatters)),
        args,
        after=after,
        in_specs=[pl.BlockSpec(memory_space=pltpu.VMEM)] * len(args),
        out_specs=[pl.BlockSpec(memory_space=pltpu.VMEM)] * len(args),
        out_shape=shapes,
        name="halve",
        cover=cover,
    )
    for n, one in enumerate(scatters):
        one.send(*outs[2 * n : 2 * n + 2])
    return [outs[0]]


def to_other_core(plan, values):
    return lax.ppermute(values, AXES, plan.core_pairs())


def split_low(plan, total, axis=0):
    if plan.low == 1:
        return total
    return lax.psum_scatter(
        total, AXES, scatter_dimension=axis, tiled=True, axis_index_groups=plan.low_groups()
    )


def dot_nt(a, b):
    return lax.dot_general(a, b, (((1,), (1,)), ((), ())), preferred_element_type=f32)


def dot_nn(a, b):
    return lax.dot_general(a, b, (((1,), (0,)), ((), ())), preferred_element_type=f32)


def transposed(a):
    return a.astype(f32).T.astype(a.dtype)


def causal(scores):
    keys = lax.broadcasted_iota(jnp.int32, scores.shape, 0)
    return jnp.where(keys <= lax.broadcasted_iota(jnp.int32, scores.shape, 1), scores, NEG)


def head_lanes(shape, h, hd):
    lane = lax.broadcasted_iota(jnp.int32, shape, 1)
    mine = (lane >= hd) if h else (lane < hd)
    return mine, lane == (0 if h else hd)


def masked_keys(k, h, hd, split):
    mine, spare = head_lanes(k.shape, h, hd)
    early = lax.broadcasted_iota(jnp.int32, k.shape, 0) < split
    return jnp.where(mine, k, jnp.where(spare & early, bf16(NEG), bf16(0)))


def masked_queries(q, h, hd, split, start):
    mine, spare = head_lanes(q.shape, h, hd)
    late = lax.broadcasted_iota(jnp.int32, q.shape, 0) + start >= split
    alone = jnp.where(mine, q, bf16(0)) * bf16(hd**-0.5)
    return alone, jnp.where(spare & late, bf16(1), alone)


def attention_kernel(split_ref, q_ref, k_ref, v_ref, *refs, seq, hd, blk):
    o_ref, lse_ref = refs[-2:]
    split = split_ref[0]
    v_t = transposed(v_ref[...])
    keys = [masked_keys(k_ref[...], h, hd, split) for h in (0, 1)]
    for i in range(seq // blk):
        rows = slice(i * blk, (i + 1) * blk)
        outs = []
        for h in (0, 1):
            _, q = masked_queries(q_ref[rows, :], h, hd, split, i * blk)
            scores = [dot_nt(keys[h][j * blk : (j + 1) * blk], q) for j in range(i + 1)]
            scores[i] = causal(scores[i])
            peak = scores[0].max(0, keepdims=True)
            for s in scores[1:]:
                peak = jnp.maximum(peak, s.max(0, keepdims=True))
            total = jnp.zeros((1, blk), f32)
            mixed = jnp.zeros((hd, blk), f32)
            for j, s in enumerate(scores):
                low = []
                for r in strips(blk, 64):
                    e = jnp.exp(s[r] - peak)
                    total += e.sum(0, keepdims=True)
                    low.append(e.astype(bf16))
                mixed += dot_nn(
                    v_t[h * hd : (h + 1) * hd, j * blk : (j + 1) * blk], jnp.concatenate(low, 0)
                )
            outs.append(mixed / total)
            lse_ref[0, h : h + 1, rows] = peak + jnp.log(total)
        o_ref[rows, :] = jnp.concatenate(outs, 0).T


def attention(split, qkv, heads, blk, start, count, into=(), after=()):
    seq, width = qkv.shape[0], qkv.shape[1] // 3
    hd, pairs = width // heads, heads // 2
    w = 2 * hd
    return launch(
        functools.partial(attention_kernel, seq=seq, hd=hd, blk=blk),
        [split, qkv, qkv, qkv, *into],
        after=after,
        grid=(count,),
        in_specs=[
            pl.BlockSpec(memory_space=pltpu.SMEM),
            pl.BlockSpec((seq, w), lambda p: (0, p + start)),
            pl.BlockSpec((seq, w), lambda p: (0, p + start + pairs)),
            pl.BlockSpec((seq, w), lambda p: (0, p + start + 2 * pairs)),
        ]
        + [pl.BlockSpec(memory_space=pl.ANY)] * len(into),
        out_specs=[
            pl.BlockSpec((seq, w), lambda p: (0, p + start)),
            pl.BlockSpec((1, 2, seq), lambda p: (p + start, 0, 0)),
        ],
        out_shape=[
            jax.ShapeDtypeStruct((seq, width), f32),
            jax.ShapeDtypeStruct((pairs, 2, seq), f32),
        ],
        aliases={4 + k: k for k in range(len(into))},
        name="attention",
        cost=(12 * seq * seq * w * count, seq * w * count * 10, 2 * count * seq * seq),
    )


def attention_back_kernel(
    split_ref, q_ref, k_ref, v_ref, da_ref, o_ref, lse_ref, dq_ref, dk_ref, dv_ref, dk_acc, dv_acc,
    *, seq, hd, blk,
):
    split = split_ref[0]
    k_t = transposed(k_ref[...])
    keys_of = [masked_keys(k_ref[...], h, hd, split) for h in (0, 1)]
    for i in range(seq // blk):
        rows = slice(i * blk, (i + 1) * blk)
        q_full, da_full = q_ref[rows, :], da_ref[rows, :]
        inner = (da_full.astype(f32) * o_ref[rows, :]).T
        dqs = []
        for h in (0, 1):
            q, q_marked = masked_queries(q_full, h, hd, split, i * blk)
            da = jnp.where(head_lanes(da_full.shape, h, hd)[0], da_full, bf16(0))
            row_inner = inner[h * hd : (h + 1) * hd].sum(0, keepdims=True)
            lse = lse_ref[0, h : h + 1, rows]
            dq = jnp.zeros((hd, blk), f32)
            for j in range(i + 1):
                keys = slice(j * blk, (j + 1) * blk)
                s = dot_nt(keys_of[h][keys], q_marked)
                if i == j:
                    s = causal(s)
                dp = dot_nt(v_ref[keys, :], da)
                p_low, ds = [], []
                for r in strips(blk, 64):
                    p = jnp.exp(s[r] - lse)
                    p_low.append(p.astype(bf16))
                    ds.append((p * (dp[r] - row_inner)).astype(bf16))
                ds = jnp.concatenate(ds, 0)
                dv = dot_nn(jnp.concatenate(p_low, 0), da)
                dk = dot_nn(ds, q)
                if i == j and h == 0:
                    dv_acc[keys, :] = dv
                    dk_acc[keys, :] = dk
                else:
                    dv_acc[keys, :] += dv
                    dk_acc[keys, :] += dk
                dq += dot_nn(k_t[h * hd : (h + 1) * hd, keys], ds)
            dqs.append(dq)
        dq_ref[rows, :] = (jnp.concatenate(dqs, 0).T * (hd**-0.5)).astype(bf16)
    dk_ref[...] = dk_acc[...].astype(bf16)
    dv_ref[...] = dv_acc[...].astype(bf16)


def attention_back(split, qkv, da, attended, lse, heads, blk, start, count, after=()):
    seq, width = qkv.shape[0], qkv.shape[1] // 3
    hd, pairs = width // heads, heads // 2
    w = 2 * hd
    column = pl.BlockSpec((seq, w), lambda p: (0, p + start))
    out = pl.BlockSpec((seq, w), lambda p: (0, p))
    return launch(
        functools.partial(attention_back_kernel, seq=seq, hd=hd, blk=blk),
        [split, qkv, qkv, qkv, da, attended, lse],
        after=after,
        grid=(count,),
        in_specs=[
            pl.BlockSpec(memory_space=pltpu.SMEM),
            column,
            pl.BlockSpec((seq, w), lambda p: (0, p + start + pairs)),
            pl.BlockSpec((seq, w), lambda p: (0, p + start + 2 * pairs)),
            column,
            column,
            pl.BlockSpec((1, 2, seq), lambda p: (p + start, 0, 0)),
        ],
        out_specs=[out, out, out],
        out_shape=[jax.ShapeDtypeStruct((seq, count * w), bf16)] * 3,
        scratch_shapes=[pltpu.VMEM((seq, w), f32)] * 2,
        name="attention_back",
    )


def grads_kernel(table_ref, place_ref, *refs, runs, n_left, n_right, begins, adds):
    lefts, rights, rest = refs[:n_left], refs[n_left : n_left + n_right], refs[n_left + n_right :]
    left = rest[-1]
    ways, rows, tokens = left.shape
    step = pl.program_id(0)
    for first, last, l, r, part in runs:

        @pl.when(step == first)
        def _():
            for w in range(ways):
                left[w] = lefts[l][table_ref[part, w], 0]

        @pl.when((step >= first) & (step < last))
        def _():
            product = [dot_nn(left[...].reshape(ways * rows, tokens), rights[k][...]) for k in r]
            product = jnp.concatenate(product, 1) if len(r) > 1 else product[0]
            product = product.reshape(ways, rows, product.shape[1])
            if adds:
                n_parts = len(begins)
                got_ref = rest[part]
                at = pl.multiple_of((step - begins[part]) * product.shape[2], 128)
                theirs = got_ref[:, :, pl.ds(at, product.shape[2])]
                going_ref, keep_ref = rest[n_parts + 2 * part : n_parts + 2 * part + 2]
                product = (product + theirs.astype(f32)).astype(bf16)
                keep_ref[...] = product[: ways // 2]
                going_ref[...] = product[ways // 2 :]
            else:
                rest[part][...] = product.astype(bf16)


def grads(tables, parts, tile, got=None, after=(), cover=False):
    groups, _, rows, tokens = parts[0][0][0].shape
    ways = tables[0].shape[0]
    lefts, rights, runs, places, spans = [], [], [], [], []
    at = 0
    for part, jobs in enumerate(parts):
        begin = at
        for left, q, group, numbers in jobs:
            for known, one in ((lefts, left), *((rights, right) for right in group)):
                if not any(one is k for k in known):
                    known.append(one)
            l = next(i for i, k in enumerate(lefts) if k is left)
            r = [next(i for i, k in enumerate(rights) if k is right) for right in group]
            runs.append((at, at + len(numbers), l, r, part))
            for n in numbers:
                places.append(([l], q, r, n))
            at += len(numbers)
        spans.append((begin, at - begin))

    def held(which, entry, count):
        lines = []
        for k in range(count):
            used = [(s, p[entry]) for s, p in enumerate(places) if k in p[which]]
            lines.append([next((v for s, v in used if s >= i), used[-1][1]) for i in range(at)])
        return lines

    place = jnp.array(held(0, 1, len(lefts)) + held(2, 3, len(rights)), jnp.int32)

    def left_spec(k):
        return pl.BlockSpec((groups, 1, rows, tokens), lambda i, t, p: (0, p[k, i], 0, 0))

    def right_spec(k):
        return pl.BlockSpec((tokens, share), lambda i, t, p: (0, p[len(lefts) + k, i]))

    def block(count, span):
        begin, steps = span
        return pl.BlockSpec(
            (count, rows, tile), lambda i, t, p: (0, 0, jnp.clip(i - begin, 0, steps - 1))
        )

    def shape(count, span):
        return jax.ShapeDtypeStruct((count, rows, span[1] * tile), bf16)

    share = tile // len(parts[0][0][2])
    adds = got is not None
    each = [ways // 2] * 2 if adds else [ways]
    return launch(
        functools.partial(
            grads_kernel,
            runs=runs,
            n_left=len(lefts),
            n_right=len(rights),
            begins=[span[0] for span in spans],
            adds=adds,
        ),
        [jnp.stack(tables), place, *lefts, *rights, *(map(in_vmem, got) if adds else [])],
        after=after,
        prefetch=2,
        grid=(at,),
        in_specs=[left_spec(k) for k in range(len(lefts))]
        + [right_spec(k) for k in range(len(rights))]
        + [pl.BlockSpec(memory_space=pltpu.VMEM)] * (len(parts) * adds),
        out_specs=[block(count, span) for span in spans for count in each],
        out_shape=[shape(count, span) for span in spans for count in each],
        scratch_shapes=[pltpu.VMEM((ways, rows, tokens), bf16)],
        name="grads_keep" if adds else "grads_send",
        cover=cover,
    )


def normalized(values):
    center = values - jnp.mean(values, axis=-1, keepdims=True)
    rate = lax.rsqrt(jnp.mean(center * center, axis=-1, keepdims=True) + epsilon)
    return center * rate, rate


def norm_back(grad, unit, rate):
    inner = jnp.mean(grad * unit, axis=-1, keepdims=True)
    return rate * (grad - jnp.mean(grad, axis=-1, keepdims=True) - unit * inner)


def by_lanes(values):
    total = values[:, :128]
    for k in range(128, values.shape[1], 128):
        total += values[:, k : k + 128]
    return total


def by_sublanes(values):
    total = values[:8]
    for k in range(8, values.shape[0], 8):
        total += values[k : k + 8]
    return total


def column_sum(values):
    return jnp.sum(values, axis=0, keepdims=True)


def resident(shape):
    return pl.BlockSpec(shape, lambda i: (0,) * len(shape), pipeline_mode=pl.Buffered(1))


def by_rows(blk, width):
    return pl.BlockSpec((blk, width), lambda i: (i, 0))


def by_columns(height, blk):
    return pl.BlockSpec((height, blk), lambda i: (0, i))


def weight_lines(w, cut, group, first=0):
    def rows(g):
        return pl.ds(pl.multiple_of(g * group, group), group)

    rest = w.shape[1] - cut
    return [
        (first, 0, 0, cut, lambda g: w.at[rows(g), pl.ds(0, cut)]),
        (first + 1, 1, 0, rest, lambda g: w.at[rows(g), pl.ds(cut, rest)]),
    ]


def project_kernel(table_ref, x_ref, *refs, cut):
    sources = refs[:8]
    qkv_ref, left_t_ref, vec_ref, hid_ref, w, raw, left_ref, sem = refs[8:]
    ways, group, lanes = raw.shape
    width = x_ref.shape[1]

    @pl.when(pl.program_id(0) == 0)
    def _():
        vec_lines = [(2, 0, cut, lanes, lambda g: raw.at[g])]
        lines = weight_lines(w, cut, group)
        fetch("start", table_ref, sources, vec_lines, sem)
        fetch("start", table_ref, sources, lines, sem)
        fetch("wait", table_ref, sources, vec_lines, sem)
        per = lanes // group
        for k in range(0, ways, per):
            row = [raw[k + j][:16, :group].astype(f32) for j in range(per)]
            vec_ref[:, k * group : (k + per) * group] = jnp.concatenate(row, 1)
        for k in range(ways):
            hid_ref[:, k * lanes : (k + 1) * lanes] = raw[k][:16].astype(f32)
        fetch("wait", table_ref, sources, lines, sem)

    for r in strips(x_ref.shape[0], 16):
        unit, _ = normalized(x_ref[r, :].astype(f32))
        left_ref[r, :] = (unit * vec_ref[0:1, :] + vec_ref[1:2, :]).astype(bf16)
    left = left_ref[...]
    left_t_ref[...] = transposed(left)
    for part, bias in ((0, 2), (1, None), (2, 3)):
        cols = slice(part * width, (part + 1) * width)
        rows = dot_nn(left, w[:, cols])
        if bias is not None:
            rows += vec_ref[bias : bias + 1, :]
        qkv_ref[:, cols] = rows.astype(bf16)


def project(plan, tokens, gathered, cut, hidden, after=(), blk=256):
    seq, width = tokens.shape
    blk = min(blk, seq)
    (table, *blocks), (table_spec, *specs) = block_operands(plan, gathered)
    return launch(
        functools.partial(project_kernel, cut=cut),
        [table, tokens, *blocks],
        after=after,
        grid=(seq // blk,),
        in_specs=[table_spec, by_rows(blk, width), *specs],
        out_specs=[
            by_rows(blk, 3 * width),
            by_columns(width, blk),
            pl.BlockSpec((16, width), lambda i: (0, 0)),
            pl.BlockSpec((16, hidden), lambda i: (0, 0)),
        ],
        out_shape=[
            jax.ShapeDtypeStruct((seq, 3 * width), bf16),
            jax.ShapeDtypeStruct((width, seq), bf16),
            jax.ShapeDtypeStruct((16, width), f32),
            jax.ShapeDtypeStruct((16, hidden), f32),
        ],
        scratch_shapes=[
            pltpu.VMEM((width, 3 * width), bf16),
            pltpu.VMEM((plan.ways, width // plan.ways, hidden // plan.ways), bf16),
            pltpu.VMEM((blk, width), bf16),
            pltpu.SemaphoreType.DMA((3, plan.ways)),
        ],
        name="project",
        cost=(6 * seq * width * width, 18 * seq * width, seq),
    )


def group_rows(g, group, stride, first=0):
    return pl.ds(pl.multiple_of(g * stride + first, group), group)


def vector(ref, row):
    return ref[row : row + 1, :]


def strips(rows, height):
    return [slice(r, r + height) for r in range(0, rows, height)]


def middle_kernel(
    table_ref, x_ref, att_ref, c_ref, vec_ref, hid_ref, scale_ref, *refs, chunk, half_q
):
    sources, refs = refs[:8], refs[8:]
    out_ref, z_t_ref, a2_t_ref, m_t_ref, df_ref, dy_ref, da_ref, dx_ref, sums_ref, hid_sums_ref = refs[:10]
    wo_ref, w1_ref, w2_ref, gate, slope, dm_keep, acc, sem = refs[10:]
    width, hidden = w1_ref.shape
    group = sources[0].shape[1]
    n_q = hidden // width

    def rows(g, stride, first=0):
        return pl.ds(pl.multiple_of(g * stride + first, group), group)

    def quarter(q):
        column = hidden * (q < half_q) + q % half_q * width
        return (2 + q, q // half_q, column, width, lambda g: w2_ref.at[rows(g, n_q * group, q * group)])

    out_lines = [(0, 1, half_q * width, width, lambda g: wo_ref.at[rows(g, group)])]
    fc1_lines = [(1, 0, 0, hidden, lambda g: w1_ref.at[rows(g, group)])]
    fc2_lines = [quarter(q) for q in range(n_q)]

    def arrived(lines):
        @pl.when(pl.program_id(0) == 0)
        def _():
            fetch("wait", table_ref, sources, lines, sem)

    chunks = [slice(k, k + chunk) for k in range(0, hidden, chunk)]

    @pl.when(pl.program_id(0) == 0)
    def _():
        for lines in (out_lines, fc1_lines, fc2_lines):
            fetch("start", table_ref, sources, lines, sem)
        sums_ref[...] = jnp.zeros_like(sums_ref)
        hid_sums_ref[...] = jnp.zeros_like(hid_sums_ref)

    def vec(row):
        return vec_ref[row : row + 1, :]

    def add_sum(row, values):
        sums_ref[row : row + 1, :] += column_sum(values)

    z = (att_ref[...] * scale_ref[...]).astype(bf16)
    z_t_ref[...] = transposed(z)
    arrived(out_lines)
    unit_1, rate_1 = normalized(dot_nn(z, wo_ref[...]) + vec(4))
    x2 = x_ref[...].astype(f32) + (unit_1 * vec(5) + vec(6))
    unit_2, rate_2 = normalized(x2)
    a2 = (unit_2 * vec(7) + vec(8)).astype(bf16)
    a2_t_ref[...] = transposed(a2)
    arrived(fc1_lines)

    total = 0.0
    root = (2.0 / jnp.pi) ** 0.5
    for ch in chunks:
        f = dot_nn(a2, w1_ref[:, ch]) + hid_ref[10:11, ch]
        square = f * f
        t = jnp.tanh(f * (root + (root * 0.044715) * square))
        half = 0.5 + 0.5 * t
        g = f * half
        gate[:, ch] = g
        slope[:, ch] = half + g * (1.0 - t) * (root + (3 * root * 0.044715) * square)
        total += jnp.sum(g, axis=-1, keepdims=True)
    mean = total / hidden
    spread = 0.0
    for ch in chunks:
        center = gate[:, ch] - mean
        spread += jnp.sum(center * center, axis=-1, keepdims=True)
    rate = lax.rsqrt(spread / hidden + epsilon)

    arrived(fc2_lines)
    grad_sum = 0.0
    grad_inner = 0.0
    for ch in chunks:
        unit = (gate[:, ch] - mean) * rate
        gate[:, ch] = unit
        gain = hid_ref[11:12, ch]
        m = (unit * gain + hid_ref[12:13, ch]).astype(bf16)
        m_t_ref[ch, :] = transposed(m)
        y = dot_nn(m, w2_ref[ch, :])
        if ch.start == 0:
            acc[...] = y
        else:
            acc[...] += y
        dm = dot_nt(c_ref[...], w2_ref[ch, :]).astype(bf16)
        dm_keep[:, ch] = dm
        dm = dm.astype(f32)
        hid_sums_ref[1:2, ch] += column_sum(dm * unit)
        hid_sums_ref[2:3, ch] += column_sum(dm)
        grad = dm * gain
        grad_sum += jnp.sum(grad, axis=-1, keepdims=True)
        grad_inner += jnp.sum(grad * unit, axis=-1, keepdims=True)
    out_ref[...] = (x2 + (acc[...] + vec(9))).astype(bf16)

    grad_sum = grad_sum / hidden
    grad_inner = grad_inner / hidden
    for ch in chunks:
        grad = dm_keep[:, ch].astype(f32) * hid_ref[11:12, ch]
        grad = rate * (grad - grad_sum - gate[:, ch] * grad_inner)
        df = (slope[:, ch] * grad).astype(bf16)
        df_ref[:, ch] = df
        hid_sums_ref[0:1, ch] += column_sum(df.astype(f32))
        back = dot_nt(df, w1_ref[:, ch])
        if ch.start == 0:
            acc[...] = back
        else:
            acc[...] += back

    upstream = c_ref[...].astype(f32)
    da2 = acc[...]
    add_sum(9, upstream)
    add_sum(7, da2 * unit_2)
    add_sum(8, da2)
    dx2 = upstream + norm_back(da2 * vec(7), unit_2, rate_2)
    dx_ref[...] = dx2
    add_sum(5, dx2 * unit_1)
    add_sum(6, dx2)
    dy = norm_back(dx2 * vec(5), unit_1, rate_1).astype(bf16)
    dy_ref[...] = dy
    add_sum(4, dy.astype(f32))
    dz = dot_nt(dy, wo_ref[...]).astype(bf16).astype(f32)
    add_sum(10, dz * att_ref[...])
    da_ref[...] = (dz * scale_ref[...]).astype(bf16)


def middle(plan, tokens, attended, cotangent, gathered, vec, hid, scale, half_q, after=(), blk=256, chunk=256):
    seq, width = tokens.shape
    hidden = hid.shape[1]
    blk = min(blk, seq)
    (table, *blocks), (table_spec, *specs) = block_operands(plan, gathered)
    row, col, wide = by_rows(blk, width), by_columns(width, blk), by_rows(blk, hidden)
    shape = jax.ShapeDtypeStruct
    return launch(
        functools.partial(middle_kernel, chunk=chunk, half_q=half_q),
        [table, tokens, attended, cotangent, vec, hid, scale, *blocks],
        after=after,
        grid=(seq // blk,),
        in_specs=[table_spec, row, row, row, *(resident(a.shape) for a in (vec, hid, scale)), *specs],
        out_specs=[
            row, col, col, by_columns(hidden, blk), wide, row, row, row,
            pl.BlockSpec((16, width), lambda i: (0, 0)),
            pl.BlockSpec((8, hidden), lambda i: (0, 0)),
        ],
        out_shape=[
            shape((seq, width), bf16),
            shape((width, seq), bf16),
            shape((width, seq), bf16),
            shape((hidden, seq), bf16),
            shape((seq, hidden), bf16),
            shape((seq, width), bf16),
            shape((seq, width), bf16),
            shape((seq, width), f32),
            shape((16, width), f32),
            shape((8, hidden), f32),
        ],
        scratch_shapes=[
            pltpu.VMEM((width, width), bf16),
            pltpu.VMEM((width, hidden), bf16),
            pltpu.VMEM((hidden, width), bf16),
            pltpu.VMEM((blk, hidden), f32),
            pltpu.VMEM((blk, hidden), f32),
            pltpu.VMEM((blk, hidden), bf16),
            pltpu.VMEM((blk, width), f32),
            pltpu.SemaphoreType.DMA((2 + hidden // width, plan.ways)),
        ],
        limit=ROWS_LIMIT,
        name="middle",
        cost=(
            4 * seq * width * (width + 2 * hidden),
            2 * width * (width + 2 * hidden) + 40 * seq * width,
            seq * hidden,
        ),
    )


def finish_kernel(table_ref, x_ref, dx_ref, vec_ref, *refs, cut, n_parts):
    grads_in, sources = refs[: 3 * n_parts], refs[3 * n_parts : 3 * n_parts + 8]
    out_ref, sums_ref, w, acc, sem = refs[3 * n_parts + 8 :]
    width = x_ref.shape[1]

    @pl.when(pl.program_id(0) == 0)
    def _():
        lines = weight_lines(w, cut, sources[0].shape[1])
        fetch("start", table_ref, sources, lines, sem)
        sums_ref[...] = jnp.zeros_like(sums_ref)
        acc[...] = jnp.zeros_like(acc)
        fetch("wait", table_ref, sources, lines, sem)

    da1 = 0.0
    column = 0
    for part in range(n_parts):
        wide = grads_in[3 * part].shape[1]
        for k in range(3):
            grad = grads_in[3 * part + k][...]
            da1 += dot_nt(grad, w[:, k * width + column : k * width + column + wide])
            if k != 1:
                row = 2 + k // 2
                sums_ref[row : row + 1, column : column + wide] += column_sum(grad.astype(f32))
        column += wide
    for r in strips(x_ref.shape[0], 16):
        grad = da1[r]
        unit, rate = normalized(x_ref[r, :].astype(f32))
        acc[:8] += by_sublanes(grad * unit)
        acc[8:] += by_sublanes(grad)
        out_ref[r, :] = dx_ref[r, :] + norm_back(grad * vec_ref[0:1, :], unit, rate)

    @pl.when(pl.program_id(0) == pl.num_programs(0) - 1)
    def _():
        sums_ref[0:1, :] = column_sum(acc[:8])
        sums_ref[1:2, :] = column_sum(acc[8:])


def finish(plan, tokens, dx2, vec, parts, gathered, cut, after=(), blk=256):
    seq, width = tokens.shape
    blk = min(blk, seq)
    row = by_rows(blk, width)
    (table, *blocks), (table_spec, *specs) = block_operands(plan, gathered)
    grads_in = [g for part in parts for g in part]
    return launch(
        functools.partial(finish_kernel, cut=cut, n_parts=len(parts)),
        [table, tokens, dx2, vec, *grads_in, *blocks],
        after=after,
        grid=(seq // blk,),
        in_specs=[table_spec, row, row, resident(vec.shape)]
        + [by_rows(blk, g.shape[1]) for g in grads_in]
        + specs,
        out_specs=[row, pl.BlockSpec((8, width), lambda i: (0, 0))],
        out_shape=[
            jax.ShapeDtypeStruct((seq, width), f32),
            jax.ShapeDtypeStruct((8, width), f32),
        ],
        scratch_shapes=[
            pltpu.VMEM((width, 3 * width), bf16),
            pltpu.VMEM((16, width), f32),
            pltpu.SemaphoreType.DMA((2, plan.ways)),
        ],
        name="finish",
    )


def local(
    plan,
    tokens,
    doc_split,
    head_scale,
    query_key_value_weight,
    output_weight,
    first_weight,
    second_weight,
    model_vectors,
    hidden_vectors,
    cotangent,
):
    seq, width = tokens.shape
    hidden = first_weight.shape[1]
    heads = head_scale.shape[0]
    blk = min(256, seq)
    ways, half = plan.ways, plan.half
    n_vec, n_hid = model_vectors.shape[0], hidden_vectors.shape[0]

    cut = 2 * width
    group, lanes = width // ways, hidden // ways
    qkv_rows = join_low(plan, query_key_value_weight)
    vec_rows = jnp.concatenate(
        [
            jnp.pad(join_low(plan, model_vectors, 1), ((0, 0), (0, lanes - group))),
            join_low(plan, hidden_vectors, 1),
            jnp.zeros((group - n_vec - n_hid, lanes), bf16),
        ],
        0,
    )
    fc1_rows = join_low(plan, first_weight)
    fc2_rows = join_low(plan, second_weight)
    out_rows = join_low(plan, output_weight)
    n_q = hidden // width
    half_q = n_q // 2
    quarters = [fc2_rows[q * group : (q + 1) * group] for q in range(n_q)]
    first = Gather(plan, [jnp.concatenate([qkv_rows[:, :cut], vec_rows], 1), qkv_rows[:, cut:]])
    second = Gather(
        plan,
        [
            jnp.concatenate([fc1_rows, *quarters[:half_q]], 1),
            jnp.concatenate([*quarters[half_q:], out_rows], 1),
        ],
    )
    first.step()
    second.step()
    while first.at < plan.steps:
        first.step()
    first.cross_held()
    first.cross_fresh()
    while second.at < plan.steps - 1:
        second.step()

    qkv, first_t, vec, hid = project(plan, tokens, first, cut, hidden, second.held)
    join_after([second], [vec])
    second.step()
    second.cross_held()
    pairs = heads // 2
    attended, lse = attention(doc_split, qkv, heads, blk, 0, pairs, after=second.held)
    second.fresh = relay(second.fresh, [lse])
    second.cross_fresh()

    scale_row = jnp.repeat(head_scale, width // heads)[None]
    output, scaled_t, second_t, hidden_t, grad_pre, grad_branch, grad_attended, grad_middle, sums, hid_sums = (
        middle(plan, tokens, attended, cotangent, second, vec, hid, scale_row, half_q)
    )
    table = plan.table(0, False)

    def by_group(left_t):
        return left_t.reshape(ways, -1, group, seq)

    def send_grads(jobs, tile, after=(), cover=False):
        sent = grads([table[half:]], [jobs], tile, None, after, cover)
        return list(sent), to_other_core(plan, sent[0])

    def keep_grads(jobs, tile, got, after=(), cover=False):
        outs = grads([table[:half]], [jobs], tile, [got], after, cover)
        return list(outs[:1]), Scatter.begun(plan, 0, *outs)

    hidden_t = by_group(hidden_t)
    fc2_jobs = [(hidden_t, q, [cotangent], [0]) for q in range(n_q)]
    fc1_jobs = [
        (by_group(second_t), 0, [grad_pre], range(n_q)),
        (by_group(scaled_t), 0, [grad_branch], [0]),
    ]
    done, got_2 = send_grads(fc2_jobs, width)
    done, got_1 = send_grads(fc1_jobs, width, done, True)
    done, fc2_sum = keep_grads(fc2_jobs, width, got_2, done, True)
    done, fc1_sum = keep_grads(fc1_jobs, width, got_1, done)

    first_t = by_group(first_t)

    def back(start, count, after):
        out = attention_back(doc_split, qkv, grad_attended, attended, lse, heads, blk, start, count, after)
        return list(out[:1]), list(out)

    some = pairs * 3 // 8
    done, part_a = back(0, some, done)
    done = step_all([fc2_sum], done)
    done, part_b = back(some, some, done)
    size = part_a[0].shape[1]
    jobs = [(first_t, 0, part, [0]) for part in (part_a, part_b)]
    done, got = send_grads(jobs, 3 * size, done)
    done = step_all([fc2_sum, fc1_sum], done, True)
    done, sum_a = keep_grads(jobs, 3 * size, got, done)
    done, part_c = back(2 * some, pairs - 2 * some, done)
    rest = part_c[0].shape[1]
    jobs = [(first_t, 0, part_c, [0])]
    done, got = send_grads(jobs, 3 * rest, done)
    done = step_all([fc2_sum, fc1_sum, sum_a], done, True)
    done, sum_b = keep_grads(jobs, 3 * rest, got, done)
    grad_tokens, last_sums = finish(
        plan, tokens, grad_middle, vec, (part_a, part_b, part_c), first, cut, done
    )
    done = step_all([fc1_sum, sum_a, sum_b], [last_sums])

    vec_grads = jnp.concatenate([last_sums[:4], sums[4:n_vec]], 0)
    head_sums = jnp.sum(sums[n_vec].reshape(heads, -1), axis=1)
    vec_blocks = jnp.concatenate(
        [
            jnp.pad(
                vec_grads.reshape(n_vec, ways, group).transpose(1, 0, 2),
                ((0, 0), (0, 0), (0, lanes - group)),
            ),
            hid_sums[:n_hid].reshape(n_hid, ways, lanes).transpose(1, 0, 2),
            jnp.broadcast_to(jnp.pad(head_sums, (0, lanes - heads)), (ways, 1, lanes)),
            jnp.zeros((ways, 15 - n_vec - n_hid, lanes), f32),
        ],
        1,
    )
    got = to_other_core(plan, vec_blocks[table[half:]])
    vec_sum = Scatter(plan, 0, vec_blocks[table[:half]], got)
    done = step_all([sum_a, sum_b, vec_sum], done)
    done = step_all([sum_b, vec_sum], done)
    while vec_sum.at < plan.steps:
        done = step_all([vec_sum], done)
    sent_vec = vec_sum.total()
    sent_a, sent_b = sum_a.total(), sum_b.total()
    sum_fc2, sum_fc1 = fc2_sum.total(), fc1_sum.total()
    columns = []
    for k in range(3):
        columns += [sent_a[:, k * size : (k + 1) * size], sent_a[:, (3 + k) * size : (4 + k) * size]]
        columns.append(sent_b[:, k * rest : (k + 1) * rest])
    sent_qkv = split_low(plan, jnp.concatenate(columns, 1))
    sent_fc1 = split_low(plan, sum_fc1[:, :hidden])
    sent_out = split_low(plan, sum_fc1[:, hidden:])
    row_blocks = [sum_fc2[:, k : k + width] for k in range(0, hidden, width)]
    sent_fc2 = split_low(plan, jnp.concatenate(row_blocks, 0))
    sent_vecd = split_low(plan, sent_vec[:n_vec, :group], 1)
    sent_vecff = split_low(plan, sent_vec[n_vec : n_vec + n_hid], 1)
    grad_heads = sent_vec[n_vec + n_hid, :heads]
    if plan.low > 1:
        grad_heads = lax.psum(grad_heads, AXES, axis_index_groups=plan.low_groups())
    return (
        output,
        grad_tokens,
        grad_heads,
        sent_qkv,
        sent_out,
        sent_fc1,
        sent_fc2,
        sent_vecd,
        sent_vecff,
    )


def solution(mesh):
    rows = P(AXES, None)
    columns = P(None, AXES)
    return jax.shard_map(
        functools.partial(local, Plan(mesh)),
        mesh=mesh,
        in_specs=(rows, P(AXES), P(), rows, rows, rows, rows, columns, columns, rows),
        out_specs=(rows, rows, P(), rows, rows, rows, rows, columns, columns),
        check_vma=False,
    )
```

profile of v0, /device:TPU:0, one launch (start us, length us, event | category | flops | bytes accessed | tf_op | source)
XLA Modules:
  0.0 450.7 jit_solution(10290249896133540195)
XLA Ops:
  2.3 4.1 collective-permute-start
  6.4 6.7 %collective-permute-done = bf16[1,32,2176]{2,1,0:T(8,128)(2,1)S(1)} collective-permute-done((bf16[1,32,2176]{2,1,0:T(8,128)(2,1)S(1)}, bf16[1,32,2176]{2,1,0:T(8,128)(2,1)S(1)}, u32[]{:S(2)}, u32[]{:S(2)}) %collective-permute-start) | collective-permute-done | bytes 139296 | tf_op jit(solution)/shard_map/ppermute | solution.py:133
  13.1 1.6 collective-permute-start.1
  16.6 3.2 collective-permute-done.1
  19.8 1.6 collective-permute-start.2
  21.9 3.8 collective-permute-start.7
  25.7 3.7 collective-permute-done.2
  31.4 9.4 %collective-permute-done.12 = bf16[1,32,6144]{2,1,0:T(8,128)(2,1)S(1)} collective-permute-done((bf16[1,32,6144]{2,1,0:T(8,128)(2,1)S(1)}, bf16[1,32,6144]{2,1,0:T(8,128)(2,1)S(1)}, u32[]{:S(2)}, u32[]{:S(2)}) %collective-permute-start.12) | collective-permute-done | bytes 393248 | tf_op jit(solution)/shard_map/ppermute | solution.py:133
  40.9 1.6 collective-permute-start.13
  43.2 12.9 %collective-permute-done.14 = bf16[1,32,3072]{2,1,0:T(8,128)(2,1)S(1)} collective-permute-done((bf16[1,32,3072]{2,1,0:T(8,128)(2,1)S(1)}, bf16[1,32,3072]{2,1,0:T(8,128)(2,1)S(1)}, u32[]{:S(2)}, u32[]{:S(2)}) %collective-permute-start.14) | collective-permute-done | bytes 196640 | tf_op jit(solution)/shard_map/ppermute | solution.py:133
  56.2 5.3 %collective-permute-start.15 = (bf16[2,32,3072]{2,1,0:T(8,128)(2,1)S(1)}, bf16[2,32,3072]{2,1,0:T(8,128)(2,1)S(1)}, u32[]{:S(2)}, u32[]{:S(2)}) collective-permute-start(bf16[2,32,3072]{2,1,0:T(8,128)(2,1)S(1)} %pad_maximum_fusion.7), channel_id=1, source_target_pairs={{0,8},{1,9},{2,10},{3,11},{4,12},{5,13},{6,14},{7,15},{8,0},{9,1},... | collective-permute-start | bytes 1179656 | tf_op jit(solution)/shard_map/ppermute | solution.py:133
  61.5 3.2 collective-permute-done.8
  69.1 8.3 %collective-permute-done.9.refs_7_.refs_18_ = bf16[8,32,1024]{2,1,0:T(8,128)(2,1)} collective-permute-done((bf16[8,32,1024]{2,1,0:T(8,128)(2,1)}, bf16[8,32,1024]{2,1,0:T(8,128)(2,1)}, u32[]{:S(2)}, u32[]{:S(2)}) %collective-permute-start.9) | collective-permute-done | bytes 524320 | tf_op jit(solution)/shard_map/ppermute | solution.py:133
  80.6 15.1 %project.1 = (bf16[1024,3072]{1,0:T(8,128)(2,1)}, bf16[1024,1024]{1,0:T(8,128)(2,1)}, f32[16,1024]{1,0:T(8,128)}, f32[16,4096]{1,0:T(8,128)}) custom-call(s32[2,32]{1,0:T(2,128)} %pad_add_fusion.refs_0_, bf16[1024,1024]{1,0:T(8,128)(2,1)} %refs_1_.13, bf16[8,32,2176]{2,1,0:T(8,128)(2,1)} %pad_maximum_fusion.1.refs_2_.refs_13_, ...), custom_call_target="tpu_custom_call" | custom-call | flops 6442450944 | bytes 18874368 | tf_op jit(solution)/shard_map/project/pallas_call | solution.py:28
  95.7 2.9 collective-permute-done.17.refs_3_
  98.6 4.0 join.1
  104.8 29.9 %attention.1 = (f32[1024,1024]{1,0:T(8,128)}, f32[8,2,1024]{2,1,0:T(2,128)}) custom-call(s32[1]{0:T(128)S(6)} %copy.57.refs_0_, bf16[1024,3072]{1,0:T(8,128)(2,1)} %get-tuple-element.80.refs_1_.refs_2_.refs_3_, bf16[1024,3072]{1,0:T(8,128)(2,1)} %get-tuple-element.80.refs_1_.refs_2_.refs_3_, bf16[1024,3072]{1,0:T(8,128)(2,1)} %get-tuple-element.80.refs_1_.refs_2_.refs_3_, ...), custom_call_target="tpu_custom_call" | custom-call | flops 12884901888 | bytes 10485760 | tf_op jit(solution)/shard_map/attention/pallas_call | solution.py:28
  134.7 4.4 collective-permute-done.19.refs_1_
  143.7 8.0 %collective-permute-done.22.refs_13_ = bf16[8,32,3072]{2,1,0:T(8,128)(2,1)S(1)} collective-permute-done((bf16[8,32,3072]{2,1,0:T(8,128)(2,1)}, bf16[8,32,3072]{2,1,0:T(8,128)(2,1)S(1)}, u32[]{:S(2)}, u32[]{:S(2)}) %collective-permute-start.22) | collective-permute-done | bytes 1572896 | tf_op jit(solution)/shard_map/ppermute | solution.py:138
  152.9 76.1 %middle.1 = (bf16[1024,1024]{1,0:T(8,128)(2,1)}, bf16[1024,1024]{1,0:T(8,128)(2,1)}, bf16[1024,1024]{1,0:T(8,128)(2,1)}, bf16[4096,1024]{1,0:T(8,128)(2,1)}, bf1...) custom-call(s32[2,32]{1,0:T(2,128)} %pad_add_fusion.refs_0_, ...), custom_call_target="tpu_custom_call" | custom-call | flops 38654705664 | bytes 60817408 | tf_op jit(solution)/shard_map/middle/pallas_call | solution.py:28
  228.9 10.2 %grads_send.4.refs_6_ = bf16[16,32,4096]{2,1,0:T(8,128)(2,1)} custom-call(s32[1,16]{1,0:T(1,128)} %get-tuple-element.161.refs_0_, s32[2,4]{1,0:T(2,128)} %constant.69.clone.refs_1_, bf16[32,4,32,1024]{3,2,1,0:T(8,128)(2,1)} %bitcast.45, bf16[1024,1024]{1,0:T(8,128)(2,1)} %refs_3_.5), custom_call_target="tpu_custom_call" | custom-call | flops 1 | bytes 1 | tf_op jit(solution)/shard_map/grads_send/pallas_call | solution.py:28
  239.5 12.8 %grads_send.5.refs_5_ = bf16[16,32,5120]{2,1,0:T(8,128)(2,1)} custom-call(s32[1,16]{1,0:T(1,128)} %get-tuple-element.161.refs_0_, s32[4,5]{1,0:T(4,128)} %constant.70.clone.refs_1_, bf16[32,1,32,1024]{3,2,1,0:T(8,128)(2,1)} %bitcast.49, bf16[32,1,32,1024]{3,2,1,0:T(8,128)(2,1)} %bitcast.47, bf16[1024,4096]{1,0:T(8,128)(2,1)} %get-tuple-element.94.refs_4_, ...), custom_call_target="tpu_custom_call" | custom-call | flops 999999995904 | bytes 1 | tf_op jit(solution)/shard_map/grads_send/pallas_call | solution.py:28
  252.4 11.4 %grads_keep.4 = (bf16[8,32,4096]{2,1,0:T(8,128)(2,1)}, bf16[8,32,4096]{2,1,0:T(8,128)(2,1)}) custom-call(s32[1,16]{1,0:T(1,128)} %get-tuple-element.162.refs_0_, s32[2,4]{1,0:T(2,128)} %constant.69.clone.refs_1_, bf16[32,4,32,1024]{3,2,1,0:T(8,128)(2,1)} %bitcast.46, bf16[1024,1024]{1,0:T(8,128)(2,1)} %refs_3_.5, ...), custom_call_target="tpu_custom_call" | custom-call | flops 999999995904 | bytes 1 | tf_op jit(solution)/shard_map/grads_keep/pallas_call | solution.py:28
  264.8 14.3 %grads_keep.5 = (bf16[8,32,5120]{2,1,0:T(8,128)(2,1)}, bf16[8,32,5120]{2,1,0:T(8,128)(2,1)}) custom-call(s32[1,16]{1,0:T(1,128)} %get-tuple-element.162.refs_0_, s32[4,5]{1,0:T(4,128)} %constant.70.clone.refs_1_, bf16[32,1,32,1024]{3,2,1,0:T(8,128)(2,1)} %bitcast.50, bf16[32,1,32,1024]{3,2,1,0:T(8,128)(2,1)} %bitcast.48, ...), custom_call_target="tpu_custom_call" | custom-call | flops 1 | bytes 1 | tf_op jit(solution)/shard_map/grads_keep/pallas_call | solution.py:28
  280.1 17.1 %attention_back.3 = (bf16[1024,384]{1,0:T(8,128)(2,1)}, bf16[1024,384]{1,0:T(8,128)(2,1)}, bf16[1024,384]{1,0:T(8,128)(2,1)}) custom-call(s32[1]{0:T(128)S(6)} %copy.57.refs_0_, bf16[1024,3072]{1,0:T(8,128)(2,1)} %get-tuple-element.80.refs_1_.refs_2_.refs_3_, bf16[1024,3072]{1,0:T(8,128)(2,1)} %get-tuple-element.80.refs_1_.refs_2_.refs_3_, ...), custom_call_target="tpu_custom_call" | custom-call | flops 1 | bytes 1 | tf_op jit(solution)/shard_map/attention_back/pallas_call | solution.py:28
  297.3 3.1 halve.8
  301.1 16.9 %attention_back.4 = (bf16[1024,384]{1,0:T(8,128)(2,1)}, bf16[1024,384]{1,0:T(8,128)(2,1)}, bf16[1024,384]{1,0:T(8,128)(2,1)}) custom-call(s32[1]{0:T(128)S(6)} %copy.57.refs_0_, bf16[1024,3072]{1,0:T(8,128)(2,1)} %get-tuple-element.80.refs_1_.refs_2_.refs_3_, bf16[1024,3072]{1,0:T(8,128)(2,1)} %get-tuple-element.80.refs_1_.refs_2_.refs_3_, ...), custom_call_target="tpu_custom_call" | custom-call | flops 1 | bytes 1 | tf_op jit(solution)/shard_map/attention_back/pallas_call | solution.py:28
  318.6 9.0 %grads_send.6.refs_4_ = bf16[16,32,2304]{2,1,0:T(8,128)(2,1)} custom-call(s32[1,16]{1,0:T(1,128)} %get-tuple-element.161.refs_0_, s32[7,2]{1,0:T(8,128)} %call_exported.0.refs_1_, bf16[32,1,32,1024]{3,2,1,0:T(8,128)(2,1)} %bitcast.41, bf16[1024,384]{1,0:T(8,128)(2,1)} %get-tuple-element.99.refs_2_.refs_3_.refs_4_, ...), custom_call_target="tpu_custom_call" | custom-call | flops 1 | bytes 1 | tf_op jit(solution)/shard_map/grads_send/pallas_call | solution.py:28
  329.1 1.7 copy-done.1
  330.8 4.1 halve.9
  336.3 9.8 %grads_keep.6 = (bf16[8,32,2304]{2,1,0:T(8,128)(2,1)}, bf16[8,32,2304]{2,1,0:T(8,128)(2,1)}) custom-call(s32[1,16]{1,0:T(1,128)} %get-tuple-element.162.refs_0_, s32[7,2]{1,0:T(8,128)} %call_exported.0.refs_1_, bf16[32,1,32,1024]{3,2,1,0:T(8,128)(2,1)} %bitcast.42, bf16[1024,384]{1,0:T(8,128)(2,1)} %get-tuple-element.99.refs_2_.refs_3_.refs_4_, ...), custom_call_target="tpu_custom_call" | custom-call | flops 1 | bytes 1 | tf_op jit(solution)/shard_map/grads_keep/pallas_call | solution.py:28
  349.7 12.3 %attention_back.5 = (bf16[1024,256]{1,0:T(8,128)(2,1)}, bf16[1024,256]{1,0:T(8,128)(2,1)}, bf16[1024,256]{1,0:T(8,128)(2,1)}) custom-call(s32[1]{0:T(128)S(6)} %copy.57.refs_0_, bf16[1024,3072]{1,0:T(8,128)(2,1)} %get-tuple-element.80.refs_1_.refs_2_.refs_3_, bf16[1024,3072]{1,0:T(8,128)(2,1)} %get-tuple-element.80.refs_1_.refs_2_.refs_3_, ...), custom_call_target="tpu_custom_call" | custom-call | flops 1 | bytes 1 | tf_op jit(solution)/shard_map/attention_back/pallas_call | solution.py:28
  362.6 4.5 %grads_send.7.refs_6_ = bf16[16,32,768]{2,1,0:T(8,128)(2,1)} custom-call(s32[1,16]{1,0:T(1,128)} %get-tuple-element.161.refs_0_, s32[4,1]{1,0:T(4,128)} %call_exported.1.refs_1_, bf16[32,1,32,1024]{3,2,1,0:T(8,128)(2,1)} %bitcast.43, bf16[1024,256]{1,0:T(8,128)(2,1)} %get-tuple-element.112.refs_3_.refs_6_.refs_10_, ...), custom_call_target="tpu_custom_call" | custom-call | flops 1 | bytes 1 | tf_op jit(solution)/shard_map/grads_send/pallas_call | solution.py:28
  367.2 3.7 halve.10
  373.4 4.9 %grads_keep.7 = (bf16[8,32,768]{2,1,0:T(8,128)(2,1)}, bf16[8,32,768]{2,1,0:T(8,128)(2,1)}) custom-call(s32[1,16]{1,0:T(1,128)} %get-tuple-element.162.refs_0_, s32[4,1]{1,0:T(4,128)} %call_exported.1.refs_1_, bf16[32,1,32,1024]{3,2,1,0:T(8,128)(2,1)} %bitcast.44, bf16[1024,256]{1,0:T(8,128)(2,1)} %get-tuple-element.112.refs_3_.refs_6_.refs_10_, ...), custom_call_target="tpu_custom_call" | custom-call | flops 1 | bytes 1 | tf_op jit(solution)/shard_map/grads_keep/pallas_call | solution.py:28
  379.5 7.1 %collective-permute-start.48 = (bf16[1,32,4096]{2,1,0:T(8,128)(2,1)S(1)}, bf16[1,32,4096]{2,1,0:T(8,128)(2,1)S(1)}, u32[]{:S(2)}, u32[]{:S(2)}) collective-permute-start(bf16[1,32,4096]{2,1,0:T(8,128)(2,1)S(1)} %copy-done.11), channel_id=1, source_target_pairs={{0,16},{1,17},{2,18},{3,19},{4,20},{5,21},{6,22},{7,23},{8,24},{9,... | collective-permute-start | bytes 786440 | tf_op jit(solution)/shard_map/ppermute | solution.py:228
  386.5 18.0 %finish.1 = (f32[1024,1024]{1,0:T(8,128)}, f32[8,1024]{1,0:T(8,128)}) custom-call(s32[2,32]{1,0:T(2,128)} %pad_add_fusion.refs_0_, bf16[1024,1024]{1,0:T(8,128)(2,1)} %refs_1_.13, f32[1024,1024]{1,0:T(8,128)} %get-tuple-element.90.refs_2_, f32[16,1024]{1,0:T(8,128)} %get-tuple-element.81.refs_4_.refs_3_, ...), custom_call_target="tpu_custom_call" | custom-call | flops 1 | bytes 1 | tf_op jit(solution)/shard_map/finish/pallas_call | solution.py:28
  407.8 2.6 halve.11
  413.3 4.5 %collective-permute-done.38.refs_3_ = bf16[4,32,768]{2,1,0:T(8,128)(2,1)S(1)} collective-permute-done((bf16[4,32,768]{2,1,0:T(8,128)(2,1)}, bf16[4,32,768]{2,1,0:T(8,128)(2,1)S(1)}, u32[]{:S(2)}, u32[]{:S(2)}) %collective-permute-start.38) | collective-permute-done | bytes 196640 | tf_op jit(solution)/shard_map/ppermute | solution.py:228
  417.8 3.1 collective-permute-done.37.refs_1_
  421.0 2.0 halve.12
  425.6 2.7 collective-permute-done.41.refs_3_
  428.3 3.0 collective-permute-done.40.refs_1_
  431.3 1.6 halve.13
  438.5 2.2 collective-permute-done.46
  440.8 1.5 collective-permute-done.43.refs_1_
  443.7 1.6 collective-permute-start.44
  445.3 3.1 collective-permute-done.44
  (200 shorter events, 53.6 us)
Async XLA Ops:
  2.3 10.8 %collective-permute-start = (bf16[1,32,2176]{2,1,0:T(8,128)(2,1)S(1)}, bf16[1,32,2176]{2,1,0:T(8,128)(2,1)S(1)}, u32[]{:S(2)}, u32[]{:S(2)}) collective-permute-start(bf16[1,32,2176]{2,1,0:T(8,128)(2,1)S(1)} %fusion.8), channel_id=1, source_target_pairs={{0,16},{1,17},{2,18},{3,19},{4,20},{5,21},{6,22},{7,23},{8,24},{9,... | collective-permute-start | bytes 417800 | tf_op jit(solution)/shard_map/ppermute | solution.py:133
  13.1 6.6 %collective-permute-start.1 = (bf16[2,32,2176]{2,1,0:T(8,128)(2,1)S(1)}, bf16[2,32,2176]{2,1,0:T(8,128)(2,1)S(1)}, u32[]{:S(2)}, u32[]{:S(2)}) collective-permute-start(bf16[2,32,2176]{2,1,0:T(8,128)(2,1)S(1)} %pad_maximum_fusion.8), channel_id=1, source_target_pairs={{0,1},{1,0},{2,6},{3,7},{4,5},{5,4},{6,2},{7,3},{8,9},{9,8},{10,14... | collective-permute-start | bytes 835592 | tf_op jit(solution)/shard_map/ppermute | solution.py:133
  15.6 6.3 %collective-permute-start.6 = (bf16[1,32,1024]{2,1,0:T(8,128)(2,1)S(1)}, bf16[1,32,1024]{2,1,0:T(8,128)(2,1)S(1)}, u32[]{:S(2)}, u32[]{:S(2)}) collective-permute-start(bf16[1,32,1024]{2,1,0:T(8,128)(2,1)S(1)} %slice_bitcast_fusion.1), channel_id=1, source_target_pairs={{0,16},{1,17},{2,18},{3,19},{4,20},{5,21},{6,22},{7,23},{8,24},{9,... | collective-permute-start | bytes 196616 | tf_op jit(solution)/shard_map/ppermute | solution.py:133
  19.8 9.6 %collective-permute-start.2 = (bf16[4,32,2176]{2,1,0:T(8,128)(2,1)S(1)}, bf16[4,32,2176]{2,1,0:T(8,128)(2,1)S(1)}, u32[]{:S(2)}, u32[]{:S(2)}) collective-permute-start(bf16[4,32,2176]{2,1,0:T(8,128)(2,1)S(1)} %pad_maximum_fusion.4), channel_id=1, source_target_pairs={{0,4},{1,5},{2,10},{3,11},{4,0},{5,1},{6,14},{7,15},{8,12},{9,13},... | collective-permute-start | bytes 1671176 | tf_op jit(solution)/shard_map/ppermute | solution.py:133
  21.5 19.4 %collective-permute-start.12 = (bf16[1,32,6144]{2,1,0:T(8,128)(2,1)S(1)}, bf16[1,32,6144]{2,1,0:T(8,128)(2,1)S(1)}, u32[]{:S(2)}, u32[]{:S(2)}) collective-permute-start(bf16[1,32,6144]{2,1,0:T(8,128)(2,1)S(1)} %maximum_bitcast_fusion), channel_id=1, source_target_pairs={{0,16},{1,17},{2,18},{3,19},{4,20},{5,21},{6,22},{7,23},{8,24},{9,... | collective-permute-start | bytes 1179656 | tf_op jit(solution)/shard_map/ppermute | solution.py:133
  21.9 20.7 %collective-permute-start.7 = (bf16[2,32,1024]{2,1,0:T(8,128)(2,1)S(1)}, bf16[2,32,1024]{2,1,0:T(8,128)(2,1)S(1)}, u32[]{:S(2)}, u32[]{:S(2)}) collective-permute-start(bf16[2,32,1024]{2,1,0:T(8,128)(2,1)S(1)} %pad_maximum_fusion.10), channel_id=1, source_target_pairs={{0,8},{1,9},{2,10},{3,11},{4,12},{5,13},{6,14},{7,15},{8,0},{9,1},... | collective-permute-start | bytes 393224 | tf_op jit(solution)/shard_map/ppermute | solution.py:133
  30.6 35.6 %collective-permute-start.3 = (bf16[8,32,2176]{2,1,0:T(8,128)(2,1)}, bf16[8,32,2176]{2,1,0:T(8,128)(2,1)}, u32[]{:S(2)}, u32[]{:S(2)}) collective-permute-start(bf16[8,32,2176]{2,1,0:T(8,128)(2,1)} %pad_maximum_fusion.1.refs_2_.refs_13_), channel_id=1, source_target_pairs={{0,8},{1,9},{2,3},{3,2},{4,12},{5,13},{6,7},{7,6},{8,0},{9,1},{10,... | collective-permute-start | bytes 3342344 | tf_op jit(solution)/shard_map/ppermute | solution.py:133
  40.9 25.8 %collective-permute-start.13 = (bf16[2,32,6144]{2,1,0:T(8,128)(2,1)S(1)}, bf16[2,32,6144]{2,1,0:T(8,128)(2,1)S(1)}, u32[]{:S(2)}, u32[]{:S(2)}) collective-permute-start(bf16[2,32,6144]{2,1,0:T(8,128)(2,1)S(1)} %pad_maximum_fusion.2), channel_id=1, source_target_pairs={{0,1},{1,0},{2,6},{3,7},{4,5},{5,4},{6,2},{7,3},{8,9},{9,8},{10,14... | collective-permute-start | bytes 2359304 | tf_op jit(solution)/shard_map/ppermute | solution.py:133
  42.5 13.6 %collective-permute-start.14 = (bf16[1,32,3072]{2,1,0:T(8,128)(2,1)S(1)}, bf16[1,32,3072]{2,1,0:T(8,128)(2,1)S(1)}, u32[]{:S(2)}, u32[]{:S(2)}) collective-permute-start(bf16[1,32,3072]{2,1,0:T(8,128)(2,1)S(1)} %maximum_bitcast_fusion.1), channel_id=1, source_target_pairs={{0,16},{1,17},{2,18},{3,19},{4,20},{5,21},{6,22},{7,23},{8,24},{9,... | collective-permute-start | bytes 589832 | tf_op jit(solution)/shard_map/ppermute | solution.py:133
  42.6 22.1 %collective-permute-start.8 = (bf16[4,32,1024]{2,1,0:T(8,128)(2,1)S(1)}, bf16[4,32,1024]{2,1,0:T(8,128)(2,1)S(1)}, u32[]{:S(2)}, u32[]{:S(2)}) collective-permute-start(bf16[4,32,1024]{2,1,0:T(8,128)(2,1)S(1)} %pad_maximum_fusion.9), channel_id=1, source_target_pairs={{0,1},{1,0},{2,3},{3,2},{4,5},{5,4},{6,7},{7,6},{8,9},{9,8},{10,11... | collective-permute-start | bytes 786440 | tf_op jit(solution)/shard_map/ppermute | solution.py:133
  56.2 12.2 %collective-permute-start.15 = (bf16[2,32,3072]{2,1,0:T(8,128)(2,1)S(1)}, bf16[2,32,3072]{2,1,0:T(8,128)(2,1)S(1)}, u32[]{:S(2)}, u32[]{:S(2)}) collective-permute-start(bf16[2,32,3072]{2,1,0:T(8,128)(2,1)S(1)} %pad_maximum_fusion.7), channel_id=1, source_target_pairs={{0,8},{1,9},{2,10},{3,11},{4,12},{5,13},{6,14},{7,15},{8,0},{9,1},... | collective-permute-start | bytes 1179656 | tf_op jit(solution)/shard_map/ppermute | solution.py:133
  65.6 11.9 %collective-permute-start.9 = (bf16[8,32,1024]{2,1,0:T(8,128)(2,1)}, bf16[8,32,1024]{2,1,0:T(8,128)(2,1)}, u32[]{:S(2)}, u32[]{:S(2)}) collective-permute-start(bf16[8,32,1024]{2,1,0:T(8,128)(2,1)} %pad_maximum_fusion.5.refs_6_.refs_17_), channel_id=1, source_target_pairs={{0,4},{1,5},{2,6},{3,7},{4,0},{5,1},{6,2},{7,3},{8,12},{9,13},{10,... | collective-permute-start | bytes 1572872 | tf_op jit(solution)/shard_map/ppermute | solution.py:133
  66.2 13.6 %collective-permute-start.4 = (bf16[8,32,2176]{2,1,0:T(8,128)(2,1)}, bf16[8,32,2176]{2,1,0:T(8,128)(2,1)}, u32[]{:S(2)}, u32[]{:S(2)}) collective-permute-start(bf16[8,32,2176]{2,1,0:T(8,128)(2,1)} %pad_maximum_fusion.1.refs_2_.refs_13_), channel_id=1, source_target_pairs={{0,2},{1,3},{2,0},{3,1},{4,6},{5,7},{6,4},{7,5},{8,10},{9,11},{10,... | collective-permute-start | bytes 3342344 | tf_op jit(solution)/shard_map/ppermute | solution.py:138
  66.2 13.6 %collective-permute-start.5 = (bf16[8,32,2176]{2,1,0:T(8,128)(2,1)}, bf16[8,32,2176]{2,1,0:T(8,128)(2,1)}, u32[]{:S(2)}, u32[]{:S(2)}) collective-permute-start(bf16[8,32,2176]{2,1,0:T(8,128)(2,1)} %collective-permute-done.3.refs_3_.refs_14_), channel_id=1, source_target_pairs={{0,2},{1,3},{2,0},{3,1},{4,6},{5,7},{6,4},{7,5},{8,10},{9,11},{10,... | collective-permute-start | bytes 3342344 | tf_op jit(solution)/shard_map/ppermute | solution.py:141
  66.9 31.7 %collective-permute-start.16 = (bf16[4,32,6144]{2,1,0:T(8,128)(2,1)S(1)}, bf16[4,32,6144]{2,1,0:T(8,128)(2,1)S(1)}, u32[]{:S(2)}, u32[]{:S(2)}) collective-permute-start(bf16[4,32,6144]{2,1,0:T(8,128)(2,1)S(1)} %pad_maximum_fusion.refs_10_.refs_0_), channel_id=1, source_target_pairs={{0,4},{1,5},{2,10},{3,11},{4,0},{5,1},{6,14},{7,15},{8,12},{9,13},... | collective-permute-start | bytes 4718600 | tf_op jit(solution)/shard_map/ppermute | solution.py:133
  69.1 9.4 %collective-permute-start.10 = (bf16[8,32,1024]{2,1,0:T(8,128)(2,1)}, bf16[8,32,1024]{2,1,0:T(8,128)(2,1)}, u32[]{:S(2)}, u32[]{:S(2)}) collective-permute-start(bf16[8,32,1024]{2,1,0:T(8,128)(2,1)} %pad_maximum_fusion.5.refs_6_.refs_17_), channel_id=1, source_target_pairs={{0,2},{1,3},{2,0},{3,1},{4,6},{5,7},{6,4},{7,5},{8,10},{9,11},{10,... | collective-permute-start | bytes 1572872 | tf_op jit(solution)/shard_map/ppermute | solution.py:138
  78.5 20.0 %collective-permute-start.17 = (bf16[4,32,3072]{2,1,0:T(8,128)(2,1)S(1)}, bf16[4,32,3072]{2,1,0:T(8,128)(2,1)S(1)}, u32[]{:S(2)}, u32[]{:S(2)}) collective-permute-start(bf16[4,32,3072]{2,1,0:T(8,128)(2,1)S(1)} %pad_maximum_fusion.3.refs_11_.refs_2_), channel_id=1, source_target_pairs={{0,1},{1,0},{2,3},{3,2},{4,5},{5,4},{6,7},{7,6},{8,9},{9,8},{10,11... | collective-permute-start | bytes 2359304 | tf_op jit(solution)/shard_map/ppermute | solution.py:133
  102.6 37.5 %collective-permute-start.18 = (bf16[8,32,6144]{2,1,0:T(8,128)(2,1)}, bf16[8,32,6144]{2,1,0:T(8,128)(2,1)S(1)}, u32[]{:S(2)}, u32[]{:S(2)}) collective-permute-start(bf16[8,32,6144]{2,1,0:T(8,128)(2,1)} %get-tuple-element.82.refs_4_.refs_7_), channel_id=1, source_target_pairs={{0,8},{1,9},{2,3},{3,2},{4,12},{5,13},{6,7},{7,6},{8,0},{9,1},{10,... | collective-permute-start | bytes 9437192 | tf_op jit(solution)/shard_map/ppermute | solution.py:133
  102.6 36.5 %collective-permute-start.19 = (bf16[8,32,3072]{2,1,0:T(8,128)(2,1)}, bf16[8,32,3072]{2,1,0:T(8,128)(2,1)S(1)}, u32[]{:S(2)}, u32[]{:S(2)}) collective-permute-start(bf16[8,32,3072]{2,1,0:T(8,128)(2,1)} %get-tuple-element.83.refs_5_.refs_11_), channel_id=1, source_target_pairs={{0,4},{1,5},{2,6},{3,7},{4,0},{5,1},{6,2},{7,3},{8,12},{9,13},{10,... | collective-permute-start | bytes 4718600 | tf_op jit(solution)/shard_map/ppermute | solution.py:133
  104.0 47.7 %collective-permute-start.20 = (bf16[8,32,6144]{2,1,0:T(8,128)(2,1)}, bf16[8,32,6144]{2,1,0:T(8,128)(2,1)}, u32[]{:S(2)}, u32[]{:S(2)}) collective-permute-start(bf16[8,32,6144]{2,1,0:T(8,128)(2,1)} %get-tuple-element.82.refs_4_.refs_7_), channel_id=1, source_target_pairs={{0,2},{1,3},{2,0},{3,1},{4,6},{5,7},{6,4},{7,5},{8,10},{9,11},{10,... | collective-permute-start | bytes 9437192 | tf_op jit(solution)/shard_map/ppermute | solution.py:138
  141.7 10.5 %collective-permute-start.21 = (bf16[8,32,6144]{2,1,0:T(8,128)(2,1)}, bf16[8,32,6144]{2,1,0:T(8,128)(2,1)}, u32[]{:S(2)}, u32[]{:S(2)}) collective-permute-start(bf16[8,32,6144]{2,1,0:T(8,128)(2,1)} %get-tuple-element.87.refs_8_), channel_id=1, source_target_pairs={{0,2},{1,3},{2,0},{3,1},{4,6},{5,7},{6,4},{7,5},{8,10},{9,11},{10,... | collective-permute-start | bytes 9437192 | tf_op jit(solution)/shard_map/ppermute | solution.py:141
  141.7 10.0 %collective-permute-start.22 = (bf16[8,32,3072]{2,1,0:T(8,128)(2,1)}, bf16[8,32,3072]{2,1,0:T(8,128)(2,1)S(1)}, u32[]{:S(2)}, u32[]{:S(2)}) collective-permute-start(bf16[8,32,3072]{2,1,0:T(8,128)(2,1)} %get-tuple-element.83.refs_5_.refs_11_), channel_id=1, source_target_pairs={{0,2},{1,3},{2,0},{3,1},{4,6},{5,7},{6,4},{7,5},{8,10},{9,11},{10,... | collective-permute-start | bytes 4718600 | tf_op jit(solution)/shard_map/ppermute | solution.py:138
  142.2 10.0 %collective-permute-start.23 = (bf16[8,32,3072]{2,1,0:T(8,128)(2,1)}, bf16[8,32,3072]{2,1,0:T(8,128)(2,1)}, u32[]{:S(2)}, u32[]{:S(2)}) collective-permute-start(bf16[8,32,3072]{2,1,0:T(8,128)(2,1)} %get-tuple-element.88.refs_12_), channel_id=1, source_target_pairs={{0,2},{1,3},{2,0},{3,1},{4,6},{5,7},{6,4},{7,5},{8,10},{9,11},{10,... | collective-permute-start | bytes 4718600 | tf_op jit(solution)/shard_map/ppermute | solution.py:141
  239.1 13.3 %collective-permute-start.25 = (bf16[16,32,4096]{2,1,0:T(8,128)(2,1)}, bf16[16,32,4096]{2,1,0:T(8,128)(2,1)}, u32[]{:S(2)}, u32[]{:S(2)}) collective-permute-start(bf16[16,32,4096]{2,1,0:T(8,128)(2,1)} %grads_send.4.refs_6_), channel_id=1, source_target_pairs={{0,2},{1,3},{2,0},{3,1},{4,6},{5,7},{6,4},{7,5},{8,10},{9,11},{10,... | collective-permute-start | bytes 12582920 | tf_op jit(solution)/shard_map/ppermute | solution.py:271
  252.3 12.6 %collective-permute-start.24 = (bf16[16,32,5120]{2,1,0:T(8,128)(2,1)}, bf16[16,32,5120]{2,1,0:T(8,128)(2,1)}, u32[]{:S(2)}, u32[]{:S(2)}) collective-permute-start(bf16[16,32,5120]{2,1,0:T(8,128)(2,1)} %grads_send.5.refs_5_), channel_id=1, source_target_pairs={{0,2},{1,3},{2,0},{3,1},{4,6},{5,7},{6,4},{7,5},{8,10},{9,11},{10,... | collective-permute-start | bytes 15728648 | tf_op jit(solution)/shard_map/ppermute | solution.py:271
  263.8 33.4 %collective-permute-start.26 = (bf16[8,32,4096]{2,1,0:T(8,128)(2,1)}, bf16[8,32,4096]{2,1,0:T(8,128)(2,1)S(1)}, u32[]{:S(2)}, u32[]{:S(2)}) collective-permute-start(bf16[8,32,4096]{2,1,0:T(8,128)(2,1)} %get-tuple-element.97.refs_7_), channel_id=1, source_target_pairs={{0,1},{1,0},{2,6},{3,7},{4,5},{5,4},{6,2},{7,3},{8,9},{9,8},{10,14... | collective-permute-start | bytes 6291464 | tf_op jit(solution)/shard_map/ppermute | solution.py:228
  279.1 48.5 %collective-permute-start.29 = (bf16[8,32,5120]{2,1,0:T(8,128)(2,1)}, bf16[8,32,5120]{2,1,0:T(8,128)(2,1)S(1)}, u32[]{:S(2)}, u32[]{:S(2)}) collective-permute-start(bf16[8,32,5120]{2,1,0:T(8,128)(2,1)} %get-tuple-element.98.refs_7_), channel_id=1, source_target_pairs={{0,1},{1,0},{2,6},{3,7},{4,5},{5,4},{6,2},{7,3},{8,9},{9,8},{10,14... | collective-permute-start | bytes 7864328 | tf_op jit(solution)/shard_map/ppermute | solution.py:228
  300.4 27.2 %collective-permute-start.28 = (bf16[4,32,4096]{2,1,0:T(8,128)(2,1)}, bf16[4,32,4096]{2,1,0:T(8,128)(2,1)S(1)}, u32[]{:S(2)}, u32[]{:S(2)}) collective-permute-start(bf16[4,32,4096]{2,1,0:T(8,128)(2,1)} %get-tuple-element.103.refs_7_), channel_id=1, source_target_pairs={{0,4},{1,5},{2,10},{3,11},{4,0},{5,1},{6,14},{7,15},{8,12},{9,13},... | collective-permute-start | bytes 3145736 | tf_op jit(solution)/shard_map/ppermute | solution.py:228
  327.6 8.7 %collective-permute-start.27 = (bf16[16,32,2304]{2,1,0:T(8,128)(2,1)}, bf16[16,32,2304]{2,1,0:T(8,128)(2,1)}, u32[]{:S(2)}, u32[]{:S(2)}) collective-permute-start(bf16[16,32,2304]{2,1,0:T(8,128)(2,1)} %grads_send.6.refs_4_), channel_id=1, source_target_pairs={{0,2},{1,3},{2,0},{3,1},{4,6},{5,7},{6,4},{7,5},{8,10},{9,11},{10,... | collective-permute-start | bytes 7077896 | tf_op jit(solution)/shard_map/ppermute | solution.py:271
  334.9 32.2 %collective-permute-start.32 = (bf16[4,32,5120]{2,1,0:T(8,128)(2,1)}, bf16[4,32,5120]{2,1,0:T(8,128)(2,1)S(1)}, u32[]{:S(2)}, u32[]{:S(2)}) collective-permute-start(bf16[4,32,5120]{2,1,0:T(8,128)(2,1)} %get-tuple-element.117), channel_id=1, source_target_pairs={{0,4},{1,5},{2,10},{3,11},{4,0},{5,1},{6,14},{7,15},{8,12},{9,13},... | collective-permute-start | bytes 3932168 | tf_op jit(solution)/shard_map/ppermute | solution.py:228
  346.0 21.1 %collective-permute-start.33 = (bf16[8,32,2304]{2,1,0:T(8,128)(2,1)}, bf16[8,32,2304]{2,1,0:T(8,128)(2,1)S(1)}, u32[]{:S(2)}, u32[]{:S(2)}) collective-permute-start(bf16[8,32,2304]{2,1,0:T(8,128)(2,1)} %get-tuple-element.111.refs_7_), channel_id=1, source_target_pairs={{0,1},{1,0},{2,6},{3,7},{4,5},{5,4},{6,2},{7,3},{8,9},{9,8},{10,14... | collective-permute-start | bytes 3538952 | tf_op jit(solution)/shard_map/ppermute | solution.py:228
  347.0 20.1 %collective-permute-start.31 = (bf16[2,32,4096]{2,1,0:T(8,128)(2,1)S(1)}, bf16[2,32,4096]{2,1,0:T(8,128)(2,1)S(1)}, u32[]{:S(2)}, u32[]{:S(2)}) collective-permute-start(bf16[2,32,4096]{2,1,0:T(8,128)(2,1)S(1)} %copy-done.7), channel_id=1, source_target_pairs={{0,8},{1,9},{2,3},{3,2},{4,12},{5,13},{6,7},{7,6},{8,0},{9,1},{10,... | collective-permute-start | bytes 1572872 | tf_op jit(solution)/shard_map/ppermute | solution.py:228
  367.1 6.3 %collective-permute-start.30 = (bf16[16,32,768]{2,1,0:T(8,128)(2,1)}, bf16[16,32,768]{2,1,0:T(8,128)(2,1)}, u32[]{:S(2)}, u32[]{:S(2)}) collective-permute-start(bf16[16,32,768]{2,1,0:T(8,128)(2,1)} %grads_send.7.refs_6_), channel_id=1, source_target_pairs={{0,2},{1,3},{2,0},{3,1},{4,6},{5,7},{6,4},{7,5},{8,10},{9,11},{10,... | collective-permute-start | bytes 2359304 | tf_op jit(solution)/shard_map/ppermute | solution.py:271
  370.9 36.9 %collective-permute-start.34 = (bf16[2,32,5120]{2,1,0:T(8,128)(2,1)}, bf16[2,32,5120]{2,1,0:T(8,128)(2,1)S(1)}, u32[]{:S(2)}, u32[]{:S(2)}) collective-permute-start(bf16[2,32,5120]{2,1,0:T(8,128)(2,1)} %get-tuple-element.123), channel_id=1, source_target_pairs={{0,8},{1,9},{2,3},{3,2},{4,12},{5,13},{6,7},{7,6},{8,0},{9,1},{10,... | collective-permute-start | bytes 1966088 | tf_op jit(solution)/shard_map/ppermute | solution.py:228
  372.2 35.6 %collective-permute-start.35 = (bf16[4,32,2304]{2,1,0:T(8,128)(2,1)}, bf16[4,32,2304]{2,1,0:T(8,128)(2,1)S(1)}, u32[]{:S(2)}, u32[]{:S(2)}) collective-permute-start(bf16[4,32,2304]{2,1,0:T(8,128)(2,1)} %get-tuple-element.125), channel_id=1, source_target_pairs={{0,4},{1,5},{2,10},{3,11},{4,0},{5,1},{6,14},{7,15},{8,12},{9,13},... | collective-permute-start | bytes 1769480 | tf_op jit(solution)/shard_map/ppermute | solution.py:228
  378.3 29.5 %collective-permute-start.36 = (bf16[8,32,768]{2,1,0:T(8,128)(2,1)}, bf16[8,32,768]{2,1,0:T(8,128)(2,1)S(1)}, u32[]{:S(2)}, u32[]{:S(2)}) collective-permute-start(bf16[8,32,768]{2,1,0:T(8,128)(2,1)} %get-tuple-element.120.refs_21_), channel_id=1, source_target_pairs={{0,1},{1,0},{2,6},{3,7},{4,5},{5,4},{6,2},{7,3},{8,9},{9,8},{10,14... | collective-permute-start | bytes 1179656 | tf_op jit(solution)/shard_map/ppermute | solution.py:228
  379.5 32.3 %collective-permute-start.48 = (bf16[1,32,4096]{2,1,0:T(8,128)(2,1)S(1)}, bf16[1,32,4096]{2,1,0:T(8,128)(2,1)S(1)}, u32[]{:S(2)}, u32[]{:S(2)}) collective-permute-start(bf16[1,32,4096]{2,1,0:T(8,128)(2,1)S(1)} %copy-done.11), channel_id=1, source_target_pairs={{0,16},{1,17},{2,18},{3,19},{4,20},{5,21},{6,22},{7,23},{8,24},{9,... | collective-permute-start | bytes 786440 | tf_op jit(solution)/shard_map/ppermute | solution.py:228
  406.4 6.9 %collective-permute-start.39 = (f32[16,16,128]{2,1,0:T(8,128)S(1)}, f32[16,16,128]{2,1,0:T(8,128)S(1)}, u32[]{:S(2)}, u32[]{:S(2)}) collective-permute-start(f32[16,16,128]{2,1,0:T(8,128)S(1)} %gather_fusion.1), channel_id=1, source_target_pairs={{0,2},{1,3},{2,0},{3,1},{4,6},{5,7},{6,4},{7,5},{8,10},{9,11},{10,... | collective-permute-start | bytes 393224 | tf_op jit(solution)/shard_map/ppermute | solution.py:271
  410.5 10.5 %collective-permute-start.37 = (bf16[2,32,2304]{2,1,0:T(8,128)(2,1)}, bf16[2,32,2304]{2,1,0:T(8,128)(2,1)S(1)}, u32[]{:S(2)}, u32[]{:S(2)}) collective-permute-start(bf16[2,32,2304]{2,1,0:T(8,128)(2,1)} %get-tuple-element.129), channel_id=1, source_target_pairs={{0,8},{1,9},{2,3},{3,2},{4,12},{5,13},{6,7},{7,6},{8,0},{9,1},{10,... | collective-permute-start | bytes 884744 | tf_op jit(solution)/shard_map/ppermute | solution.py:228
  411.8 22.4 %collective-permute-start.47 = (bf16[1,32,5120]{2,1,0:T(8,128)(2,1)}, bf16[1,32,5120]{2,1,0:T(8,128)(2,1)S(1)}, u32[]{:S(2)}, u32[]{:S(2)}) collective-permute-start(bf16[1,32,5120]{2,1,0:T(8,128)(2,1)} %get-tuple-element.134.refs_6_), channel_id=1, source_target_pairs={{0,16},{1,17},{2,18},{3,19},{4,20},{5,21},{6,22},{7,23},{8,24},{9,... | collective-permute-start | bytes 983048 | tf_op jit(solution)/shard_map/ppermute | solution.py:228
  411.9 5.9 %collective-permute-start.38 = (bf16[4,32,768]{2,1,0:T(8,128)(2,1)}, bf16[4,32,768]{2,1,0:T(8,128)(2,1)S(1)}, u32[]{:S(2)}, u32[]{:S(2)}) collective-permute-start(bf16[4,32,768]{2,1,0:T(8,128)(2,1)} %get-tuple-element.131), channel_id=1, source_target_pairs={{0,4},{1,5},{2,10},{3,11},{4,0},{5,1},{6,14},{7,15},{8,12},{9,13},... | collective-permute-start | bytes 589832 | tf_op jit(solution)/shard_map/ppermute | solution.py:228
  422.9 8.4 %collective-permute-start.40 = (bf16[2,32,768]{2,1,0:T(8,128)(2,1)}, bf16[2,32,768]{2,1,0:T(8,128)(2,1)S(1)}, u32[]{:S(2)}, u32[]{:S(2)}) collective-permute-start(bf16[2,32,768]{2,1,0:T(8,128)(2,1)} %get-tuple-element.136), channel_id=1, source_target_pairs={{0,8},{1,9},{2,3},{3,2},{4,12},{5,13},{6,7},{7,6},{8,0},{9,1},{10,... | collective-permute-start | bytes 294920 | tf_op jit(solution)/shard_map/ppermute | solution.py:228
  423.7 4.6 %collective-permute-start.41 = (f32[8,16,128]{2,1,0:T(8,128)}, f32[8,16,128]{2,1,0:T(8,128)S(1)}, u32[]{:S(2)}, u32[]{:S(2)}) collective-permute-start(f32[8,16,128]{2,1,0:T(8,128)} %get-tuple-element.138), channel_id=1, source_target_pairs={{0,1},{1,0},{2,6},{3,7},{4,5},{5,4},{6,2},{7,3},{8,9},{9,8},{10,14... | collective-permute-start | bytes 196616 | tf_op jit(solution)/shard_map/ppermute | solution.py:228
  425.6 12.8 %collective-permute-start.45 = (bf16[1,32,2304]{2,1,0:T(8,128)(2,1)}, bf16[1,32,2304]{2,1,0:T(8,128)(2,1)S(1)}, u32[]{:S(2)}, u32[]{:S(2)}) collective-permute-start(bf16[1,32,2304]{2,1,0:T(8,128)(2,1)} %get-tuple-element.139.refs_4_), channel_id=1, source_target_pairs={{0,16},{1,17},{2,18},{3,19},{4,20},{5,21},{6,22},{7,23},{8,24},{9,... | collective-permute-start | bytes 442376 | tf_op jit(solution)/shard_map/ppermute | solution.py:228
  432.9 4.2 collective-permute-start.42
  435.8 5.0 %collective-permute-start.46 = (bf16[1,32,768]{2,1,0:T(8,128)(2,1)S(1)}, bf16[1,32,768]{2,1,0:T(8,128)(2,1)S(1)}, u32[]{:S(2)}, u32[]{:S(2)}) collective-permute-start(bf16[1,32,768]{2,1,0:T(8,128)(2,1)S(1)} %copy-done.15), channel_id=1, source_target_pairs={{0,16},{1,17},{2,18},{3,19},{4,20},{5,21},{6,22},{7,23},{8,24},{9,... | collective-permute-start | bytes 147464 | tf_op jit(solution)/shard_map/ppermute | solution.py:228
  438.4 3.9 collective-permute-start.43
  443.7 4.8 %collective-permute-start.44 = (f32[1,16,128]{2,1,0:T(8,128)}, f32[1,16,128]{2,1,0:T(8,128)S(1)}, u32[]{:S(2)}, u32[]{:S(2)}) collective-permute-start(f32[1,16,128]{2,1,0:T(8,128)} %get-tuple-element.146), channel_id=1, source_target_pairs={{0,16},{1,17},{2,18},{3,19},{4,20},{5,21},{6,22},{7,23},{8,24},{9,... | collective-permute-start | bytes 24584 | tf_op jit(solution)/shard_map/ppermute | solution.py:228
  (32 other events, 243.5 us)
where the time goes:
time: 458 us; the launch traced here: 451 us
  Pallas kernels  286 us (62%)
  waiting for transfers between devices  86.2 us (19%)
  starting transfers between devices  49.3 us (11%)
  local copies, waits for them, and re-layouts  18.3 us (4%)
  other arithmetic  8.55 us (2%)
    pallas_call x25, Pallas kernels, launch(): pl.pallas_call(body, grid_spec=pltpu.PrefetchScalarGridSpec(num_scalar_pr...  286 us
    ppermute x16, waiting for transfers between devices, step(): lax.ppermute(h, AXES, self.plan.pairs(part, self.at, True))  56.1 us
    ppermute x20, starting transfers between devices, send(): lax.ppermute(going, AXES, self.plan.pairs(self.part, self.at, False))  23.8 us
    ppermute x16, starting transfers between devices, step(): lax.ppermute(h, AXES, self.plan.pairs(part, self.at, True))  23.1 us
    ppermute x20, waiting for transfers between devices, send(): lax.ppermute(going, AXES, self.plan.pairs(self.part, self.at, False))  21.6 us
  transfers between devices with their start and end apart: 49, of which 21 were waited for; matrix products, arithmetic and copies ran while one was open for 4% of the time, Pallas kernels for 43%

commit v1 on v0

--- a/solution.py
+++ b/solution.py
@@ -152,7 +152,7 @@
         out[half:] = refs[2 * n + 1][...]
 
 
-def join_after(gathers, after):
+def join_after(gathers, after=()):
     args = [
         a
         for one in gathers
@@ -853,30 +853,27 @@
     )
 
 
-def finish_kernel(table_ref, x_ref, dx_ref, vec_ref, *refs, cut, n_parts):
+def finish_kernel(
+    table_ref, order_ref, x_ref, dx_ref, vec_ref, sums_ref, hid_sums_ref, heads_ref, *refs,
+    cut, n_parts, n_vec, n_hid,
+):
     grads_in, sources = refs[: 3 * n_parts], refs[3 * n_parts : 3 * n_parts + 8]
-    out_ref, sums_ref, w, acc, sem = refs[3 * n_parts + 8 :]
+    out_ref, keep_ref, send_ref, w, acc, rows, packed, sem = refs[3 * n_parts + 8 :]
     width = x_ref.shape[1]
 
     @pl.when(pl.program_id(0) == 0)
     def _():
         lines = weight_lines(w, cut, sources[0].shape[1])
         fetch("start", table_ref, sources, lines, sem)
-        sums_ref[...] = jnp.zeros_like(sums_ref)
+        rows[...] = jnp.zeros_like(rows)
         acc[...] = jnp.zeros_like(acc)
         fetch("wait", table_ref, sources, lines, sem)
 
-    da1 = 0.0
-    column = 0
-    for part in range(n_parts):
-        wide = grads_in[3 * part].shape[1]
-        for k in range(3):
-            grad = grads_in[3 * part + k][...]
-            da1 += dot_nt(grad, w[:, k * width + column : k * width + column + wide])
-            if k != 1:
-                row = 2 + k // 2
-                sums_ref[row : row + 1, column : column + wide] += column_sum(grad.astype(f32))
-        column += wide
+    ordered = [grads_in[3 * part + k][...] for k in range(3) for part in range(n_parts)]
+    grad = jnp.concatenate(ordered, 1)
+    da1 = dot_nt(grad, w[...])
+    for row, columns in ((2, slice(0, width)), (3, slice(2 * width, 3 * width))):
+        rows[row : row + 1, :] += column_sum(grad[:, columns].astype(f32))
     for r in strips(x_ref.shape[0], 16):
         grad = da1[r]
         unit, rate = normalized(x_ref[r, :].astype(f32))
@@ -886,32 +883,45 @@
 
     @pl.when(pl.program_id(0) == pl.num_programs(0) - 1)
     def _():
-        sums_ref[0:1, :] = column_sum(acc[:8])
-        sums_ref[1:2, :] = column_sum(acc[8:])
-
-
-def finish(plan, tokens, dx2, vec, parts, gathered, cut, after=(), blk=256):
+        rows[0:1, :] = column_sum(acc[:8])
+        rows[1:2, :] = column_sum(acc[8:])
+        rows[4:n_vec, :] = sums_ref[4:n_vec, :]
+        ways, _, lanes = packed.shape
+        group = width // ways
+        packed[...] = jnp.zeros_like(packed)
+        for g in range(ways):
+            packed[g, :n_vec, :group] = rows[:n_vec, g * group : (g + 1) * group]
+            packed[g, n_vec : n_vec + n_hid, :] = hid_sums_ref[:n_hid, g * lanes : (g + 1) * lanes]
+            packed[g, n_vec + n_hid : n_vec + n_hid + 1, :] = heads_ref[0:1, :]
+        for k in range(ways // 2):
+            keep_ref[k] = packed[order_ref[k]]
+            send_ref[k] = packed[order_ref[ways // 2 + k]]
+
+
+def finish(plan, order, tokens, dx2, vec, sums, parts, gathered, cut, n_vec, n_hid, after=(), blk=256):
     seq, width = tokens.shape
     blk = min(blk, seq)
     row = by_rows(blk, width)
     (table, *blocks), (table_spec, *specs) = block_operands(plan, gathered)
     grads_in = [g for part in parts for g in part]
+    lanes = sums[1].shape[1] // plan.ways
+    packed = jax.ShapeDtypeStruct((plan.half, 16, lanes), f32)
+    packed_spec = pl.BlockSpec(packed.shape, lambda i: (0, 0, 0))
     return launch(
-        functools.partial(finish_kernel, cut=cut, n_parts=len(parts)),
-        [table, tokens, dx2, vec, *grads_in, *blocks],
+        functools.partial(finish_kernel, cut=cut, n_parts=len(parts), n_vec=n_vec, n_hid=n_hid),
+        [table, order, tokens, dx2, vec, *sums, *grads_in, *blocks],
         after=after,
         grid=(seq // blk,),
-        in_specs=[table_spec, row, row, resident(vec.shape)]
+        in_specs=[table_spec, table_spec, row, row, *(resident(a.shape) for a in (vec, *sums))]
         + [by_rows(blk, g.shape[1]) for g in grads_in]
         + specs,
-        out_specs=[row, pl.BlockSpec((8, width), lambda i: (0, 0))],
-        out_shape=[
-            jax.ShapeDtypeStruct((seq, width), f32),
-            jax.ShapeDtypeStruct((8, width), f32),
-        ],
+        out_specs=[row, packed_spec, packed_spec],
+        out_shape=[jax.ShapeDtypeStruct((seq, width), f32), packed, packed],
         scratch_shapes=[
             pltpu.VMEM((width, 3 * width), bf16),
             pltpu.VMEM((16, width), f32),
+            pltpu.VMEM((16, width), f32),
+            pltpu.VMEM((plan.ways, 16, lanes), f32),
             pltpu.SemaphoreType.DMA((2, plan.ways)),
         ],
         name="finish",
@@ -964,15 +974,21 @@
         ],
     )
     first.step()
+    join_after([first])
+    first.step()
+    second.held = relay(second.held, first.held[:1])
     second.step()
     while first.at < plan.steps:
+        join_after([first])
         first.step()
     first.cross_held()
+    while second.at < plan.steps - 2:
+        second.step()
+    second.fresh = relay(second.fresh, first.fresh)
+    second.step()
     first.cross_fresh()
-    while second.at < plan.steps - 1:
-        second.step()
-
-    qkv, first_t, vec, hid = project(plan, tokens, first, cut, hidden, second.held)
+
+    qkv, first_t, vec, hid = project(plan, tokens, first, cut, hidden)
     join_after([second], [vec])
     second.step()
     second.cross_held()
@@ -1030,31 +1046,27 @@
     done, got = send_grads(jobs, 3 * rest, done)
     done = step_all([fc2_sum, fc1_sum, sum_a], done, True)
     done, sum_b = keep_grads(jobs, 3 * rest, got, done)
-    grad_tokens, last_sums = finish(
-        plan, tokens, grad_middle, vec, (part_a, part_b, part_c), first, cut, done
-    )
-    done = step_all([fc1_sum, sum_a, sum_b], [last_sums])
-
-    vec_grads = jnp.concatenate([last_sums[:4], sums[4:n_vec]], 0)
     head_sums = jnp.sum(sums[n_vec].reshape(heads, -1), axis=1)
-    vec_blocks = jnp.concatenate(
-        [
-            jnp.pad(
-                vec_grads.reshape(n_vec, ways, group).transpose(1, 0, 2),
-                ((0, 0), (0, 0), (0, lanes - group)),
-            ),
-            hid_sums[:n_hid].reshape(n_hid, ways, lanes).transpose(1, 0, 2),
-            jnp.broadcast_to(jnp.pad(head_sums, (0, lanes - heads)), (ways, 1, lanes)),
-            jnp.zeros((ways, 15 - n_vec - n_hid, lanes), f32),
-        ],
-        1,
-    )
-    got = to_other_core(plan, vec_blocks[table[half:]])
-    vec_sum = Scatter(plan, 0, vec_blocks[table[:half]], got)
-    done = step_all([sum_a, sum_b, vec_sum], done)
-    done = step_all([sum_b, vec_sum], done)
+    head_row = jnp.broadcast_to(jnp.pad(head_sums, (0, lanes - heads)), (8, lanes))
+    grad_tokens, vec_keep, vec_send = finish(
+        plan,
+        table,
+        tokens,
+        grad_middle,
+        vec,
+        (sums, hid_sums, head_row),
+        (part_a, part_b, part_c),
+        first,
+        cut,
+        n_vec,
+        n_hid,
+        done,
+    )
+    vec_sum = Scatter(plan, 0, vec_keep, to_other_core(plan, vec_send))
+    done = step_all([fc1_sum, sum_a, sum_b], [vec_keep], True)
+    done = step_all([vec_sum], done)
     while vec_sum.at < plan.steps:
-        done = step_all([vec_sum], done)
+        done = step_all([one for one in (sum_a, sum_b, vec_sum) if one.at < plan.steps], done)
     sent_vec = vec_sum.total()
     sent_a, sent_b = sum_a.total(), sum_b.total()
     sum_fc2, sum_fc1 = fc2_sum.total(), fc1_sum.total()

time: 458 us -> 447 us (0.976)
  waiting for transfers between devices: 86.2 us -> 71.6 us
  local copies, waits for them, and re-layouts: 18.3 us -> 23.5 us
  Pallas kernels: 286 us -> 291 us
    ppermute x16, waiting for transfers between devices: 56.1 us -> 44.9 us  [step(): lax.ppermute(h, AXES, self.plan.pairs(part, self.at, True))]
    unnamed x70 -> x86, local copies, waits for them, and re-layouts: 7.22 us -> 12.8 us
    pallas_call x25 -> x30, Pallas kernels: 286 us -> 291 us  [launch(): pl.pallas_call(body, grid_spec=pltpu.PrefetchScalarGridSpec(num_scalar_pr...]
  transfers between devices with their start and end apart: 49 -> 49, of which waited for: 21 -> 20; matrix products, arithmetic and copies ran while one was open for 4% -> 4% of each run, Pallas kernels for 43% -> 45%
where the time goes in v1:
time: 447 us; the launch traced here: 439 us
  Pallas kernels  291 us (65%)
  waiting for transfers between devices  71.6 us (16%)
  starting transfers between devices  45.2 us (10%)
  local copies, waits for them, and re-layouts  23.5 us (5%)
  other arithmetic  5.86 us (1%)
    pallas_call x30, Pallas kernels, launch(): pl.pallas_call(body, grid_spec=pltpu.PrefetchScalarGridSpec(num_scalar_pr...  291 us
    ppermute x16, waiting for transfers between devices, step(): lax.ppermute(h, AXES, self.plan.pairs(part, self.at, True))  44.9 us
    ppermute x20, starting transfers between devices, send(): lax.ppermute(going, AXES, self.plan.pairs(self.part, self.at, False))  21.9 us
    ppermute x16, starting transfers between devices, step(): lax.ppermute(h, AXES, self.plan.pairs(part, self.at, True))  20.8 us
    ppermute x20, waiting for transfers between devices, send(): lax.ppermute(going, AXES, self.plan.pairs(self.part, self.at, False))  18.8 us
    unnamed x86, local copies, waits for them, and re-layouts  12.8 us
  transfers between devices with their start and end apart: 49, of which 20 were waited for; matrix products, arithmetic and copies ran while one was open for 4% of the time, Pallas kernels for 45%

profile of v1, /device:TPU:0, one launch (start us, length us, event | category | flops | bytes accessed | tf_op | source)
XLA Modules:
  0.0 439.1 jit_solution(10452722893482423786)
XLA Ops:
  2.3 4.1 collective-permute-start
  8.3 1.7 maximum_bitcast_fusion.refs_0_
  10.0 5.9 %collective-permute-done.1.refs_3_ = bf16[1,32,1024]{2,1,0:T(8,128)(2,1)S(1)} collective-permute-done((bf16[1,32,1024]{2,1,0:T(8,128)(2,1)S(1)}, bf16[1,32,1024]{2,1,0:T(8,128)(2,1)S(1)}, u32[]{:S(2)}, u32[]{:S(2)}) %collective-permute-start.1) | collective-permute-done | bytes 65568 | tf_op jit(solution)/shard_map/ppermute | solution.py:133
  15.9 1.7 join.4
  20.5 3.4 collective-permute-start.12
  24.4 1.9 join.5
  26.3 2.1 collective-permute-start.4
  29.4 3.0 collective-permute-start.14
  33.7 6.6 %collective-permute-done.5.refs_3_ = bf16[4,32,1024]{2,1,0:T(8,128)(2,1)S(1)} collective-permute-done((bf16[4,32,1024]{2,1,0:T(8,128)(2,1)}, bf16[4,32,1024]{2,1,0:T(8,128)(2,1)S(1)}, u32[]{:S(2)}, u32[]{:S(2)}) %collective-permute-start.5) | collective-permute-done | bytes 262176 | tf_op jit(solution)/shard_map/ppermute | solution.py:133
  40.3 2.4 join.6
  43.0 3.6 collective-permute-done.12
  47.5 2.4 collective-permute-done.14
  50.7 19.4 %collective-permute-done.15.refs_1_ = bf16[2,32,3072]{2,1,0:T(8,128)(2,1)S(1)} collective-permute-done((bf16[2,32,3072]{2,1,0:T(8,128)(2,1)S(1)}, bf16[2,32,3072]{2,1,0:T(8,128)(2,1)S(1)}, u32[]{:S(2)}, u32[]{:S(2)}) %collective-permute-start.15) | collective-permute-done | bytes 393248 | tf_op jit(solution)/shard_map/ppermute | solution.py:133
  78.3 15.1 %project.1 = (bf16[1024,3072]{1,0:T(8,128)(2,1)}, bf16[1024,1024]{1,0:T(8,128)(2,1)}, f32[16,1024]{1,0:T(8,128)}, f32[16,4096]{1,0:T(8,128)}) custom-call(s32[2,32]{1,0:T(2,128)} %pad_add_fusion.refs_0_, bf16[1024,1024]{1,0:T(8,128)(2,1)} %refs_2_.1, bf16[8,32,2176]{2,1,0:T(8,128)(2,1)} %get-tuple-element.95.refs_2_.refs_17_, ...), custom_call_target="tpu_custom_call" | custom-call | flops 6442450944 | bytes 18874368 | tf_op jit(solution)/shard_map/project/pallas_call | solution.py:28
  93.4 1.9 collective-permute-done.17.refs_3_
  95.3 4.0 join.7
  102.1 29.9 %attention.1 = (f32[1024,1024]{1,0:T(8,128)}, f32[8,2,1024]{2,1,0:T(2,128)}) custom-call(s32[1]{0:T(128)S(6)} %copy.65.refs_0_, bf16[1024,3072]{1,0:T(8,128)(2,1)} %get-tuple-element.97.refs_1_.refs_2_.refs_3_, bf16[1024,3072]{1,0:T(8,128)(2,1)} %get-tuple-element.97.refs_1_.refs_2_.refs_3_, bf16[1024,3072]{1,0:T(8,128)(2,1)} %get-tuple-element.97.refs_1_.refs_2_.refs_3_, ...), custom_call_target="tpu_custom_call" | custom-call | flops 12884901888 | bytes 10485760 | tf_op jit(solution)/shard_map/attention/pallas_call | solution.py:28
  132.0 4.6 %collective-permute-done.19.refs_1_ = bf16[8,32,3072]{2,1,0:T(8,128)(2,1)S(1)} collective-permute-done((bf16[8,32,3072]{2,1,0:T(8,128)(2,1)}, bf16[8,32,3072]{2,1,0:T(8,128)(2,1)S(1)}, u32[]{:S(2)}, u32[]{:S(2)}) %collective-permute-start.19) | collective-permute-done | bytes 1572896 | tf_op jit(solution)/shard_map/ppermute | solution.py:133
  141.3 7.4 %collective-permute-done.22.refs_13_ = bf16[8,32,3072]{2,1,0:T(8,128)(2,1)S(1)} collective-permute-done((bf16[8,32,3072]{2,1,0:T(8,128)(2,1)}, bf16[8,32,3072]{2,1,0:T(8,128)(2,1)S(1)}, u32[]{:S(2)}, u32[]{:S(2)}) %collective-permute-start.22) | collective-permute-done | bytes 1572896 | tf_op jit(solution)/shard_map/ppermute | solution.py:138
  149.9 76.0 %middle.1 = (bf16[1024,1024]{1,0:T(8,128)(2,1)}, bf16[1024,1024]{1,0:T(8,128)(2,1)}, bf16[1024,1024]{1,0:T(8,128)(2,1)}, bf16[4096,1024]{1,0:T(8,128)(2,1)}, bf1...) custom-call(s32[2,32]{1,0:T(2,128)} %pad_add_fusion.refs_0_, ...), custom_call_target="tpu_custom_call" | custom-call | flops 38654705664 | bytes 60817408 | tf_op jit(solution)/shard_map/middle/pallas_call | solution.py:28
  226.0 10.2 %grads_send.4.refs_6_ = bf16[16,32,4096]{2,1,0:T(8,128)(2,1)} custom-call(s32[1,16]{1,0:T(1,128)} %get-tuple-element.181.refs_0_, s32[2,4]{1,0:T(2,128)} %constant.65.clone.refs_1_, bf16[32,4,32,1024]{3,2,1,0:T(8,128)(2,1)} %bitcast.38, bf16[1024,1024]{1,0:T(8,128)(2,1)} %refs_3_.5), custom_call_target="tpu_custom_call" | custom-call | flops 1 | bytes 1 | tf_op jit(solution)/shard_map/grads_send/pallas_call | solution.py:28
  236.5 12.7 %grads_send.5.refs_5_ = bf16[16,32,5120]{2,1,0:T(8,128)(2,1)} custom-call(s32[1,16]{1,0:T(1,128)} %get-tuple-element.181.refs_0_, s32[4,5]{1,0:T(4,128)} %constant.66.clone.refs_1_, bf16[32,1,32,1024]{3,2,1,0:T(8,128)(2,1)} %bitcast.42, bf16[32,1,32,1024]{3,2,1,0:T(8,128)(2,1)} %bitcast.40, bf16[1024,4096]{1,0:T(8,128)(2,1)} %get-tuple-element.117.refs_4_, ...), custom_call_target="tpu_custom_call" | custom-call | flops 999999995904 | bytes 1 | tf_op jit(solution)/shard_map/grads_send/pallas_call | solution.py:28
  249.4 11.4 %grads_keep.4 = (bf16[8,32,4096]{2,1,0:T(8,128)(2,1)}, bf16[8,32,4096]{2,1,0:T(8,128)(2,1)}) custom-call(s32[1,16]{1,0:T(1,128)} %get-tuple-element.182.refs_0_, s32[2,4]{1,0:T(2,128)} %constant.65.clone.refs_1_, bf16[32,4,32,1024]{3,2,1,0:T(8,128)(2,1)} %bitcast.39, bf16[1024,1024]{1,0:T(8,128)(2,1)} %refs_3_.5, ...), custom_call_target="tpu_custom_call" | custom-call | flops 999999995904 | bytes 1 | tf_op jit(solution)/shard_map/grads_keep/pallas_call | solution.py:28
  261.9 14.4 %grads_keep.5 = (bf16[8,32,5120]{2,1,0:T(8,128)(2,1)}, bf16[8,32,5120]{2,1,0:T(8,128)(2,1)}) custom-call(s32[1,16]{1,0:T(1,128)} %get-tuple-element.182.refs_0_, s32[4,5]{1,0:T(4,128)} %constant.66.clone.refs_1_, bf16[32,1,32,1024]{3,2,1,0:T(8,128)(2,1)} %bitcast.43, bf16[32,1,32,1024]{3,2,1,0:T(8,128)(2,1)} %bitcast.41, ...), custom_call_target="tpu_custom_call" | custom-call | flops 1 | bytes 1 | tf_op jit(solution)/shard_map/grads_keep/pallas_call | solution.py:28
  277.3 17.1 %attention_back.3 = (bf16[1024,384]{1,0:T(8,128)(2,1)}, bf16[1024,384]{1,0:T(8,128)(2,1)}, bf16[1024,384]{1,0:T(8,128)(2,1)}) custom-call(s32[1]{0:T(128)S(6)} %copy.65.refs_0_, bf16[1024,3072]{1,0:T(8,128)(2,1)} %get-tuple-element.97.refs_1_.refs_2_.refs_3_, bf16[1024,3072]{1,0:T(8,128)(2,1)} %get-tuple-element.97.refs_1_.refs_2_.refs_3_, ...), custom_call_target="tpu_custom_call" | custom-call | flops 1 | bytes 1 | tf_op jit(solution)/shard_map/attention_back/pallas_call | solution.py:28
  294.3 3.1 halve.8
  299.0 17.1 %attention_back.4 = (bf16[1024,384]{1,0:T(8,128)(2,1)}, bf16[1024,384]{1,0:T(8,128)(2,1)}, bf16[1024,384]{1,0:T(8,128)(2,1)}) custom-call(s32[1]{0:T(128)S(6)} %copy.65.refs_0_, bf16[1024,3072]{1,0:T(8,128)(2,1)} %get-tuple-element.97.refs_1_.refs_2_.refs_3_, bf16[1024,3072]{1,0:T(8,128)(2,1)} %get-tuple-element.97.refs_1_.refs_2_.refs_3_, ...), custom_call_target="tpu_custom_call" | custom-call | flops 1 | bytes 1 | tf_op jit(solution)/shard_map/attention_back/pallas_call | solution.py:28
  316.7 9.1 %grads_send.6.refs_4_ = bf16[16,32,2304]{2,1,0:T(8,128)(2,1)} custom-call(s32[1,16]{1,0:T(1,128)} %get-tuple-element.181.refs_0_, s32[7,2]{1,0:T(8,128)} %call_exported.0.refs_1_, bf16[32,1,32,1024]{3,2,1,0:T(8,128)(2,1)} %bitcast.34, bf16[1024,384]{1,0:T(8,128)(2,1)} %get-tuple-element.122.refs_2_.refs_3_.refs_8_, ...), custom_call_target="tpu_custom_call" | custom-call | flops 1 | bytes 1 | tf_op jit(solution)/shard_map/grads_send/pallas_call | solution.py:28
  327.3 1.7 copy-done.1
  329.0 4.1 halve.9
  333.6 9.7 %grads_keep.6 = (bf16[8,32,2304]{2,1,0:T(8,128)(2,1)}, bf16[8,32,2304]{2,1,0:T(8,128)(2,1)}) custom-call(s32[1,16]{1,0:T(1,128)} %get-tuple-element.182.refs_0_, s32[7,2]{1,0:T(8,128)} %call_exported.0.refs_1_, bf16[32,1,32,1024]{3,2,1,0:T(8,128)(2,1)} %bitcast.35, bf16[1024,384]{1,0:T(8,128)(2,1)} %get-tuple-element.122.refs_2_.refs_3_.refs_8_, ...), custom_call_target="tpu_custom_call" | custom-call | flops 1 | bytes 1 | tf_op jit(solution)/shard_map/grads_keep/pallas_call | solution.py:28
  345.6 12.3 %attention_back.5 = (bf16[1024,256]{1,0:T(8,128)(2,1)}, bf16[1024,256]{1,0:T(8,128)(2,1)}, bf16[1024,256]{1,0:T(8,128)(2,1)}) custom-call(s32[1]{0:T(128)S(6)} %copy.65.refs_0_, bf16[1024,3072]{1,0:T(8,128)(2,1)} %get-tuple-element.97.refs_1_.refs_2_.refs_3_, bf16[1024,3072]{1,0:T(8,128)(2,1)} %get-tuple-element.97.refs_1_.refs_2_.refs_3_, ...), custom_call_target="tpu_custom_call" | custom-call | flops 1 | bytes 1 | tf_op jit(solution)/shard_map/attention_back/pallas_call | solution.py:28
  358.4 4.5 %grads_send.7.refs_6_ = bf16[16,32,768]{2,1,0:T(8,128)(2,1)} custom-call(s32[1,16]{1,0:T(1,128)} %get-tuple-element.181.refs_0_, s32[4,1]{1,0:T(4,128)} %call_exported.1.refs_1_, bf16[32,1,32,1024]{3,2,1,0:T(8,128)(2,1)} %bitcast.36, bf16[1024,256]{1,0:T(8,128)(2,1)} %get-tuple-element.135.refs_3_.refs_6_.refs_14_, ...), custom_call_target="tpu_custom_call" | custom-call | flops 1 | bytes 1 | tf_op jit(solution)/shard_map/grads_send/pallas_call | solution.py:28
  363.0 1.9 collective-permute-done.33.refs_5_
  364.9 3.6 halve.10
  370.6 4.7 %grads_keep.7 = (bf16[8,32,768]{2,1,0:T(8,128)(2,1)}, bf16[8,32,768]{2,1,0:T(8,128)(2,1)}) custom-call(s32[1,16]{1,0:T(1,128)} %get-tuple-element.182.refs_0_, s32[4,1]{1,0:T(4,128)} %call_exported.1.refs_1_, bf16[32,1,32,1024]{3,2,1,0:T(8,128)(2,1)} %bitcast.37, bf16[1024,256]{1,0:T(8,128)(2,1)} %get-tuple-element.135.refs_3_.refs_6_.refs_14_, ...), custom_call_target="tpu_custom_call" | custom-call | flops 1 | bytes 1 | tf_op jit(solution)/shard_map/grads_keep/pallas_call | solution.py:28
  377.5 2.1 collective-permute-start.48
  380.2 16.5 %finish.1 = (f32[1024,1024]{1,0:T(8,128)}, f32[16,16,128]{2,1,0:T(8,128)}, f32[16,16,128]{2,1,0:T(8,128)}) custom-call(s32[2,32]{1,0:T(2,128)} %pad_add_fusion.refs_0_, s32[32]{0:T(128)} %copy-done.27, bf16[1024,1024]{1,0:T(8,128)(2,1)} %refs_2_.1, f32[1024,1024]{1,0:T(8,128)} %get-tuple-element.111.refs_3_, f32[16,1024]{1,0:T(8,128)} %get-tuple-element.102.refs_4_, ...), custom_call_target="tpu_custom_call" | custom-call | flops 1 | bytes 1 | tf_op jit(solution)/shard_map/finish/pallas_call | solution.py:28
  396.9 2.7 halve.11
  399.6 1.6 halve.12
  406.1 2.7 collective-permute-done.38.refs_3_
  408.8 4.6 %collective-permute-done.37.refs_1_ = bf16[2,32,2304]{2,1,0:T(8,128)(2,1)S(1)} collective-permute-done((bf16[2,32,2304]{2,1,0:T(8,128)(2,1)}, bf16[2,32,2304]{2,1,0:T(8,128)(2,1)S(1)}, u32[]{:S(2)}, u32[]{:S(2)}) %collective-permute-start.37) | collective-permute-done | bytes 294944 | tf_op jit(solution)/shard_map/ppermute | solution.py:228
  413.4 1.9 halve.13
  415.3 1.6 collective-permute-start.42
  417.0 2.5 collective-permute-done.42.refs_3_
  419.5 4.8 %collective-permute-done.41.refs_1_ = bf16[2,32,768]{2,1,0:T(8,128)(2,1)S(1)} collective-permute-done((bf16[2,32,768]{2,1,0:T(8,128)(2,1)}, bf16[2,32,768]{2,1,0:T(8,128)(2,1)S(1)}, u32[]{:S(2)}, u32[]{:S(2)}) %collective-permute-start.41) | collective-permute-done | bytes 98336 | tf_op jit(solution)/shard_map/ppermute | solution.py:228
  426.8 1.9 collective-permute-start.45
  432.8 2.9 collective-permute-start.46
  (202 shorter events, 56.2 us)
Async XLA Ops:
  2.3 13.6 %collective-permute-start = (bf16[1,32,2176]{2,1,0:T(8,128)(2,1)S(1)}, bf16[1,32,2176]{2,1,0:T(8,128)(2,1)S(1)}, u32[]{:S(2)}, u32[]{:S(2)}) collective-permute-start(bf16[1,32,2176]{2,1,0:T(8,128)(2,1)S(1)} %fusion.6.refs_0_), channel_id=1, source_target_pairs={{0,16},{1,17},{2,18},{3,19},{4,20},{5,21},{6,22},{7,23},{8,24},{9,... | collective-permute-start | bytes 417800 | tf_op jit(solution)/shard_map/ppermute | solution.py:133
  7.3 8.6 %collective-permute-start.1 = (bf16[1,32,1024]{2,1,0:T(8,128)(2,1)S(1)}, bf16[1,32,1024]{2,1,0:T(8,128)(2,1)S(1)}, u32[]{:S(2)}, u32[]{:S(2)}) collective-permute-start(bf16[1,32,1024]{2,1,0:T(8,128)(2,1)S(1)} %slice_bitcast_fusion.refs_2_), channel_id=1, source_target_pairs={{0,16},{1,17},{2,18},{3,19},{4,20},{5,21},{6,22},{7,23},{8,24},{9,... | collective-permute-start | bytes 196616 | tf_op jit(solution)/shard_map/ppermute | solution.py:133
  17.6 6.8 %collective-permute-start.2 = (bf16[2,32,2176]{2,1,0:T(8,128)(2,1)}, bf16[2,32,2176]{2,1,0:T(8,128)(2,1)S(1)}, u32[]{:S(2)}, u32[]{:S(2)}) collective-permute-start(bf16[2,32,2176]{2,1,0:T(8,128)(2,1)} %get-tuple-element.91.refs_0_.refs_2_), channel_id=1, source_target_pairs={{0,1},{1,0},{2,6},{3,7},{4,5},{5,4},{6,2},{7,3},{8,9},{9,8},{10,14... | collective-permute-start | bytes 835592 | tf_op jit(solution)/shard_map/ppermute | solution.py:133
  19.2 5.2 %collective-permute-start.3 = (bf16[2,32,1024]{2,1,0:T(8,128)(2,1)}, bf16[2,32,1024]{2,1,0:T(8,128)(2,1)S(1)}, u32[]{:S(2)}, u32[]{:S(2)}) collective-permute-start(bf16[2,32,1024]{2,1,0:T(8,128)(2,1)} %get-tuple-element.92.refs_2_), channel_id=1, source_target_pairs={{0,8},{1,9},{2,10},{3,11},{4,12},{5,13},{6,14},{7,15},{8,0},{9,1},... | collective-permute-start | bytes 393224 | tf_op jit(solution)/shard_map/ppermute | solution.py:133
  20.5 26.1 %collective-permute-start.12 = (bf16[1,32,6144]{2,1,0:T(8,128)(2,1)}, bf16[1,32,6144]{2,1,0:T(8,128)(2,1)S(1)}, u32[]{:S(2)}, u32[]{:S(2)}) collective-permute-start(bf16[1,32,6144]{2,1,0:T(8,128)(2,1)} %get-tuple-element.98), channel_id=1, source_target_pairs={{0,16},{1,17},{2,18},{3,19},{4,20},{5,21},{6,22},{7,23},{8,24},{9,... | collective-permute-start | bytes 1179656 | tf_op jit(solution)/shard_map/ppermute | solution.py:133
  26.3 14.0 %collective-permute-start.4 = (bf16[4,32,2176]{2,1,0:T(8,128)(2,1)}, bf16[4,32,2176]{2,1,0:T(8,128)(2,1)S(1)}, u32[]{:S(2)}, u32[]{:S(2)}) collective-permute-start(bf16[4,32,2176]{2,1,0:T(8,128)(2,1)} %get-tuple-element.93.refs_0_), channel_id=1, source_target_pairs={{0,4},{1,5},{2,10},{3,11},{4,0},{5,1},{6,14},{7,15},{8,12},{9,13},... | collective-permute-start | bytes 1671176 | tf_op jit(solution)/shard_map/ppermute | solution.py:133
  29.4 20.5 %collective-permute-start.14 = (bf16[1,32,3072]{2,1,0:T(8,128)(2,1)}, bf16[1,32,3072]{2,1,0:T(8,128)(2,1)S(1)}, u32[]{:S(2)}, u32[]{:S(2)}) collective-permute-start(bf16[1,32,3072]{2,1,0:T(8,128)(2,1)} %get-tuple-element.99), channel_id=1, source_target_pairs={{0,16},{1,17},{2,18},{3,19},{4,20},{5,21},{6,22},{7,23},{8,24},{9,... | collective-permute-start | bytes 589832 | tf_op jit(solution)/shard_map/ppermute | solution.py:133
  32.3 7.9 %collective-permute-start.5 = (bf16[4,32,1024]{2,1,0:T(8,128)(2,1)}, bf16[4,32,1024]{2,1,0:T(8,128)(2,1)S(1)}, u32[]{:S(2)}, u32[]{:S(2)}) collective-permute-start(bf16[4,32,1024]{2,1,0:T(8,128)(2,1)} %get-tuple-element.94.refs_2_), channel_id=1, source_target_pairs={{0,1},{1,0},{2,3},{3,2},{4,5},{5,4},{6,7},{7,6},{8,9},{9,8},{10,11... | collective-permute-start | bytes 786440 | tf_op jit(solution)/shard_map/ppermute | solution.py:133
  42.6 27.5 %collective-permute-start.6 = (bf16[8,32,2176]{2,1,0:T(8,128)(2,1)}, bf16[8,32,2176]{2,1,0:T(8,128)(2,1)S(1)}, u32[]{:S(2)}, u32[]{:S(2)}) collective-permute-start(bf16[8,32,2176]{2,1,0:T(8,128)(2,1)} %get-tuple-element.95.refs_2_.refs_17_), channel_id=1, source_target_pairs={{0,8},{1,9},{2,3},{3,2},{4,12},{5,13},{6,7},{7,6},{8,0},{9,1},{10,... | collective-permute-start | bytes 3342344 | tf_op jit(solution)/shard_map/ppermute | solution.py:133
  46.7 23.9 %collective-permute-start.13 = (bf16[2,32,6144]{2,1,0:T(8,128)(2,1)S(1)}, bf16[2,32,6144]{2,1,0:T(8,128)(2,1)S(1)}, u32[]{:S(2)}, u32[]{:S(2)}) collective-permute-start(bf16[2,32,6144]{2,1,0:T(8,128)(2,1)S(1)} %pad_maximum_fusion), channel_id=1, source_target_pairs={{0,1},{1,0},{2,6},{3,7},{4,5},{5,4},{6,2},{7,3},{8,9},{9,8},{10,14... | collective-permute-start | bytes 2359304 | tf_op jit(solution)/shard_map/ppermute | solution.py:133
  49.9 20.2 %collective-permute-start.15 = (bf16[2,32,3072]{2,1,0:T(8,128)(2,1)S(1)}, bf16[2,32,3072]{2,1,0:T(8,128)(2,1)S(1)}, u32[]{:S(2)}, u32[]{:S(2)}) collective-permute-start(bf16[2,32,3072]{2,1,0:T(8,128)(2,1)S(1)} %pad_maximum_fusion.2), channel_id=1, source_target_pairs={{0,8},{1,9},{2,10},{3,11},{4,12},{5,13},{6,14},{7,15},{8,0},{9,1},... | collective-permute-start | bytes 1179656 | tf_op jit(solution)/shard_map/ppermute | solution.py:133
  50.0 20.7 %collective-permute-start.9 = (bf16[8,32,1024]{2,1,0:T(8,128)(2,1)}, bf16[8,32,1024]{2,1,0:T(8,128)(2,1)S(1)}, u32[]{:S(2)}, u32[]{:S(2)}) collective-permute-start(bf16[8,32,1024]{2,1,0:T(8,128)(2,1)} %get-tuple-element.96.refs_6_.refs_21_), channel_id=1, source_target_pairs={{0,4},{1,5},{2,6},{3,7},{4,0},{5,1},{6,2},{7,3},{8,12},{9,13},{10,... | collective-permute-start | bytes 1572872 | tf_op jit(solution)/shard_map/ppermute | solution.py:133
  50.7 26.8 %collective-permute-start.7 = (bf16[8,32,2176]{2,1,0:T(8,128)(2,1)S(1)}, bf16[8,32,2176]{2,1,0:T(8,128)(2,1)}, u32[]{:S(2)}, u32[]{:S(2)}) collective-permute-start(bf16[8,32,2176]{2,1,0:T(8,128)(2,1)S(1)} %copy-done.13), channel_id=1, source_target_pairs={{0,2},{1,3},{2,0},{3,1},{4,6},{5,7},{6,4},{7,5},{8,10},{9,11},{10,... | collective-permute-start | bytes 3342344 | tf_op jit(solution)/shard_map/ppermute | solution.py:138
  70.1 5.2 %collective-permute-start.10 = (bf16[8,32,1024]{2,1,0:T(8,128)(2,1)}, bf16[8,32,1024]{2,1,0:T(8,128)(2,1)}, u32[]{:S(2)}, u32[]{:S(2)}) collective-permute-start(bf16[8,32,1024]{2,1,0:T(8,128)(2,1)} %get-tuple-element.96.refs_6_.refs_21_), channel_id=1, source_target_pairs={{0,2},{1,3},{2,0},{3,1},{4,6},{5,7},{6,4},{7,5},{8,10},{9,11},{10,... | collective-permute-start | bytes 1572872 | tf_op jit(solution)/shard_map/ppermute | solution.py:138
  70.1 7.3 %collective-permute-start.8 = (bf16[8,32,2176]{2,1,0:T(8,128)(2,1)S(1)}, bf16[8,32,2176]{2,1,0:T(8,128)(2,1)}, u32[]{:S(2)}, u32[]{:S(2)}) collective-permute-start(bf16[8,32,2176]{2,1,0:T(8,128)(2,1)S(1)} %collective-permute-done.6.refs_3_.refs_2_.refs_18_), channel_id=1, source_target_pairs={{0,2},{1,3},{2,0},{3,1},{4,6},{5,7},{6,4},{7,5},{8,10},{9,11},{10,... | collective-permute-start | bytes 3342344 | tf_op jit(solution)/shard_map/ppermute | solution.py:141
  73.6 21.7 %collective-permute-start.16 = (bf16[4,32,6144]{2,1,0:T(8,128)(2,1)S(1)}, bf16[4,32,6144]{2,1,0:T(8,128)(2,1)S(1)}, u32[]{:S(2)}, u32[]{:S(2)}) collective-permute-start(bf16[4,32,6144]{2,1,0:T(8,128)(2,1)S(1)} %constant_dynamic-update-slice_fusion.refs_0_), channel_id=1, source_target_pairs={{0,4},{1,5},{2,10},{3,11},{4,0},{5,1},{6,14},{7,15},{8,12},{9,13},... | collective-permute-start | bytes 4718600 | tf_op jit(solution)/shard_map/ppermute | solution.py:133
  75.3 19.9 %collective-permute-start.17 = (bf16[4,32,3072]{2,1,0:T(8,128)(2,1)S(1)}, bf16[4,32,3072]{2,1,0:T(8,128)(2,1)S(1)}, u32[]{:S(2)}, u32[]{:S(2)}) collective-permute-start(bf16[4,32,3072]{2,1,0:T(8,128)(2,1)S(1)} %constant_dynamic-update-slice_fusion.3.refs_2_), channel_id=1, source_target_pairs={{0,1},{1,0},{2,3},{3,2},{4,5},{5,4},{6,7},{7,6},{8,9},{9,8},{10,11... | collective-permute-start | bytes 2359304 | tf_op jit(solution)/shard_map/ppermute | solution.py:133
  99.2 37.5 %collective-permute-start.18 = (bf16[8,32,6144]{2,1,0:T(8,128)(2,1)}, bf16[8,32,6144]{2,1,0:T(8,128)(2,1)S(1)}, u32[]{:S(2)}, u32[]{:S(2)}) collective-permute-start(bf16[8,32,6144]{2,1,0:T(8,128)(2,1)} %get-tuple-element.103.refs_4_.refs_7_), channel_id=1, source_target_pairs={{0,8},{1,9},{2,3},{3,2},{4,12},{5,13},{6,7},{7,6},{8,0},{9,1},{10,... | collective-permute-start | bytes 9437192 | tf_op jit(solution)/shard_map/ppermute | solution.py:133
  100.3 36.3 %collective-permute-start.19 = (bf16[8,32,3072]{2,1,0:T(8,128)(2,1)}, bf16[8,32,3072]{2,1,0:T(8,128)(2,1)S(1)}, u32[]{:S(2)}, u32[]{:S(2)}) collective-permute-start(bf16[8,32,3072]{2,1,0:T(8,128)(2,1)} %get-tuple-element.104.refs_5_.refs_11_), channel_id=1, source_target_pairs={{0,4},{1,5},{2,6},{3,7},{4,0},{5,1},{6,2},{7,3},{8,12},{9,13},{10,... | collective-permute-start | bytes 4718600 | tf_op jit(solution)/shard_map/ppermute | solution.py:133
  101.5 47.2 %collective-permute-start.20 = (bf16[8,32,6144]{2,1,0:T(8,128)(2,1)}, bf16[8,32,6144]{2,1,0:T(8,128)(2,1)}, u32[]{:S(2)}, u32[]{:S(2)}) collective-permute-start(bf16[8,32,6144]{2,1,0:T(8,128)(2,1)} %get-tuple-element.103.refs_4_.refs_7_), channel_id=1, source_target_pairs={{0,2},{1,3},{2,0},{3,1},{4,6},{5,7},{6,4},{7,5},{8,10},{9,11},{10,... | collective-permute-start | bytes 9437192 | tf_op jit(solution)/shard_map/ppermute | solution.py:138
  138.7 10.5 %collective-permute-start.21 = (bf16[8,32,6144]{2,1,0:T(8,128)(2,1)}, bf16[8,32,6144]{2,1,0:T(8,128)(2,1)}, u32[]{:S(2)}, u32[]{:S(2)}) collective-permute-start(bf16[8,32,6144]{2,1,0:T(8,128)(2,1)} %get-tuple-element.108.refs_8_), channel_id=1, source_target_pairs={{0,2},{1,3},{2,0},{3,1},{4,6},{5,7},{6,4},{7,5},{8,10},{9,11},{10,... | collective-permute-start | bytes 9437192 | tf_op jit(solution)/shard_map/ppermute | solution.py:141
  138.7 10.0 %collective-permute-start.22 = (bf16[8,32,3072]{2,1,0:T(8,128)(2,1)}, bf16[8,32,3072]{2,1,0:T(8,128)(2,1)S(1)}, u32[]{:S(2)}, u32[]{:S(2)}) collective-permute-start(bf16[8,32,3072]{2,1,0:T(8,128)(2,1)} %get-tuple-element.104.refs_5_.refs_11_), channel_id=1, source_target_pairs={{0,2},{1,3},{2,0},{3,1},{4,6},{5,7},{6,4},{7,5},{8,10},{9,11},{10,... | collective-permute-start | bytes 4718600 | tf_op jit(solution)/shard_map/ppermute | solution.py:138
  139.2 10.0 %collective-permute-start.23 = (bf16[8,32,3072]{2,1,0:T(8,128)(2,1)}, bf16[8,32,3072]{2,1,0:T(8,128)(2,1)}, u32[]{:S(2)}, u32[]{:S(2)}) collective-permute-start(bf16[8,32,3072]{2,1,0:T(8,128)(2,1)} %get-tuple-element.109.refs_12_), channel_id=1, source_target_pairs={{0,2},{1,3},{2,0},{3,1},{4,6},{5,7},{6,4},{7,5},{8,10},{9,11},{10,... | collective-permute-start | bytes 4718600 | tf_op jit(solution)/shard_map/ppermute | solution.py:141
  236.2 13.2 %collective-permute-start.25 = (bf16[16,32,4096]{2,1,0:T(8,128)(2,1)}, bf16[16,32,4096]{2,1,0:T(8,128)(2,1)}, u32[]{:S(2)}, u32[]{:S(2)}) collective-permute-start(bf16[16,32,4096]{2,1,0:T(8,128)(2,1)} %grads_send.4.refs_6_), channel_id=1, source_target_pairs={{0,2},{1,3},{2,0},{3,1},{4,6},{5,7},{6,4},{7,5},{8,10},{9,11},{10,... | collective-permute-start | bytes 12582920 | tf_op jit(solution)/shard_map/ppermute | solution.py:271
  249.2 12.7 %collective-permute-start.24 = (bf16[16,32,5120]{2,1,0:T(8,128)(2,1)}, bf16[16,32,5120]{2,1,0:T(8,128)(2,1)}, u32[]{:S(2)}, u32[]{:S(2)}) collective-permute-start(bf16[16,32,5120]{2,1,0:T(8,128)(2,1)} %grads_send.5.refs_5_), channel_id=1, source_target_pairs={{0,2},{1,3},{2,0},{3,1},{4,6},{5,7},{6,4},{7,5},{8,10},{9,11},{10,... | collective-permute-start | bytes 15728648 | tf_op jit(solution)/shard_map/ppermute | solution.py:271
  260.8 33.5 %collective-permute-start.26 = (bf16[8,32,4096]{2,1,0:T(8,128)(2,1)}, bf16[8,32,4096]{2,1,0:T(8,128)(2,1)S(1)}, u32[]{:S(2)}, u32[]{:S(2)}) collective-permute-start(bf16[8,32,4096]{2,1,0:T(8,128)(2,1)} %get-tuple-element.120.refs_7_), channel_id=1, source_target_pairs={{0,1},{1,0},{2,6},{3,7},{4,5},{5,4},{6,2},{7,3},{8,9},{9,8},{10,14... | collective-permute-start | bytes 6291464 | tf_op jit(solution)/shard_map/ppermute | solution.py:228
  276.3 49.4 %collective-permute-start.29 = (bf16[8,32,5120]{2,1,0:T(8,128)(2,1)}, bf16[8,32,5120]{2,1,0:T(8,128)(2,1)S(1)}, u32[]{:S(2)}, u32[]{:S(2)}) collective-permute-start(bf16[8,32,5120]{2,1,0:T(8,128)(2,1)} %get-tuple-element.121.refs_7_), channel_id=1, source_target_pairs={{0,1},{1,0},{2,6},{3,7},{4,5},{5,4},{6,2},{7,3},{8,9},{9,8},{10,14... | collective-permute-start | bytes 7864328 | tf_op jit(solution)/shard_map/ppermute | solution.py:228
  297.5 28.3 %collective-permute-start.28 = (bf16[4,32,4096]{2,1,0:T(8,128)(2,1)}, bf16[4,32,4096]{2,1,0:T(8,128)(2,1)S(1)}, u32[]{:S(2)}, u32[]{:S(2)}) collective-permute-start(bf16[4,32,4096]{2,1,0:T(8,128)(2,1)} %get-tuple-element.126.refs_7_), channel_id=1, source_target_pairs={{0,4},{1,5},{2,10},{3,11},{4,0},{5,1},{6,14},{7,15},{8,12},{9,13},... | collective-permute-start | bytes 3145736 | tf_op jit(solution)/shard_map/ppermute | solution.py:228
  325.8 7.9 %collective-permute-start.27 = (bf16[16,32,2304]{2,1,0:T(8,128)(2,1)}, bf16[16,32,2304]{2,1,0:T(8,128)(2,1)}, u32[]{:S(2)}, u32[]{:S(2)}) collective-permute-start(bf16[16,32,2304]{2,1,0:T(8,128)(2,1)} %grads_send.6.refs_4_), channel_id=1, source_target_pairs={{0,2},{1,3},{2,0},{3,1},{4,6},{5,7},{6,4},{7,5},{8,10},{9,11},{10,... | collective-permute-start | bytes 7077896 | tf_op jit(solution)/shard_map/ppermute | solution.py:271
  333.1 29.8 %collective-permute-start.32 = (bf16[4,32,5120]{2,1,0:T(8,128)(2,1)}, bf16[4,32,5120]{2,1,0:T(8,128)(2,1)S(1)}, u32[]{:S(2)}, u32[]{:S(2)}) collective-permute-start(bf16[4,32,5120]{2,1,0:T(8,128)(2,1)} %get-tuple-element.140), channel_id=1, source_target_pairs={{0,4},{1,5},{2,10},{3,11},{4,0},{5,1},{6,14},{7,15},{8,12},{9,13},... | collective-permute-start | bytes 3932168 | tf_op jit(solution)/shard_map/ppermute | solution.py:228
  343.4 21.5 %collective-permute-start.33 = (bf16[8,32,2304]{2,1,0:T(8,128)(2,1)}, bf16[8,32,2304]{2,1,0:T(8,128)(2,1)S(1)}, u32[]{:S(2)}, u32[]{:S(2)}) collective-permute-start(bf16[8,32,2304]{2,1,0:T(8,128)(2,1)} %get-tuple-element.134.refs_7_), channel_id=1, source_target_pairs={{0,1},{1,0},{2,6},{3,7},{4,5},{5,4},{6,2},{7,3},{8,9},{9,8},{10,14... | collective-permute-start | bytes 3538952 | tf_op jit(solution)/shard_map/ppermute | solution.py:228
  344.5 18.5 %collective-permute-start.31 = (bf16[2,32,4096]{2,1,0:T(8,128)(2,1)S(1)}, bf16[2,32,4096]{2,1,0:T(8,128)(2,1)S(1)}, u32[]{:S(2)}, u32[]{:S(2)}) collective-permute-start(bf16[2,32,4096]{2,1,0:T(8,128)(2,1)S(1)} %copy-done.17), channel_id=1, source_target_pairs={{0,8},{1,9},{2,3},{3,2},{4,12},{5,13},{6,7},{7,6},{8,0},{9,1},{10,... | collective-permute-start | bytes 1572872 | tf_op jit(solution)/shard_map/ppermute | solution.py:228
  363.0 7.6 %collective-permute-start.30 = (bf16[16,32,768]{2,1,0:T(8,128)(2,1)}, bf16[16,32,768]{2,1,0:T(8,128)(2,1)}, u32[]{:S(2)}, u32[]{:S(2)}) collective-permute-start(bf16[16,32,768]{2,1,0:T(8,128)(2,1)} %grads_send.7.refs_6_), channel_id=1, source_target_pairs={{0,2},{1,3},{2,0},{3,1},{4,6},{5,7},{6,4},{7,5},{8,10},{9,11},{10,... | collective-permute-start | bytes 2359304 | tf_op jit(solution)/shard_map/ppermute | solution.py:271
  368.5 28.3 %collective-permute-start.34 = (bf16[2,32,5120]{2,1,0:T(8,128)(2,1)}, bf16[2,32,5120]{2,1,0:T(8,128)(2,1)S(1)}, u32[]{:S(2)}, u32[]{:S(2)}) collective-permute-start(bf16[2,32,5120]{2,1,0:T(8,128)(2,1)} %get-tuple-element.146), channel_id=1, source_target_pairs={{0,8},{1,9},{2,3},{3,2},{4,12},{5,13},{6,7},{7,6},{8,0},{9,1},{10,... | collective-permute-start | bytes 1966088 | tf_op jit(solution)/shard_map/ppermute | solution.py:228
  370.1 26.7 %collective-permute-start.35 = (bf16[4,32,2304]{2,1,0:T(8,128)(2,1)}, bf16[4,32,2304]{2,1,0:T(8,128)(2,1)S(1)}, u32[]{:S(2)}, u32[]{:S(2)}) collective-permute-start(bf16[4,32,2304]{2,1,0:T(8,128)(2,1)} %get-tuple-element.148), channel_id=1, source_target_pairs={{0,4},{1,5},{2,10},{3,11},{4,0},{5,1},{6,14},{7,15},{8,12},{9,13},... | collective-permute-start | bytes 1769480 | tf_op jit(solution)/shard_map/ppermute | solution.py:228
  375.3 21.5 %collective-permute-start.36 = (bf16[8,32,768]{2,1,0:T(8,128)(2,1)}, bf16[8,32,768]{2,1,0:T(8,128)(2,1)S(1)}, u32[]{:S(2)}, u32[]{:S(2)}) collective-permute-start(bf16[8,32,768]{2,1,0:T(8,128)(2,1)} %get-tuple-element.143.refs_25_), channel_id=1, source_target_pairs={{0,1},{1,0},{2,6},{3,7},{4,5},{5,4},{6,2},{7,3},{8,9},{9,8},{10,14... | collective-permute-start | bytes 1179656 | tf_op jit(solution)/shard_map/ppermute | solution.py:228
  377.5 27.0 %collective-permute-start.48 = (bf16[1,32,4096]{2,1,0:T(8,128)(2,1)}, bf16[1,32,4096]{2,1,0:T(8,128)(2,1)}, u32[]{:S(2)}, u32[]{:S(2)}) collective-permute-start(bf16[1,32,4096]{2,1,0:T(8,128)(2,1)} %get-tuple-element.142.refs_7_), channel_id=1, source_target_pairs={{0,16},{1,17},{2,18},{3,19},{4,20},{5,21},{6,22},{7,23},{8,24},{9,... | collective-permute-start | bytes 786440 | tf_op jit(solution)/shard_map/ppermute | solution.py:228
  396.7 2.8 collective-permute-start.39
  401.2 4.9 %collective-permute-start.40 = (f32[8,16,128]{2,1,0:T(8,128)}, f32[8,16,128]{2,1,0:T(8,128)S(1)}, u32[]{:S(2)}, u32[]{:S(2)}) collective-permute-start(f32[8,16,128]{2,1,0:T(8,128)} %get-tuple-element.158.refs_6_), channel_id=1, source_target_pairs={{0,1},{1,0},{2,6},{3,7},{4,5},{5,4},{6,2},{7,3},{8,9},{9,8},{10,14... | collective-permute-start | bytes 196616 | tf_op jit(solution)/shard_map/ppermute | solution.py:228
  402.0 11.4 %collective-permute-start.37 = (bf16[2,32,2304]{2,1,0:T(8,128)(2,1)}, bf16[2,32,2304]{2,1,0:T(8,128)(2,1)S(1)}, u32[]{:S(2)}, u32[]{:S(2)}) collective-permute-start(bf16[2,32,2304]{2,1,0:T(8,128)(2,1)} %get-tuple-element.152), channel_id=1, source_target_pairs={{0,8},{1,9},{2,3},{3,2},{4,12},{5,13},{6,7},{7,6},{8,0},{9,1},{10,... | collective-permute-start | bytes 884744 | tf_op jit(solution)/shard_map/ppermute | solution.py:228
  402.9 5.9 %collective-permute-start.38 = (bf16[4,32,768]{2,1,0:T(8,128)(2,1)}, bf16[4,32,768]{2,1,0:T(8,128)(2,1)S(1)}, u32[]{:S(2)}, u32[]{:S(2)}) collective-permute-start(bf16[4,32,768]{2,1,0:T(8,128)(2,1)} %get-tuple-element.154), channel_id=1, source_target_pairs={{0,4},{1,5},{2,10},{3,11},{4,0},{5,1},{6,14},{7,15},{8,12},{9,13},... | collective-permute-start | bytes 589832 | tf_op jit(solution)/shard_map/ppermute | solution.py:228
  405.5 25.8 %collective-permute-start.47 = (bf16[1,32,5120]{2,1,0:T(8,128)(2,1)}, bf16[1,32,5120]{2,1,0:T(8,128)(2,1)S(1)}, u32[]{:S(2)}, u32[]{:S(2)}) collective-permute-start(bf16[1,32,5120]{2,1,0:T(8,128)(2,1)} %get-tuple-element.156.refs_2_), channel_id=1, source_target_pairs={{0,16},{1,17},{2,18},{3,19},{4,20},{5,21},{6,22},{7,23},{8,24},{9,... | collective-permute-start | bytes 983048 | tf_op jit(solution)/shard_map/ppermute | solution.py:228
  415.3 9.1 %collective-permute-start.41 = (bf16[2,32,768]{2,1,0:T(8,128)(2,1)}, bf16[2,32,768]{2,1,0:T(8,128)(2,1)S(1)}, u32[]{:S(2)}, u32[]{:S(2)}) collective-permute-start(bf16[2,32,768]{2,1,0:T(8,128)(2,1)} %get-tuple-element.160), channel_id=1, source_target_pairs={{0,8},{1,9},{2,3},{3,2},{4,12},{5,13},{6,7},{7,6},{8,0},{9,1},{10,... | collective-permute-start | bytes 294920 | tf_op jit(solution)/shard_map/ppermute | solution.py:228
  415.3 4.2 collective-permute-start.42
  425.9 4.0 collective-permute-start.43
  426.8 10.7 %collective-permute-start.45 = (bf16[1,32,2304]{2,1,0:T(8,128)(2,1)S(1)}, bf16[1,32,2304]{2,1,0:T(8,128)(2,1)S(1)}, u32[]{:S(2)}, u32[]{:S(2)}) collective-permute-start(bf16[1,32,2304]{2,1,0:T(8,128)(2,1)S(1)} %copy-done.21), channel_id=1, source_target_pairs={{0,16},{1,17},{2,18},{3,19},{4,20},{5,21},{6,22},{7,23},{8,24},{9,... | collective-permute-start | bytes 442376 | tf_op jit(solution)/shard_map/ppermute | solution.py:228
  431.2 5.1 %collective-permute-start.44 = (f32[1,16,128]{2,1,0:T(8,128)}, f32[1,16,128]{2,1,0:T(8,128)S(1)}, u32[]{:S(2)}, u32[]{:S(2)}) collective-permute-start(f32[1,16,128]{2,1,0:T(8,128)} %get-tuple-element.168), channel_id=1, source_target_pairs={{0,16},{1,17},{2,18},{3,19},{4,20},{5,21},{6,22},{7,23},{8,24},{9,... | collective-permute-start | bytes 24584 | tf_op jit(solution)/shard_map/ppermute | solution.py:228
  432.8 5.0 %collective-permute-start.46 = (bf16[1,32,768]{2,1,0:T(8,128)(2,1)S(1)}, bf16[1,32,768]{2,1,0:T(8,128)(2,1)S(1)}, u32[]{:S(2)}, u32[]{:S(2)}) collective-permute-start(bf16[1,32,768]{2,1,0:T(8,128)(2,1)S(1)} %copy-done.24), channel_id=1, source_target_pairs={{0,16},{1,17},{2,18},{3,19},{4,20},{5,21},{6,22},{7,23},{8,24},{9,... | collective-permute-start | bytes 147464 | tf_op jit(solution)/shard_map/ppermute | solution.py:228
  (38 other events, 354.6 us)

commit v2 on v1

--- a/solution.py
+++ b/solution.py
@@ -91,6 +91,14 @@
 
     def core_pairs(self):
         return [(i, i ^ (self.core * self.low)) for i in range(self.count)]
+
+    def corner_pairs(self, part):
+        out = []
+        for i in range(self.count):
+            group = i // self.low
+            mask = self.core ^ self.order(int(not group & self.core), part, False)[0]
+            out.append((i, i ^ (mask * self.low)))
+        return out
 
     def low_groups(self):
         return [[g * self.low + i for i in range(self.low)] for g in range(self.ways)]
@@ -858,7 +866,7 @@
     cut, n_parts, n_vec, n_hid,
 ):
     grads_in, sources = refs[: 3 * n_parts], refs[3 * n_parts : 3 * n_parts + 8]
-    out_ref, keep_ref, send_ref, w, acc, rows, packed, sem = refs[3 * n_parts + 8 :]
+    out_ref, *quarters, w, acc, rows, packed, sem = refs[3 * n_parts + 8 :]
     width = x_ref.shape[1]
 
     @pl.when(pl.program_id(0) == 0)
@@ -893,9 +901,8 @@
             packed[g, :n_vec, :group] = rows[:n_vec, g * group : (g + 1) * group]
             packed[g, n_vec : n_vec + n_hid, :] = hid_sums_ref[:n_hid, g * lanes : (g + 1) * lanes]
             packed[g, n_vec + n_hid : n_vec + n_hid + 1, :] = heads_ref[0:1, :]
-        for k in range(ways // 2):
-            keep_ref[k] = packed[order_ref[k]]
-            send_ref[k] = packed[order_ref[ways // 2 + k]]
+        for k in range(ways):
+            quarters[4 * k // ways][k % (ways // 4)] = packed[order_ref[k]]
 
 
 def finish(plan, order, tokens, dx2, vec, sums, parts, gathered, cut, n_vec, n_hid, after=(), blk=256):
@@ -905,7 +912,7 @@
     (table, *blocks), (table_spec, *specs) = block_operands(plan, gathered)
     grads_in = [g for part in parts for g in part]
     lanes = sums[1].shape[1] // plan.ways
-    packed = jax.ShapeDtypeStruct((plan.half, 16, lanes), f32)
+    packed = jax.ShapeDtypeStruct((plan.ways // 4, 16, lanes), f32)
     packed_spec = pl.BlockSpec(packed.shape, lambda i: (0, 0, 0))
     return launch(
         functools.partial(finish_kernel, cut=cut, n_parts=len(parts), n_vec=n_vec, n_hid=n_hid),
@@ -915,8 +922,8 @@
         in_specs=[table_spec, table_spec, row, row, *(resident(a.shape) for a in (vec, *sums))]
         + [by_rows(blk, g.shape[1]) for g in grads_in]
         + specs,
-        out_specs=[row, packed_spec, packed_spec],
-        out_shape=[jax.ShapeDtypeStruct((seq, width), f32), packed, packed],
+        out_specs=[row] + [packed_spec] * 4,
+        out_shape=[jax.ShapeDtypeStruct((seq, width), f32)] + [packed] * 4,
         scratch_shapes=[
             pltpu.VMEM((width, 3 * width), bf16),
             pltpu.VMEM((16, width), f32),
@@ -944,7 +951,7 @@
     seq, width = tokens.shape
     hidden = first_weight.shape[1]
     heads = head_scale.shape[0]
-    blk = min(256, seq)
+    blk = min(512, seq)
     ways, half = plan.ways, plan.half
     n_vec, n_hid = model_vectors.shape[0], hidden_vectors.shape[0]
 
@@ -1048,7 +1055,7 @@
     done, sum_b = keep_grads(jobs, 3 * rest, got, done)
     head_sums = jnp.sum(sums[n_vec].reshape(heads, -1), axis=1)
     head_row = jnp.broadcast_to(jnp.pad(head_sums, (0, lanes - heads)), (8, lanes))
-    grad_tokens, vec_keep, vec_send = finish(
+    grad_tokens, *vec_parts = finish(
         plan,
         table,
         tokens,
@@ -1062,11 +1069,16 @@
         n_hid,
         done,
     )
-    vec_sum = Scatter(plan, 0, vec_keep, to_other_core(plan, vec_send))
-    done = step_all([fc1_sum, sum_a, sum_b], [vec_keep], True)
-    done = step_all([vec_sum], done)
-    while vec_sum.at < plan.steps:
-        done = step_all([one for one in (sum_a, sum_b, vec_sum) if one.at < plan.steps], done)
+    done = step_all([fc1_sum, sum_a, sum_b], [grad_tokens])
+    ways_out = (plan.pairs(0, 0, False), plan.core_pairs(), plan.corner_pairs(0))
+    vec_all = vec_parts[0]
+    for one, pairs_of in zip(relay(vec_parts[1:], done), ways_out):
+        vec_all += lax.ppermute(one, AXES, pairs_of)
+    vec_sum = Scatter(plan, 0, None, None)
+    vec_sum.at = 1
+    vec_sum.send(vec_all[half // 4 :], vec_all[: half // 4])
+    done = step_all([sum_a, sum_b, vec_sum], done)
+    step_all([sum_b, vec_sum], done)
     sent_vec = vec_sum.total()
     sent_a, sent_b = sum_a.total(), sum_b.total()
     sum_fc2, sum_fc1 = fc2_sum.total(), fc1_sum.total()

time: 447 us -> 442 us (0.989)
  Pallas kernels: 291 us -> 277 us
  starting transfers between devices: 45.2 us -> 52.1 us
    pallas_call x30 -> x29, Pallas kernels: 291 us -> 277 us  [launch(): pl.pallas_call(body, grid_spec=pltpu.PrefetchScalarGridSpec(num_scalar_pr...]
    ppermute x16, waiting for transfers between devices: 44.9 us -> 50 us  [step(): lax.ppermute(h, AXES, self.plan.pairs(part, self.at, True))]
    ppermute x20 -> x19, waiting for transfers between devices: 18.8 us -> 15.5 us  [send(): lax.ppermute(going, AXES, self.plan.pairs(self.part, self.at, False))]
    ppermute x20 -> x19, starting transfers between devices: 21.9 us -> 23.3 us  [send(): lax.ppermute(going, AXES, self.plan.pairs(self.part, self.at, False))]
    unnamed x86 -> x88, local copies, waits for them, and re-layouts: 12.8 us -> 12.8 us
  transfers between devices with their start and end apart: 49 -> 50, of which waited for: 20 -> 19; matrix products, arithmetic and copies ran while one was open for 4% -> 4% of each run, Pallas kernels for 45% -> 43%
where the time goes in v2:
time: 442 us; the launch traced here: 434 us
  Pallas kernels  277 us (63%)
  waiting for transfers between devices  73.7 us (17%)
  starting transfers between devices  52.1 us (12%)
  local copies, waits for them, and re-layouts  24 us (5%)
  other arithmetic  4.94 us (1%)
    pallas_call x29, Pallas kernels, launch(): pl.pallas_call(body, grid_spec=pltpu.PrefetchScalarGridSpec(num_scalar_pr...  277 us
    ppermute x16, waiting for transfers between devices, step(): lax.ppermute(h, AXES, self.plan.pairs(part, self.at, True))  50 us
    ppermute x19, starting transfers between devices, send(): lax.ppermute(going, AXES, self.plan.pairs(self.part, self.at, False))  23.3 us
    ppermute x16, starting transfers between devices, step(): lax.ppermute(h, AXES, self.plan.pairs(part, self.at, True))  20.8 us
    ppermute x19, waiting for transfers between devices, send(): lax.ppermute(going, AXES, self.plan.pairs(self.part, self.at, False))  15.5 us
    unnamed x88, local copies, waits for them, and re-layouts  12.8 us
  transfers between devices with their start and end apart: 50, of which 19 were waited for; matrix products, arithmetic and copies ran while one was open for 4% of the time, Pallas kernels for 43%

profile of v2, /device:TPU:0, one launch (start us, length us, event | category | flops | bytes accessed | tf_op | source)
XLA Modules:
  0.0 434.2 jit_solution(13771370031457192037)
XLA Ops:
  2.3 4.1 collective-permute-start
  8.3 1.7 maximum_bitcast_fusion.refs_0_
  10.0 5.9 %collective-permute-done.1.refs_3_ = bf16[1,32,1024]{2,1,0:T(8,128)(2,1)S(1)} collective-permute-done((bf16[1,32,1024]{2,1,0:T(8,128)(2,1)S(1)}, bf16[1,32,1024]{2,1,0:T(8,128)(2,1)S(1)}, u32[]{:S(2)}, u32[]{:S(2)}) %collective-permute-start.1) | collective-permute-done | bytes 65568 | tf_op jit(solution)/shard_map/ppermute | solution.py:141
  15.9 1.7 join.4
  20.5 3.4 collective-permute-start.12
  24.4 1.9 join.5
  26.3 2.1 collective-permute-start.4
  29.4 3.0 collective-permute-start.14
  33.7 6.6 %collective-permute-done.5.refs_3_ = bf16[4,32,1024]{2,1,0:T(8,128)(2,1)S(1)} collective-permute-done((bf16[4,32,1024]{2,1,0:T(8,128)(2,1)}, bf16[4,32,1024]{2,1,0:T(8,128)(2,1)S(1)}, u32[]{:S(2)}, u32[]{:S(2)}) %collective-permute-start.5) | collective-permute-done | bytes 262176 | tf_op jit(solution)/shard_map/ppermute | solution.py:141
  40.3 2.4 join.6
  43.0 3.6 collective-permute-done.12
  47.5 2.4 collective-permute-done.14
  50.7 19.4 %collective-permute-done.15.refs_1_ = bf16[2,32,3072]{2,1,0:T(8,128)(2,1)S(1)} collective-permute-done((bf16[2,32,3072]{2,1,0:T(8,128)(2,1)S(1)}, bf16[2,32,3072]{2,1,0:T(8,128)(2,1)S(1)}, u32[]{:S(2)}, u32[]{:S(2)}) %collective-permute-start.15) | collective-permute-done | bytes 393248 | tf_op jit(solution)/shard_map/ppermute | solution.py:141
  78.3 15.1 %project.1 = (bf16[1024,3072]{1,0:T(8,128)(2,1)}, bf16[1024,1024]{1,0:T(8,128)(2,1)}, f32[16,1024]{1,0:T(8,128)}, f32[16,4096]{1,0:T(8,128)}) custom-call(s32[2,32]{1,0:T(2,128)} %pad_add_fusion.refs_0_, bf16[1024,1024]{1,0:T(8,128)(2,1)} %refs_2_.1, bf16[8,32,2176]{2,1,0:T(8,128)(2,1)} %get-tuple-element.96.refs_2_.refs_17_, ...), custom_call_target="tpu_custom_call" | custom-call | flops 6442450944 | bytes 18874368 | tf_op jit(solution)/shard_map/project/pallas_call | solution.py:28
  93.4 1.9 collective-permute-done.17.refs_3_
  95.3 4.0 join.7
  102.1 24.8 %attention.1 = (f32[1024,1024]{1,0:T(8,128)}, f32[8,2,1024]{2,1,0:T(2,128)}) custom-call(s32[1]{0:T(128)S(6)} %copy.71.refs_0_, bf16[1024,3072]{1,0:T(8,128)(2,1)} %get-tuple-element.98.refs_1_.refs_2_.refs_3_, bf16[1024,3072]{1,0:T(8,128)(2,1)} %get-tuple-element.98.refs_1_.refs_2_.refs_3_, bf16[1024,3072]{1,0:T(8,128)(2,1)} %get-tuple-element.98.refs_1_.refs_2_.refs_3_, ...), custom_call_target="tpu_custom_call" | custom-call | flops 12884901888 | bytes 10485760 | tf_op jit(solution)/shard_map/attention/pallas_call | solution.py:28
  126.9 9.7 %collective-permute-done.19.refs_1_ = bf16[8,32,3072]{2,1,0:T(8,128)(2,1)S(1)} collective-permute-done((bf16[8,32,3072]{2,1,0:T(8,128)(2,1)}, bf16[8,32,3072]{2,1,0:T(8,128)(2,1)S(1)}, u32[]{:S(2)}, u32[]{:S(2)}) %collective-permute-start.19) | collective-permute-done | bytes 1572896 | tf_op jit(solution)/shard_map/ppermute | solution.py:141
  141.2 7.5 %collective-permute-done.22.refs_13_ = bf16[8,32,3072]{2,1,0:T(8,128)(2,1)S(1)} collective-permute-done((bf16[8,32,3072]{2,1,0:T(8,128)(2,1)}, bf16[8,32,3072]{2,1,0:T(8,128)(2,1)S(1)}, u32[]{:S(2)}, u32[]{:S(2)}) %collective-permute-start.22) | collective-permute-done | bytes 1572896 | tf_op jit(solution)/shard_map/ppermute | solution.py:146
  149.9 75.9 %middle.1 = (bf16[1024,1024]{1,0:T(8,128)(2,1)}, bf16[1024,1024]{1,0:T(8,128)(2,1)}, bf16[1024,1024]{1,0:T(8,128)(2,1)}, bf16[4096,1024]{1,0:T(8,128)(2,1)}, bf1...) custom-call(s32[2,32]{1,0:T(2,128)} %pad_add_fusion.refs_0_, ...), custom_call_target="tpu_custom_call" | custom-call | flops 38654705664 | bytes 60817408 | tf_op jit(solution)/shard_map/middle/pallas_call | solution.py:28
  225.8 10.2 %grads_send.4.refs_6_ = bf16[16,32,4096]{2,1,0:T(8,128)(2,1)} custom-call(s32[1,16]{1,0:T(1,128)} %get-tuple-element.185.refs_0_, s32[2,4]{1,0:T(2,128)} %constant.65.clone.refs_1_, bf16[32,4,32,1024]{3,2,1,0:T(8,128)(2,1)} %bitcast.38, bf16[1024,1024]{1,0:T(8,128)(2,1)} %refs_3_.5), custom_call_target="tpu_custom_call" | custom-call | flops 1 | bytes 1 | tf_op jit(solution)/shard_map/grads_send/pallas_call | solution.py:28
  236.4 12.8 %grads_send.5.refs_5_ = bf16[16,32,5120]{2,1,0:T(8,128)(2,1)} custom-call(s32[1,16]{1,0:T(1,128)} %get-tuple-element.185.refs_0_, s32[4,5]{1,0:T(4,128)} %constant.66.clone.refs_1_, bf16[32,1,32,1024]{3,2,1,0:T(8,128)(2,1)} %bitcast.42, bf16[32,1,32,1024]{3,2,1,0:T(8,128)(2,1)} %bitcast.40, bf16[1024,4096]{1,0:T(8,128)(2,1)} %get-tuple-element.118.refs_4_, ...), custom_call_target="tpu_custom_call" | custom-call | flops 999999995904 | bytes 1 | tf_op jit(solution)/shard_map/grads_send/pallas_call | solution.py:28
  249.3 11.4 %grads_keep.4 = (bf16[8,32,4096]{2,1,0:T(8,128)(2,1)}, bf16[8,32,4096]{2,1,0:T(8,128)(2,1)}) custom-call(s32[1,16]{1,0:T(1,128)} %get-tuple-element.186.refs_0_, s32[2,4]{1,0:T(2,128)} %constant.65.clone.refs_1_, bf16[32,4,32,1024]{3,2,1,0:T(8,128)(2,1)} %bitcast.39, bf16[1024,1024]{1,0:T(8,128)(2,1)} %refs_3_.5, ...), custom_call_target="tpu_custom_call" | custom-call | flops 999999995904 | bytes 1 | tf_op jit(solution)/shard_map/grads_keep/pallas_call | solution.py:28
  261.9 14.3 %grads_keep.5 = (bf16[8,32,5120]{2,1,0:T(8,128)(2,1)}, bf16[8,32,5120]{2,1,0:T(8,128)(2,1)}) custom-call(s32[1,16]{1,0:T(1,128)} %get-tuple-element.186.refs_0_, s32[4,5]{1,0:T(4,128)} %constant.66.clone.refs_1_, bf16[32,1,32,1024]{3,2,1,0:T(8,128)(2,1)} %bitcast.43, bf16[32,1,32,1024]{3,2,1,0:T(8,128)(2,1)} %bitcast.41, ...), custom_call_target="tpu_custom_call" | custom-call | flops 1 | bytes 1 | tf_op jit(solution)/shard_map/grads_keep/pallas_call | solution.py:28
  277.1 15.2 %attention_back.3 = (bf16[1024,384]{1,0:T(8,128)(2,1)}, bf16[1024,384]{1,0:T(8,128)(2,1)}, bf16[1024,384]{1,0:T(8,128)(2,1)}) custom-call(s32[1]{0:T(128)S(6)} %copy.71.refs_0_, bf16[1024,3072]{1,0:T(8,128)(2,1)} %get-tuple-element.98.refs_1_.refs_2_.refs_3_, bf16[1024,3072]{1,0:T(8,128)(2,1)} %get-tuple-element.98.refs_1_.refs_2_.refs_3_, ...), custom_call_target="tpu_custom_call" | custom-call | flops 1 | bytes 1 | tf_op jit(solution)/shard_map/attention_back/pallas_call | solution.py:28
  292.3 3.1 halve.6
  297.0 15.0 %attention_back.4 = (bf16[1024,384]{1,0:T(8,128)(2,1)}, bf16[1024,384]{1,0:T(8,128)(2,1)}, bf16[1024,384]{1,0:T(8,128)(2,1)}) custom-call(s32[1]{0:T(128)S(6)} %copy.71.refs_0_, bf16[1024,3072]{1,0:T(8,128)(2,1)} %get-tuple-element.98.refs_1_.refs_2_.refs_3_, bf16[1024,3072]{1,0:T(8,128)(2,1)} %get-tuple-element.98.refs_1_.refs_2_.refs_3_, ...), custom_call_target="tpu_custom_call" | custom-call | flops 1 | bytes 1 | tf_op jit(solution)/shard_map/attention_back/pallas_call | solution.py:28
  312.7 8.7 %grads_send.6.refs_4_ = bf16[16,32,2304]{2,1,0:T(8,128)(2,1)} custom-call(s32[1,16]{1,0:T(1,128)} %get-tuple-element.185.refs_0_, s32[7,2]{1,0:T(8,128)} %call_exported.0.refs_1_, bf16[32,1,32,1024]{3,2,1,0:T(8,128)(2,1)} %bitcast.34, bf16[1024,384]{1,0:T(8,128)(2,1)} %get-tuple-element.123.refs_2_.refs_3_.refs_8_, ...), custom_call_target="tpu_custom_call" | custom-call | flops 1 | bytes 1 | tf_op jit(solution)/shard_map/grads_send/pallas_call | solution.py:28
  323.3 1.7 copy-done.1
  325.1 4.1 halve.7
  330.7 9.9 %grads_keep.6 = (bf16[8,32,2304]{2,1,0:T(8,128)(2,1)}, bf16[8,32,2304]{2,1,0:T(8,128)(2,1)}) custom-call(s32[1,16]{1,0:T(1,128)} %get-tuple-element.186.refs_0_, s32[7,2]{1,0:T(8,128)} %call_exported.0.refs_1_, bf16[32,1,32,1024]{3,2,1,0:T(8,128)(2,1)} %bitcast.35, bf16[1024,384]{1,0:T(8,128)(2,1)} %get-tuple-element.123.refs_2_.refs_3_.refs_8_, ...), custom_call_target="tpu_custom_call" | custom-call | flops 1 | bytes 1 | tf_op jit(solution)/shard_map/grads_keep/pallas_call | solution.py:28
  341.8 10.7 %attention_back.5 = (bf16[1024,256]{1,0:T(8,128)(2,1)}, bf16[1024,256]{1,0:T(8,128)(2,1)}, bf16[1024,256]{1,0:T(8,128)(2,1)}) custom-call(s32[1]{0:T(128)S(6)} %copy.71.refs_0_, bf16[1024,3072]{1,0:T(8,128)(2,1)} %get-tuple-element.98.refs_1_.refs_2_.refs_3_, bf16[1024,3072]{1,0:T(8,128)(2,1)} %get-tuple-element.98.refs_1_.refs_2_.refs_3_, ...), custom_call_target="tpu_custom_call" | custom-call | flops 1 | bytes 1 | tf_op jit(solution)/shard_map/attention_back/pallas_call | solution.py:28
  353.1 4.5 %grads_send.7.refs_6_ = bf16[16,32,768]{2,1,0:T(8,128)(2,1)} custom-call(s32[1,16]{1,0:T(1,128)} %get-tuple-element.185.refs_0_, s32[4,1]{1,0:T(4,128)} %call_exported.1.refs_1_, bf16[32,1,32,1024]{3,2,1,0:T(8,128)(2,1)} %bitcast.36, bf16[1024,256]{1,0:T(8,128)(2,1)} %get-tuple-element.136.refs_3_.refs_6_.refs_14_, ...), custom_call_target="tpu_custom_call" | custom-call | flops 1 | bytes 1 | tf_op jit(solution)/shard_map/grads_send/pallas_call | solution.py:28
  357.6 3.1 collective-permute-start.30
  360.7 1.9 collective-permute-done.33.refs_5_
  362.6 3.7 halve.8
  367.5 4.8 %grads_keep.7 = (bf16[8,32,768]{2,1,0:T(8,128)(2,1)}, bf16[8,32,768]{2,1,0:T(8,128)(2,1)}) custom-call(s32[1,16]{1,0:T(1,128)} %get-tuple-element.186.refs_0_, s32[4,1]{1,0:T(4,128)} %call_exported.1.refs_1_, bf16[32,1,32,1024]{3,2,1,0:T(8,128)(2,1)} %bitcast.37, bf16[1024,256]{1,0:T(8,128)(2,1)} %get-tuple-element.136.refs_3_.refs_6_.refs_14_, ...), custom_call_target="tpu_custom_call" | custom-call | flops 1 | bytes 1 | tf_op jit(solution)/shard_map/grads_keep/pallas_call | solution.py:28
  373.9 1.9 collective-permute-start.49
  377.3 16.8 %finish.1 = (f32[1024,1024]{1,0:T(8,128)}, f32[8,16,128]{2,1,0:T(8,128)}, f32[8,16,128]{2,1,0:T(8,128)}, f32[8,16,128]{2,1,0:T(8,128)}, f32[8,16,128]{2,1,0:T(8,128)}) custom-call(s32[2,32]{1,0:T(2,128)} %pad_add_fusion.refs_0_, s32[32]{0:T(128)} %copy-done.27, bf16[1024,1024]{1,0:T(8,128)(2,1)} %refs_2_.1, f32[1024,1024]{1,0:T(8,128)} %get-tuple-element.112.refs_3_, ...), custom_call_target="tpu_custom_call" | custom-call | flops 1 | bytes 1 | tf_op jit(solution)/shard_map/finish/pallas_call | solution.py:28
  394.1 2.7 halve.9
  399.6 2.0 collective-permute-start.37
  404.4 3.5 collective-permute-done.42.refs_5_
  408.0 5.3 %collective-permute-done.37.refs_1_ = bf16[2,32,2304]{2,1,0:T(8,128)(2,1)S(1)} collective-permute-done((bf16[2,32,2304]{2,1,0:T(8,128)(2,1)}, bf16[2,32,2304]{2,1,0:T(8,128)(2,1)S(1)}, u32[]{:S(2)}, u32[]{:S(2)}) %collective-permute-start.37) | collective-permute-done | bytes 294944 | tf_op jit(solution)/shard_map/ppermute | solution.py:236
  413.3 1.9 halve.10
  415.2 2.4 collective-permute-start.43
  418.5 2.9 collective-permute-start.46
  424.0 1.9 collective-permute-start.45
  430.0 3.0 collective-permute-done.47
  (207 shorter events, 55.6 us)
Async XLA Ops:
  2.3 13.6 %collective-permute-start = (bf16[1,32,2176]{2,1,0:T(8,128)(2,1)S(1)}, bf16[1,32,2176]{2,1,0:T(8,128)(2,1)S(1)}, u32[]{:S(2)}, u32[]{:S(2)}) collective-permute-start(bf16[1,32,2176]{2,1,0:T(8,128)(2,1)S(1)} %fusion.6.refs_0_), channel_id=1, source_target_pairs={{0,16},{1,17},{2,18},{3,19},{4,20},{5,21},{6,22},{7,23},{8,24},{9,... | collective-permute-start | bytes 417800 | tf_op jit(solution)/shard_map/ppermute | solution.py:141
  7.3 8.6 %collective-permute-start.1 = (bf16[1,32,1024]{2,1,0:T(8,128)(2,1)S(1)}, bf16[1,32,1024]{2,1,0:T(8,128)(2,1)S(1)}, u32[]{:S(2)}, u32[]{:S(2)}) collective-permute-start(bf16[1,32,1024]{2,1,0:T(8,128)(2,1)S(1)} %slice_bitcast_fusion.refs_2_), channel_id=1, source_target_pairs={{0,16},{1,17},{2,18},{3,19},{4,20},{5,21},{6,22},{7,23},{8,24},{9,... | collective-permute-start | bytes 196616 | tf_op jit(solution)/shard_map/ppermute | solution.py:141
  17.6 6.8 %collective-permute-start.2 = (bf16[2,32,2176]{2,1,0:T(8,128)(2,1)}, bf16[2,32,2176]{2,1,0:T(8,128)(2,1)S(1)}, u32[]{:S(2)}, u32[]{:S(2)}) collective-permute-start(bf16[2,32,2176]{2,1,0:T(8,128)(2,1)} %get-tuple-element.92.refs_0_.refs_2_), channel_id=1, source_target_pairs={{0,1},{1,0},{2,6},{3,7},{4,5},{5,4},{6,2},{7,3},{8,9},{9,8},{10,14... | collective-permute-start | bytes 835592 | tf_op jit(solution)/shard_map/ppermute | solution.py:141
  19.2 5.2 %collective-permute-start.3 = (bf16[2,32,1024]{2,1,0:T(8,128)(2,1)}, bf16[2,32,1024]{2,1,0:T(8,128)(2,1)S(1)}, u32[]{:S(2)}, u32[]{:S(2)}) collective-permute-start(bf16[2,32,1024]{2,1,0:T(8,128)(2,1)} %get-tuple-element.93.refs_2_), channel_id=1, source_target_pairs={{0,8},{1,9},{2,10},{3,11},{4,12},{5,13},{6,14},{7,15},{8,0},{9,1},... | collective-permute-start | bytes 393224 | tf_op jit(solution)/shard_map/ppermute | solution.py:141
  20.5 26.1 %collective-permute-start.12 = (bf16[1,32,6144]{2,1,0:T(8,128)(2,1)}, bf16[1,32,6144]{2,1,0:T(8,128)(2,1)S(1)}, u32[]{:S(2)}, u32[]{:S(2)}) collective-permute-start(bf16[1,32,6144]{2,1,0:T(8,128)(2,1)} %get-tuple-element.99), channel_id=1, source_target_pairs={{0,16},{1,17},{2,18},{3,19},{4,20},{5,21},{6,22},{7,23},{8,24},{9,... | collective-permute-start | bytes 1179656 | tf_op jit(solution)/shard_map/ppermute | solution.py:141
  26.3 14.0 %collective-permute-start.4 = (bf16[4,32,2176]{2,1,0:T(8,128)(2,1)}, bf16[4,32,2176]{2,1,0:T(8,128)(2,1)S(1)}, u32[]{:S(2)}, u32[]{:S(2)}) collective-permute-start(bf16[4,32,2176]{2,1,0:T(8,128)(2,1)} %get-tuple-element.94.refs_0_), channel_id=1, source_target_pairs={{0,4},{1,5},{2,10},{3,11},{4,0},{5,1},{6,14},{7,15},{8,12},{9,13},... | collective-permute-start | bytes 1671176 | tf_op jit(solution)/shard_map/ppermute | solution.py:141
  29.4 20.5 %collective-permute-start.14 = (bf16[1,32,3072]{2,1,0:T(8,128)(2,1)}, bf16[1,32,3072]{2,1,0:T(8,128)(2,1)S(1)}, u32[]{:S(2)}, u32[]{:S(2)}) collective-permute-start(bf16[1,32,3072]{2,1,0:T(8,128)(2,1)} %get-tuple-element.100), channel_id=1, source_target_pairs={{0,16},{1,17},{2,18},{3,19},{4,20},{5,21},{6,22},{7,23},{8,24},{9,... | collective-permute-start | bytes 589832 | tf_op jit(solution)/shard_map/ppermute | solution.py:141
  32.3 7.9 %collective-permute-start.5 = (bf16[4,32,1024]{2,1,0:T(8,128)(2,1)}, bf16[4,32,1024]{2,1,0:T(8,128)(2,1)S(1)}, u32[]{:S(2)}, u32[]{:S(2)}) collective-permute-start(bf16[4,32,1024]{2,1,0:T(8,128)(2,1)} %get-tuple-element.95.refs_2_), channel_id=1, source_target_pairs={{0,1},{1,0},{2,3},{3,2},{4,5},{5,4},{6,7},{7,6},{8,9},{9,8},{10,11... | collective-permute-start | bytes 786440 | tf_op jit(solution)/shard_map/ppermute | solution.py:141
  42.6 27.5 %collective-permute-start.6 = (bf16[8,32,2176]{2,1,0:T(8,128)(2,1)}, bf16[8,32,2176]{2,1,0:T(8,128)(2,1)S(1)}, u32[]{:S(2)}, u32[]{:S(2)}) collective-permute-start(bf16[8,32,2176]{2,1,0:T(8,128)(2,1)} %get-tuple-element.96.refs_2_.refs_17_), channel_id=1, source_target_pairs={{0,8},{1,9},{2,3},{3,2},{4,12},{5,13},{6,7},{7,6},{8,0},{9,1},{10,... | collective-permute-start | bytes 3342344 | tf_op jit(solution)/shard_map/ppermute | solution.py:141
  46.7 23.9 %collective-permute-start.13 = (bf16[2,32,6144]{2,1,0:T(8,128)(2,1)S(1)}, bf16[2,32,6144]{2,1,0:T(8,128)(2,1)S(1)}, u32[]{:S(2)}, u32[]{:S(2)}) collective-permute-start(bf16[2,32,6144]{2,1,0:T(8,128)(2,1)S(1)} %pad_maximum_fusion), channel_id=1, source_target_pairs={{0,1},{1,0},{2,6},{3,7},{4,5},{5,4},{6,2},{7,3},{8,9},{9,8},{10,14... | collective-permute-start | bytes 2359304 | tf_op jit(solution)/shard_map/ppermute | solution.py:141
  49.9 20.2 %collective-permute-start.15 = (bf16[2,32,3072]{2,1,0:T(8,128)(2,1)S(1)}, bf16[2,32,3072]{2,1,0:T(8,128)(2,1)S(1)}, u32[]{:S(2)}, u32[]{:S(2)}) collective-permute-start(bf16[2,32,3072]{2,1,0:T(8,128)(2,1)S(1)} %pad_maximum_fusion.2), channel_id=1, source_target_pairs={{0,8},{1,9},{2,10},{3,11},{4,12},{5,13},{6,14},{7,15},{8,0},{9,1},... | collective-permute-start | bytes 1179656 | tf_op jit(solution)/shard_map/ppermute | solution.py:141
  50.0 20.7 %collective-permute-start.9 = (bf16[8,32,1024]{2,1,0:T(8,128)(2,1)}, bf16[8,32,1024]{2,1,0:T(8,128)(2,1)S(1)}, u32[]{:S(2)}, u32[]{:S(2)}) collective-permute-start(bf16[8,32,1024]{2,1,0:T(8,128)(2,1)} %get-tuple-element.97.refs_6_.refs_21_), channel_id=1, source_target_pairs={{0,4},{1,5},{2,6},{3,7},{4,0},{5,1},{6,2},{7,3},{8,12},{9,13},{10,... | collective-permute-start | bytes 1572872 | tf_op jit(solution)/shard_map/ppermute | solution.py:141
  50.7 26.8 %collective-permute-start.7 = (bf16[8,32,2176]{2,1,0:T(8,128)(2,1)S(1)}, bf16[8,32,2176]{2,1,0:T(8,128)(2,1)}, u32[]{:S(2)}, u32[]{:S(2)}) collective-permute-start(bf16[8,32,2176]{2,1,0:T(8,128)(2,1)S(1)} %copy-done.13), channel_id=1, source_target_pairs={{0,2},{1,3},{2,0},{3,1},{4,6},{5,7},{6,4},{7,5},{8,10},{9,11},{10,... | collective-permute-start | bytes 3342344 | tf_op jit(solution)/shard_map/ppermute | solution.py:146
  70.1 5.2 %collective-permute-start.10 = (bf16[8,32,1024]{2,1,0:T(8,128)(2,1)}, bf16[8,32,1024]{2,1,0:T(8,128)(2,1)}, u32[]{:S(2)}, u32[]{:S(2)}) collective-permute-start(bf16[8,32,1024]{2,1,0:T(8,128)(2,1)} %get-tuple-element.97.refs_6_.refs_21_), channel_id=1, source_target_pairs={{0,2},{1,3},{2,0},{3,1},{4,6},{5,7},{6,4},{7,5},{8,10},{9,11},{10,... | collective-permute-start | bytes 1572872 | tf_op jit(solution)/shard_map/ppermute | solution.py:146
  70.1 7.3 %collective-permute-start.8 = (bf16[8,32,2176]{2,1,0:T(8,128)(2,1)S(1)}, bf16[8,32,2176]{2,1,0:T(8,128)(2,1)}, u32[]{:S(2)}, u32[]{:S(2)}) collective-permute-start(bf16[8,32,2176]{2,1,0:T(8,128)(2,1)S(1)} %collective-permute-done.6.refs_3_.refs_2_.refs_18_), channel_id=1, source_target_pairs={{0,2},{1,3},{2,0},{3,1},{4,6},{5,7},{6,4},{7,5},{8,10},{9,11},{10,... | collective-permute-start | bytes 3342344 | tf_op jit(solution)/shard_map/ppermute | solution.py:149
  73.6 21.7 %collective-permute-start.16 = (bf16[4,32,6144]{2,1,0:T(8,128)(2,1)S(1)}, bf16[4,32,6144]{2,1,0:T(8,128)(2,1)S(1)}, u32[]{:S(2)}, u32[]{:S(2)}) collective-permute-start(bf16[4,32,6144]{2,1,0:T(8,128)(2,1)S(1)} %constant_dynamic-update-slice_fusion.refs_0_), channel_id=1, source_target_pairs={{0,4},{1,5},{2,10},{3,11},{4,0},{5,1},{6,14},{7,15},{8,12},{9,13},... | collective-permute-start | bytes 4718600 | tf_op jit(solution)/shard_map/ppermute | solution.py:141
  75.3 19.9 %collective-permute-start.17 = (bf16[4,32,3072]{2,1,0:T(8,128)(2,1)S(1)}, bf16[4,32,3072]{2,1,0:T(8,128)(2,1)S(1)}, u32[]{:S(2)}, u32[]{:S(2)}) collective-permute-start(bf16[4,32,3072]{2,1,0:T(8,128)(2,1)S(1)} %constant_dynamic-update-slice_fusion.3.refs_2_), channel_id=1, source_target_pairs={{0,1},{1,0},{2,3},{3,2},{4,5},{5,4},{6,7},{7,6},{8,9},{9,8},{10,11... | collective-permute-start | bytes 2359304 | tf_op jit(solution)/shard_map/ppermute | solution.py:141
  99.2 37.5 %collective-permute-start.18 = (bf16[8,32,6144]{2,1,0:T(8,128)(2,1)}, bf16[8,32,6144]{2,1,0:T(8,128)(2,1)S(1)}, u32[]{:S(2)}, u32[]{:S(2)}) collective-permute-start(bf16[8,32,6144]{2,1,0:T(8,128)(2,1)} %get-tuple-element.104.refs_4_.refs_7_), channel_id=1, source_target_pairs={{0,8},{1,9},{2,3},{3,2},{4,12},{5,13},{6,7},{7,6},{8,0},{9,1},{10,... | collective-permute-start | bytes 9437192 | tf_op jit(solution)/shard_map/ppermute | solution.py:141
  100.3 36.3 %collective-permute-start.19 = (bf16[8,32,3072]{2,1,0:T(8,128)(2,1)}, bf16[8,32,3072]{2,1,0:T(8,128)(2,1)S(1)}, u32[]{:S(2)}, u32[]{:S(2)}) collective-permute-start(bf16[8,32,3072]{2,1,0:T(8,128)(2,1)} %get-tuple-element.105.refs_5_.refs_11_), channel_id=1, source_target_pairs={{0,4},{1,5},{2,6},{3,7},{4,0},{5,1},{6,2},{7,3},{8,12},{9,13},{10,... | collective-permute-start | bytes 4718600 | tf_op jit(solution)/shard_map/ppermute | solution.py:141
  101.5 47.2 %collective-permute-start.20 = (bf16[8,32,6144]{2,1,0:T(8,128)(2,1)}, bf16[8,32,6144]{2,1,0:T(8,128)(2,1)}, u32[]{:S(2)}, u32[]{:S(2)}) collective-permute-start(bf16[8,32,6144]{2,1,0:T(8,128)(2,1)} %get-tuple-element.104.refs_4_.refs_7_), channel_id=1, source_target_pairs={{0,2},{1,3},{2,0},{3,1},{4,6},{5,7},{6,4},{7,5},{8,10},{9,11},{10,... | collective-permute-start | bytes 9437192 | tf_op jit(solution)/shard_map/ppermute | solution.py:146
  138.7 10.5 %collective-permute-start.21 = (bf16[8,32,6144]{2,1,0:T(8,128)(2,1)}, bf16[8,32,6144]{2,1,0:T(8,128)(2,1)}, u32[]{:S(2)}, u32[]{:S(2)}) collective-permute-start(bf16[8,32,6144]{2,1,0:T(8,128)(2,1)} %get-tuple-element.109.refs_8_), channel_id=1, source_target_pairs={{0,2},{1,3},{2,0},{3,1},{4,6},{5,7},{6,4},{7,5},{8,10},{9,11},{10,... | collective-permute-start | bytes 9437192 | tf_op jit(solution)/shard_map/ppermute | solution.py:149
  138.7 10.0 %collective-permute-start.22 = (bf16[8,32,3072]{2,1,0:T(8,128)(2,1)}, bf16[8,32,3072]{2,1,0:T(8,128)(2,1)S(1)}, u32[]{:S(2)}, u32[]{:S(2)}) collective-permute-start(bf16[8,32,3072]{2,1,0:T(8,128)(2,1)} %get-tuple-element.105.refs_5_.refs_11_), channel_id=1, source_target_pairs={{0,2},{1,3},{2,0},{3,1},{4,6},{5,7},{6,4},{7,5},{8,10},{9,11},{10,... | collective-permute-start | bytes 4718600 | tf_op jit(solution)/shard_map/ppermute | solution.py:146
  139.2 10.0 %collective-permute-start.23 = (bf16[8,32,3072]{2,1,0:T(8,128)(2,1)}, bf16[8,32,3072]{2,1,0:T(8,128)(2,1)}, u32[]{:S(2)}, u32[]{:S(2)}) collective-permute-start(bf16[8,32,3072]{2,1,0:T(8,128)(2,1)} %get-tuple-element.110.refs_12_), channel_id=1, source_target_pairs={{0,2},{1,3},{2,0},{3,1},{4,6},{5,7},{6,4},{7,5},{8,10},{9,11},{10,... | collective-permute-start | bytes 4718600 | tf_op jit(solution)/shard_map/ppermute | solution.py:149
  236.0 13.3 %collective-permute-start.25 = (bf16[16,32,4096]{2,1,0:T(8,128)(2,1)}, bf16[16,32,4096]{2,1,0:T(8,128)(2,1)}, u32[]{:S(2)}, u32[]{:S(2)}) collective-permute-start(bf16[16,32,4096]{2,1,0:T(8,128)(2,1)} %grads_send.4.refs_6_), channel_id=1, source_target_pairs={{0,2},{1,3},{2,0},{3,1},{4,6},{5,7},{6,4},{7,5},{8,10},{9,11},{10,... | collective-permute-start | bytes 12582920 | tf_op jit(solution)/shard_map/ppermute | solution.py:279
  249.2 12.7 %collective-permute-start.24 = (bf16[16,32,5120]{2,1,0:T(8,128)(2,1)}, bf16[16,32,5120]{2,1,0:T(8,128)(2,1)}, u32[]{:S(2)}, u32[]{:S(2)}) collective-permute-start(bf16[16,32,5120]{2,1,0:T(8,128)(2,1)} %grads_send.5.refs_5_), channel_id=1, source_target_pairs={{0,2},{1,3},{2,0},{3,1},{4,6},{5,7},{6,4},{7,5},{8,10},{9,11},{10,... | collective-permute-start | bytes 15728648 | tf_op jit(solution)/shard_map/ppermute | solution.py:279
  260.7 31.6 %collective-permute-start.26 = (bf16[8,32,4096]{2,1,0:T(8,128)(2,1)}, bf16[8,32,4096]{2,1,0:T(8,128)(2,1)S(1)}, u32[]{:S(2)}, u32[]{:S(2)}) collective-permute-start(bf16[8,32,4096]{2,1,0:T(8,128)(2,1)} %get-tuple-element.121.refs_7_), channel_id=1, source_target_pairs={{0,1},{1,0},{2,6},{3,7},{4,5},{5,4},{6,2},{7,3},{8,9},{9,8},{10,14... | collective-permute-start | bytes 6291464 | tf_op jit(solution)/shard_map/ppermute | solution.py:236
  276.2 45.6 %collective-permute-start.29 = (bf16[8,32,5120]{2,1,0:T(8,128)(2,1)}, bf16[8,32,5120]{2,1,0:T(8,128)(2,1)S(1)}, u32[]{:S(2)}, u32[]{:S(2)}) collective-permute-start(bf16[8,32,5120]{2,1,0:T(8,128)(2,1)} %get-tuple-element.122.refs_7_), channel_id=1, source_target_pairs={{0,1},{1,0},{2,6},{3,7},{4,5},{5,4},{6,2},{7,3},{8,9},{9,8},{10,14... | collective-permute-start | bytes 7864328 | tf_op jit(solution)/shard_map/ppermute | solution.py:236
  295.5 26.3 %collective-permute-start.28 = (bf16[4,32,4096]{2,1,0:T(8,128)(2,1)}, bf16[4,32,4096]{2,1,0:T(8,128)(2,1)S(1)}, u32[]{:S(2)}, u32[]{:S(2)}) collective-permute-start(bf16[4,32,4096]{2,1,0:T(8,128)(2,1)} %get-tuple-element.127.refs_7_), channel_id=1, source_target_pairs={{0,4},{1,5},{2,10},{3,11},{4,0},{5,1},{6,14},{7,15},{8,12},{9,13},... | collective-permute-start | bytes 3145736 | tf_op jit(solution)/shard_map/ppermute | solution.py:236
  321.4 9.4 %collective-permute-start.27 = (bf16[16,32,2304]{2,1,0:T(8,128)(2,1)}, bf16[16,32,2304]{2,1,0:T(8,128)(2,1)}, u32[]{:S(2)}, u32[]{:S(2)}) collective-permute-start(bf16[16,32,2304]{2,1,0:T(8,128)(2,1)} %grads_send.6.refs_4_), channel_id=1, source_target_pairs={{0,2},{1,3},{2,0},{3,1},{4,6},{5,7},{6,4},{7,5},{8,10},{9,11},{10,... | collective-permute-start | bytes 7077896 | tf_op jit(solution)/shard_map/ppermute | solution.py:279
  329.2 31.6 %collective-permute-start.32 = (bf16[4,32,5120]{2,1,0:T(8,128)(2,1)}, bf16[4,32,5120]{2,1,0:T(8,128)(2,1)S(1)}, u32[]{:S(2)}, u32[]{:S(2)}) collective-permute-start(bf16[4,32,5120]{2,1,0:T(8,128)(2,1)} %get-tuple-element.141), channel_id=1, source_target_pairs={{0,4},{1,5},{2,10},{3,11},{4,0},{5,1},{6,14},{7,15},{8,12},{9,13},... | collective-permute-start | bytes 3932168 | tf_op jit(solution)/shard_map/ppermute | solution.py:236
  340.6 22.0 %collective-permute-start.33 = (bf16[8,32,2304]{2,1,0:T(8,128)(2,1)}, bf16[8,32,2304]{2,1,0:T(8,128)(2,1)S(1)}, u32[]{:S(2)}, u32[]{:S(2)}) collective-permute-start(bf16[8,32,2304]{2,1,0:T(8,128)(2,1)} %get-tuple-element.135.refs_7_), channel_id=1, source_target_pairs={{0,1},{1,0},{2,6},{3,7},{4,5},{5,4},{6,2},{7,3},{8,9},{9,8},{10,14... | collective-permute-start | bytes 3538952 | tf_op jit(solution)/shard_map/ppermute | solution.py:236
  341.7 19.1 %collective-permute-start.31 = (bf16[2,32,4096]{2,1,0:T(8,128)(2,1)S(1)}, bf16[2,32,4096]{2,1,0:T(8,128)(2,1)S(1)}, u32[]{:S(2)}, u32[]{:S(2)}) collective-permute-start(bf16[2,32,4096]{2,1,0:T(8,128)(2,1)S(1)} %copy-done.17), channel_id=1, source_target_pairs={{0,8},{1,9},{2,3},{3,2},{4,12},{5,13},{6,7},{7,6},{8,0},{9,1},{10,... | collective-permute-start | bytes 1572872 | tf_op jit(solution)/shard_map/ppermute | solution.py:236
  357.6 9.9 %collective-permute-start.30 = (bf16[16,32,768]{2,1,0:T(8,128)(2,1)}, bf16[16,32,768]{2,1,0:T(8,128)(2,1)}, u32[]{:S(2)}, u32[]{:S(2)}) collective-permute-start(bf16[16,32,768]{2,1,0:T(8,128)(2,1)} %grads_send.7.refs_6_), channel_id=1, source_target_pairs={{0,2},{1,3},{2,0},{3,1},{4,6},{5,7},{6,4},{7,5},{8,10},{9,11},{10,... | collective-permute-start | bytes 2359304 | tf_op jit(solution)/shard_map/ppermute | solution.py:279
  366.3 27.8 %collective-permute-start.34 = (bf16[2,32,5120]{2,1,0:T(8,128)(2,1)}, bf16[2,32,5120]{2,1,0:T(8,128)(2,1)S(1)}, u32[]{:S(2)}, u32[]{:S(2)}) collective-permute-start(bf16[2,32,5120]{2,1,0:T(8,128)(2,1)} %get-tuple-element.147), channel_id=1, source_target_pairs={{0,8},{1,9},{2,3},{3,2},{4,12},{5,13},{6,7},{7,6},{8,0},{9,1},{10,... | collective-permute-start | bytes 1966088 | tf_op jit(solution)/shard_map/ppermute | solution.py:236
  366.3 27.8 %collective-permute-start.35 = (bf16[4,32,2304]{2,1,0:T(8,128)(2,1)}, bf16[4,32,2304]{2,1,0:T(8,128)(2,1)S(1)}, u32[]{:S(2)}, u32[]{:S(2)}) collective-permute-start(bf16[4,32,2304]{2,1,0:T(8,128)(2,1)} %get-tuple-element.149), channel_id=1, source_target_pairs={{0,4},{1,5},{2,10},{3,11},{4,0},{5,1},{6,14},{7,15},{8,12},{9,13},... | collective-permute-start | bytes 1769480 | tf_op jit(solution)/shard_map/ppermute | solution.py:236
  372.4 21.7 %collective-permute-start.36 = (bf16[8,32,768]{2,1,0:T(8,128)(2,1)}, bf16[8,32,768]{2,1,0:T(8,128)(2,1)S(1)}, u32[]{:S(2)}, u32[]{:S(2)}) collective-permute-start(bf16[8,32,768]{2,1,0:T(8,128)(2,1)} %get-tuple-element.144.refs_25_), channel_id=1, source_target_pairs={{0,1},{1,0},{2,6},{3,7},{4,5},{5,4},{6,2},{7,3},{8,9},{9,8},{10,14... | collective-permute-start | bytes 1179656 | tf_op jit(solution)/shard_map/ppermute | solution.py:236
  373.9 25.6 %collective-permute-start.49 = (bf16[1,32,4096]{2,1,0:T(8,128)(2,1)S(1)}, bf16[1,32,4096]{2,1,0:T(8,128)(2,1)S(1)}, u32[]{:S(2)}, u32[]{:S(2)}) collective-permute-start(bf16[1,32,4096]{2,1,0:T(8,128)(2,1)S(1)} %copy-done.19), channel_id=1, source_target_pairs={{0,16},{1,17},{2,18},{3,19},{4,20},{5,21},{6,22},{7,23},{8,24},{9,... | collective-permute-start | bytes 786440 | tf_op jit(solution)/shard_map/ppermute | solution.py:236
  396.8 4.9 %collective-permute-start.39 = (f32[8,16,128]{2,1,0:T(8,128)}, f32[8,16,128]{2,1,0:T(8,128)S(1)}, u32[]{:S(2)}, u32[]{:S(2)}) collective-permute-start(f32[8,16,128]{2,1,0:T(8,128)} %get-tuple-element.160), channel_id=1, source_target_pairs={{0,1},{1,0},{2,6},{3,7},{4,5},{5,4},{6,2},{7,3},{8,9},{9,8},{10,14... | collective-permute-start | bytes 196616 | tf_op jit(solution)/shard_map/ppermute | solution.py:1076
  397.7 5.4 %collective-permute-start.40 = (f32[8,16,128]{2,1,0:T(8,128)}, f32[8,16,128]{2,1,0:T(8,128)S(1)}, u32[]{:S(2)}, u32[]{:S(2)}) collective-permute-start(f32[8,16,128]{2,1,0:T(8,128)} %get-tuple-element.161), channel_id=1, source_target_pairs={{0,2},{1,3},{2,0},{3,1},{4,6},{5,7},{6,4},{7,5},{8,10},{9,11},{10,... | collective-permute-start | bytes 196616 | tf_op jit(solution)/shard_map/ppermute | solution.py:1076
  397.7 5.4 %collective-permute-start.41 = (f32[8,16,128]{2,1,0:T(8,128)}, f32[8,16,128]{2,1,0:T(8,128)S(1)}, u32[]{:S(2)}, u32[]{:S(2)}) collective-permute-start(f32[8,16,128]{2,1,0:T(8,128)} %get-tuple-element.162), channel_id=1, source_target_pairs={{0,6},{1,7},{2,1},{3,0},{4,2},{5,3},{6,5},{7,4},{8,14},{9,15},{10,... | collective-permute-start | bytes 196616 | tf_op jit(solution)/shard_map/ppermute | solution.py:1076
  399.5 26.5 %collective-permute-start.48 = (bf16[1,32,5120]{2,1,0:T(8,128)(2,1)}, bf16[1,32,5120]{2,1,0:T(8,128)(2,1)S(1)}, u32[]{:S(2)}, u32[]{:S(2)}) collective-permute-start(bf16[1,32,5120]{2,1,0:T(8,128)(2,1)} %get-tuple-element.159.refs_3_.refs_6_), channel_id=1, source_target_pairs={{0,16},{1,17},{2,18},{3,19},{4,20},{5,21},{6,22},{7,23},{8,24},{9,... | collective-permute-start | bytes 983048 | tf_op jit(solution)/shard_map/ppermute | solution.py:236
  399.6 13.7 %collective-permute-start.37 = (bf16[2,32,2304]{2,1,0:T(8,128)(2,1)}, bf16[2,32,2304]{2,1,0:T(8,128)(2,1)S(1)}, u32[]{:S(2)}, u32[]{:S(2)}) collective-permute-start(bf16[2,32,2304]{2,1,0:T(8,128)(2,1)} %get-tuple-element.152), channel_id=1, source_target_pairs={{0,8},{1,9},{2,3},{3,2},{4,12},{5,13},{6,7},{7,6},{8,0},{9,1},{10,... | collective-permute-start | bytes 884744 | tf_op jit(solution)/shard_map/ppermute | solution.py:236
  401.7 6.2 %collective-permute-start.38 = (bf16[4,32,768]{2,1,0:T(8,128)(2,1)}, bf16[4,32,768]{2,1,0:T(8,128)(2,1)S(1)}, u32[]{:S(2)}, u32[]{:S(2)}) collective-permute-start(bf16[4,32,768]{2,1,0:T(8,128)(2,1)} %get-tuple-element.154), channel_id=1, source_target_pairs={{0,4},{1,5},{2,10},{3,11},{4,0},{5,1},{6,14},{7,15},{8,12},{9,13},... | collective-permute-start | bytes 589832 | tf_op jit(solution)/shard_map/ppermute | solution.py:236
  415.2 7.3 %collective-permute-start.43 = (bf16[2,32,768]{2,1,0:T(8,128)(2,1)}, bf16[2,32,768]{2,1,0:T(8,128)(2,1)S(1)}, u32[]{:S(2)}, u32[]{:S(2)}) collective-permute-start(bf16[2,32,768]{2,1,0:T(8,128)(2,1)} %get-tuple-element.164), channel_id=1, source_target_pairs={{0,8},{1,9},{2,3},{3,2},{4,12},{5,13},{6,7},{7,6},{8,0},{9,1},{10,... | collective-permute-start | bytes 294920 | tf_op jit(solution)/shard_map/ppermute | solution.py:236
  417.6 4.9 %collective-permute-start.44 = (f32[2,16,128]{2,1,0:T(8,128)}, f32[2,16,128]{2,1,0:T(8,128)S(1)}, u32[]{:S(2)}, u32[]{:S(2)}) collective-permute-start(f32[2,16,128]{2,1,0:T(8,128)} %get-tuple-element.166), channel_id=1, source_target_pairs={{0,8},{1,9},{2,3},{3,2},{4,12},{5,13},{6,7},{7,6},{8,0},{9,1},{10,... | collective-permute-start | bytes 49160 | tf_op jit(solution)/shard_map/ppermute | solution.py:236
  418.5 11.5 %collective-permute-start.46 = (bf16[1,32,2304]{2,1,0:T(8,128)(2,1)}, bf16[1,32,2304]{2,1,0:T(8,128)(2,1)S(1)}, u32[]{:S(2)}, u32[]{:S(2)}) collective-permute-start(bf16[1,32,2304]{2,1,0:T(8,128)(2,1)} %get-tuple-element.167.refs_4_), channel_id=1, source_target_pairs={{0,16},{1,17},{2,18},{3,19},{4,20},{5,21},{6,22},{7,23},{8,24},{9,... | collective-permute-start | bytes 442376 | tf_op jit(solution)/shard_map/ppermute | solution.py:236
  424.0 4.8 %collective-permute-start.45 = (f32[1,16,128]{2,1,0:T(8,128)}, f32[1,16,128]{2,1,0:T(8,128)S(1)}, u32[]{:S(2)}, u32[]{:S(2)}) collective-permute-start(f32[1,16,128]{2,1,0:T(8,128)} %get-tuple-element.169), channel_id=1, source_target_pairs={{0,16},{1,17},{2,18},{3,19},{4,20},{5,21},{6,22},{7,23},{8,24},{9,... | collective-permute-start | bytes 24584 | tf_op jit(solution)/shard_map/ppermute | solution.py:236
  427.5 5.5 %collective-permute-start.47 = (bf16[1,32,768]{2,1,0:T(8,128)(2,1)S(1)}, bf16[1,32,768]{2,1,0:T(8,128)(2,1)S(1)}, u32[]{:S(2)}, u32[]{:S(2)}) collective-permute-start(bf16[1,32,768]{2,1,0:T(8,128)(2,1)S(1)} %copy-done.37), channel_id=1, source_target_pairs={{0,16},{1,17},{2,18},{3,19},{4,20},{5,21},{6,22},{7,23},{8,24},{9,... | collective-permute-start | bytes 147464 | tf_op jit(solution)/shard_map/ppermute | solution.py:236
  (40 other events, 355.3 us)

commit v3 on v2

--- a/solution.py
+++ b/solution.py
@@ -323,6 +323,18 @@
     return alone, jnp.where(spare & late, bf16(1), alone)
 
 
+def key_pieces(i, blk):
+    half = blk // 2
+    whole = [(j * blk, blk, 0) for j in range(i)]
+    return whole + [(i * blk, half, 0), (i * blk + half, half, half)]
+
+
+def added(total, more, first):
+    if not first:
+        return total + more
+    return jnp.concatenate([total[:, :first], total[:, first:] + more], 1)
+
+
 def attention_kernel(split_ref, q_ref, k_ref, v_ref, *refs, seq, hd, blk):
     o_ref, lse_ref = refs[-2:]
     split = split_ref[0]
@@ -333,22 +345,26 @@
         outs = []
         for h in (0, 1):
             _, q = masked_queries(q_ref[rows, :], h, hd, split, i * blk)
-            scores = [dot_nt(keys[h][j * blk : (j + 1) * blk], q) for j in range(i + 1)]
-            scores[i] = causal(scores[i])
+            pieces = key_pieces(i, blk)
+            scores = [dot_nt(keys[h][at : at + count], q[first:]) for at, count, first in pieces]
+            scores[i:] = [causal(s) for s in scores[i:]]
             peak = scores[0].max(0, keepdims=True)
-            for s in scores[1:]:
+            for s in scores[1:-1]:
                 peak = jnp.maximum(peak, s.max(0, keepdims=True))
+            first = pieces[-1][2]
+            late = jnp.maximum(peak[:, first:], scores[-1].max(0, keepdims=True))
+            peak = jnp.concatenate([peak[:, :first], late], 1)
             total = jnp.zeros((1, blk), f32)
             mixed = jnp.zeros((hd, blk), f32)
-            for j, s in enumerate(scores):
+            for (at, count, first), s in zip(pieces, scores):
                 low = []
-                for r in strips(blk, 64):
-                    e = jnp.exp(s[r] - peak)
-                    total += e.sum(0, keepdims=True)
+                for r in strips(count, 64):
+                    e = jnp.exp(s[r] - peak[:, first:])
+                    total = added(total, e.sum(0, keepdims=True), first)
                     low.append(e.astype(bf16))
-                mixed += dot_nn(
-                    v_t[h * hd : (h + 1) * hd, j * blk : (j + 1) * blk], jnp.concatenate(low, 0)
-                )
+                low = jnp.concatenate(low, 0)
+                values = v_t[h * hd : (h + 1) * hd, at : at + count]
+                mixed = added(mixed, dot_nn(values, low), first)
             outs.append(mixed / total)
             lse_ref[0, h : h + 1, rows] = peak + jnp.log(total)
         o_ref[rows, :] = jnp.concatenate(outs, 0).T
@@ -402,27 +418,28 @@
             row_inner = inner[h * hd : (h + 1) * hd].sum(0, keepdims=True)
             lse = lse_ref[0, h : h + 1, rows]
             dq = jnp.zeros((hd, blk), f32)
-            for j in range(i + 1):
-                keys = slice(j * blk, (j + 1) * blk)
-                s = dot_nt(keys_of[h][keys], q_marked)
-                if i == j:
+            for at, count, first in key_pieces(i, blk):
+                keys = slice(at, at + count)
+                diagonal = at >= i * blk
+                s = dot_nt(keys_of[h][keys], q_marked[first:])
+                if diagonal:
                     s = causal(s)
-                dp = dot_nt(v_ref[keys, :], da)
+                dp = dot_nt(v_ref[keys, :], da[first:])
                 p_low, ds = [], []
-                for r in strips(blk, 64):
-                    p = jnp.exp(s[r] - lse)
+                for r in strips(count, 64):
+                    p = jnp.exp(s[r] - lse[:, first:])
                     p_low.append(p.astype(bf16))
-                    ds.append((p * (dp[r] - row_inner)).astype(bf16))
+                    ds.append((p * (dp[r] - row_inner[:, first:])).astype(bf16))
                 ds = jnp.concatenate(ds, 0)
-                dv = dot_nn(jnp.concatenate(p_low, 0), da)
-                dk = dot_nn(ds, q)
-                if i == j and h == 0:
+                dv = dot_nn(jnp.concatenate(p_low, 0), da[first:])
+                dk = dot_nn(ds, q[first:])
+                if diagonal and h == 0:
                     dv_acc[keys, :] = dv
                     dk_acc[keys, :] = dk
                 else:
                     dv_acc[keys, :] += dv
                     dk_acc[keys, :] += dk
-                dq += dot_nn(k_t[h * hd : (h + 1) * hd, keys], ds)
+                dq = added(dq, dot_nn(k_t[h * hd : (h + 1) * hd, keys], ds), first)
             dqs.append(dq)
         dq_ref[rows, :] = (jnp.concatenate(dqs, 0).T * (hd**-0.5)).astype(bf16)
     dk_ref[...] = dk_acc[...].astype(bf16)

time: 442 us -> 441 us (level)
    pallas_call x29, Pallas kernels: 277 us -> 273 us  [launch(): pl.pallas_call(body, grid_spec=pltpu.PrefetchScalarGridSpec(num_scalar_pr...]
  transfers between devices with their start and end apart: 50 -> 50, of which waited for: 19 -> 19; matrix products, arithmetic and copies ran while one was open for 4% -> 4% of each run, Pallas kernels for 43% -> 42%
where the time goes in v3:
time: 441 us; the launch traced here: 433 us
  Pallas kernels  273 us (62%)
  waiting for transfers between devices  76.3 us (17%)
  starting transfers between devices  53.2 us (12%)
  local copies, waits for them, and re-layouts  24 us (5%)
  other arithmetic  4.94 us (1%)
    pallas_call x29, Pallas kernels, launch(): pl.pallas_call(body, grid_spec=pltpu.PrefetchScalarGridSpec(num_scalar_pr...  273 us
    ppermute x16, waiting for transfers between devices, step(): lax.ppermute(h, AXES, self.plan.pairs(part, self.at, True))  51.7 us
    ppermute x19, starting transfers between devices, send(): lax.ppermute(going, AXES, self.plan.pairs(self.part, self.at, False))  23.3 us
    ppermute x16, starting transfers between devices, step(): lax.ppermute(h, AXES, self.plan.pairs(part, self.at, True))  20.8 us
    ppermute x19, waiting for transfers between devices, send(): lax.ppermute(going, AXES, self.plan.pairs(self.part, self.at, False))  16.5 us
    unnamed x88, local copies, waits for them, and re-layouts  12.8 us
  transfers between devices with their start and end apart: 50, of which 19 were waited for; matrix products, arithmetic and copies ran while one was open for 4% of the time, Pallas kernels for 42%

profile of v3, /device:TPU:0, one launch (start us, length us, event | category | flops | bytes accessed | tf_op | source)
XLA Modules:
  0.0 433.3 jit_solution(7435271118233883099)
XLA Ops:
  2.3 4.1 collective-permute-start
  8.3 1.7 maximum_bitcast_fusion.refs_0_
  10.0 5.9 %collective-permute-done.1.refs_3_ = bf16[1,32,1024]{2,1,0:T(8,128)(2,1)S(1)} collective-permute-done((bf16[1,32,1024]{2,1,0:T(8,128)(2,1)S(1)}, bf16[1,32,1024]{2,1,0:T(8,128)(2,1)S(1)}, u32[]{:S(2)}, u32[]{:S(2)}) %collective-permute-start.1) | collective-permute-done | bytes 65568 | tf_op jit(solution)/shard_map/ppermute | solution.py:141
  15.9 1.7 join.4
  20.5 3.4 collective-permute-start.12
  24.4 1.9 join.5
  26.3 2.1 collective-permute-start.4
  29.4 3.0 collective-permute-start.14
  33.7 6.6 %collective-permute-done.5.refs_3_ = bf16[4,32,1024]{2,1,0:T(8,128)(2,1)S(1)} collective-permute-done((bf16[4,32,1024]{2,1,0:T(8,128)(2,1)}, bf16[4,32,1024]{2,1,0:T(8,128)(2,1)S(1)}, u32[]{:S(2)}, u32[]{:S(2)}) %collective-permute-start.5) | collective-permute-done | bytes 262176 | tf_op jit(solution)/shard_map/ppermute | solution.py:141
  40.3 2.4 join.6
  43.0 3.6 collective-permute-done.12
  47.5 2.4 collective-permute-done.14
  50.7 19.4 %collective-permute-done.15.refs_1_ = bf16[2,32,3072]{2,1,0:T(8,128)(2,1)S(1)} collective-permute-done((bf16[2,32,3072]{2,1,0:T(8,128)(2,1)S(1)}, bf16[2,32,3072]{2,1,0:T(8,128)(2,1)S(1)}, u32[]{:S(2)}, u32[]{:S(2)}) %collective-permute-start.15) | collective-permute-done | bytes 393248 | tf_op jit(solution)/shard_map/ppermute | solution.py:141
  78.3 15.1 %project.1 = (bf16[1024,3072]{1,0:T(8,128)(2,1)}, bf16[1024,1024]{1,0:T(8,128)(2,1)}, f32[16,1024]{1,0:T(8,128)}, f32[16,4096]{1,0:T(8,128)}) custom-call(s32[2,32]{1,0:T(2,128)} %pad_add_fusion.refs_0_, bf16[1024,1024]{1,0:T(8,128)(2,1)} %refs_2_.1, bf16[8,32,2176]{2,1,0:T(8,128)(2,1)} %get-tuple-element.96.refs_2_.refs_17_, ...), custom_call_target="tpu_custom_call" | custom-call | flops 6442450944 | bytes 18874368 | tf_op jit(solution)/shard_map/project/pallas_call | solution.py:28
  93.4 1.9 collective-permute-done.17.refs_3_
  95.3 4.0 join.7
  102.1 23.1 %attention.1 = (f32[1024,1024]{1,0:T(8,128)}, f32[8,2,1024]{2,1,0:T(2,128)}) custom-call(s32[1]{0:T(128)S(6)} %copy.71.refs_0_, bf16[1024,3072]{1,0:T(8,128)(2,1)} %get-tuple-element.98.refs_1_.refs_2_.refs_3_, bf16[1024,3072]{1,0:T(8,128)(2,1)} %get-tuple-element.98.refs_1_.refs_2_.refs_3_, bf16[1024,3072]{1,0:T(8,128)(2,1)} %get-tuple-element.98.refs_1_.refs_2_.refs_3_, ...), custom_call_target="tpu_custom_call" | custom-call | flops 12884901888 | bytes 10485760 | tf_op jit(solution)/shard_map/attention/pallas_call | solution.py:28
  125.2 11.4 %collective-permute-done.19.refs_1_ = bf16[8,32,3072]{2,1,0:T(8,128)(2,1)S(1)} collective-permute-done((bf16[8,32,3072]{2,1,0:T(8,128)(2,1)}, bf16[8,32,3072]{2,1,0:T(8,128)(2,1)S(1)}, u32[]{:S(2)}, u32[]{:S(2)}) %collective-permute-start.19) | collective-permute-done | bytes 1572896 | tf_op jit(solution)/shard_map/ppermute | solution.py:141
  141.2 7.5 %collective-permute-done.22.refs_13_ = bf16[8,32,3072]{2,1,0:T(8,128)(2,1)S(1)} collective-permute-done((bf16[8,32,3072]{2,1,0:T(8,128)(2,1)}, bf16[8,32,3072]{2,1,0:T(8,128)(2,1)S(1)}, u32[]{:S(2)}, u32[]{:S(2)}) %collective-permute-start.22) | collective-permute-done | bytes 1572896 | tf_op jit(solution)/shard_map/ppermute | solution.py:146
  149.9 75.9 %middle.1 = (bf16[1024,1024]{1,0:T(8,128)(2,1)}, bf16[1024,1024]{1,0:T(8,128)(2,1)}, bf16[1024,1024]{1,0:T(8,128)(2,1)}, bf16[4096,1024]{1,0:T(8,128)(2,1)}, bf1...) custom-call(s32[2,32]{1,0:T(2,128)} %pad_add_fusion.refs_0_, ...), custom_call_target="tpu_custom_call" | custom-call | flops 38654705664 | bytes 60817408 | tf_op jit(solution)/shard_map/middle/pallas_call | solution.py:28
  225.8 10.2 %grads_send.4.refs_6_ = bf16[16,32,4096]{2,1,0:T(8,128)(2,1)} custom-call(s32[1,16]{1,0:T(1,128)} %get-tuple-element.185.refs_0_, s32[2,4]{1,0:T(2,128)} %constant.65.clone.refs_1_, bf16[32,4,32,1024]{3,2,1,0:T(8,128)(2,1)} %bitcast.38, bf16[1024,1024]{1,0:T(8,128)(2,1)} %refs_3_.5), custom_call_target="tpu_custom_call" | custom-call | flops 1 | bytes 1 | tf_op jit(solution)/shard_map/grads_send/pallas_call | solution.py:28
  236.4 12.8 %grads_send.5.refs_5_ = bf16[16,32,5120]{2,1,0:T(8,128)(2,1)} custom-call(s32[1,16]{1,0:T(1,128)} %get-tuple-element.185.refs_0_, s32[4,5]{1,0:T(4,128)} %constant.66.clone.refs_1_, bf16[32,1,32,1024]{3,2,1,0:T(8,128)(2,1)} %bitcast.42, bf16[32,1,32,1024]{3,2,1,0:T(8,128)(2,1)} %bitcast.40, bf16[1024,4096]{1,0:T(8,128)(2,1)} %get-tuple-element.118.refs_4_, ...), custom_call_target="tpu_custom_call" | custom-call | flops 999999995904 | bytes 1 | tf_op jit(solution)/shard_map/grads_send/pallas_call | solution.py:28
  249.3 11.4 %grads_keep.4 = (bf16[8,32,4096]{2,1,0:T(8,128)(2,1)}, bf16[8,32,4096]{2,1,0:T(8,128)(2,1)}) custom-call(s32[1,16]{1,0:T(1,128)} %get-tuple-element.186.refs_0_, s32[2,4]{1,0:T(2,128)} %constant.65.clone.refs_1_, bf16[32,4,32,1024]{3,2,1,0:T(8,128)(2,1)} %bitcast.39, bf16[1024,1024]{1,0:T(8,128)(2,1)} %refs_3_.5, ...), custom_call_target="tpu_custom_call" | custom-call | flops 999999995904 | bytes 1 | tf_op jit(solution)/shard_map/grads_keep/pallas_call | solution.py:28
  261.9 14.3 %grads_keep.5 = (bf16[8,32,5120]{2,1,0:T(8,128)(2,1)}, bf16[8,32,5120]{2,1,0:T(8,128)(2,1)}) custom-call(s32[1,16]{1,0:T(1,128)} %get-tuple-element.186.refs_0_, s32[4,5]{1,0:T(4,128)} %constant.66.clone.refs_1_, bf16[32,1,32,1024]{3,2,1,0:T(8,128)(2,1)} %bitcast.43, bf16[32,1,32,1024]{3,2,1,0:T(8,128)(2,1)} %bitcast.41, ...), custom_call_target="tpu_custom_call" | custom-call | flops 1 | bytes 1 | tf_op jit(solution)/shard_map/grads_keep/pallas_call | solution.py:28
  277.1 14.1 %attention_back.3 = (bf16[1024,384]{1,0:T(8,128)(2,1)}, bf16[1024,384]{1,0:T(8,128)(2,1)}, bf16[1024,384]{1,0:T(8,128)(2,1)}) custom-call(s32[1]{0:T(128)S(6)} %copy.71.refs_0_, bf16[1024,3072]{1,0:T(8,128)(2,1)} %get-tuple-element.98.refs_1_.refs_2_.refs_3_, bf16[1024,3072]{1,0:T(8,128)(2,1)} %get-tuple-element.98.refs_1_.refs_2_.refs_3_, ...), custom_call_target="tpu_custom_call" | custom-call | flops 1 | bytes 1 | tf_op jit(solution)/shard_map/attention_back/pallas_call | solution.py:28
  291.2 3.1 halve.6
  295.9 13.9 %attention_back.4 = (bf16[1024,384]{1,0:T(8,128)(2,1)}, bf16[1024,384]{1,0:T(8,128)(2,1)}, bf16[1024,384]{1,0:T(8,128)(2,1)}) custom-call(s32[1]{0:T(128)S(6)} %copy.71.refs_0_, bf16[1024,3072]{1,0:T(8,128)(2,1)} %get-tuple-element.98.refs_1_.refs_2_.refs_3_, bf16[1024,3072]{1,0:T(8,128)(2,1)} %get-tuple-element.98.refs_1_.refs_2_.refs_3_, ...), custom_call_target="tpu_custom_call" | custom-call | flops 1 | bytes 1 | tf_op jit(solution)/shard_map/attention_back/pallas_call | solution.py:28
  310.4 8.7 %grads_send.6.refs_4_ = bf16[16,32,2304]{2,1,0:T(8,128)(2,1)} custom-call(s32[1,16]{1,0:T(1,128)} %get-tuple-element.185.refs_0_, s32[7,2]{1,0:T(8,128)} %call_exported.0.refs_1_, bf16[32,1,32,1024]{3,2,1,0:T(8,128)(2,1)} %bitcast.34, bf16[1024,384]{1,0:T(8,128)(2,1)} %get-tuple-element.123.refs_2_.refs_3_.refs_8_, ...), custom_call_target="tpu_custom_call" | custom-call | flops 1 | bytes 1 | tf_op jit(solution)/shard_map/grads_send/pallas_call | solution.py:28
  322.2 1.7 copy-done.1
  324.0 4.1 halve.7
  329.6 9.9 %grads_keep.6 = (bf16[8,32,2304]{2,1,0:T(8,128)(2,1)}, bf16[8,32,2304]{2,1,0:T(8,128)(2,1)}) custom-call(s32[1,16]{1,0:T(1,128)} %get-tuple-element.186.refs_0_, s32[7,2]{1,0:T(8,128)} %call_exported.0.refs_1_, bf16[32,1,32,1024]{3,2,1,0:T(8,128)(2,1)} %bitcast.35, bf16[1024,384]{1,0:T(8,128)(2,1)} %get-tuple-element.123.refs_2_.refs_3_.refs_8_, ...), custom_call_target="tpu_custom_call" | custom-call | flops 1 | bytes 1 | tf_op jit(solution)/shard_map/grads_keep/pallas_call | solution.py:28
  340.7 10.0 %attention_back.5 = (bf16[1024,256]{1,0:T(8,128)(2,1)}, bf16[1024,256]{1,0:T(8,128)(2,1)}, bf16[1024,256]{1,0:T(8,128)(2,1)}) custom-call(s32[1]{0:T(128)S(6)} %copy.71.refs_0_, bf16[1024,3072]{1,0:T(8,128)(2,1)} %get-tuple-element.98.refs_1_.refs_2_.refs_3_, bf16[1024,3072]{1,0:T(8,128)(2,1)} %get-tuple-element.98.refs_1_.refs_2_.refs_3_, ...), custom_call_target="tpu_custom_call" | custom-call | flops 1 | bytes 1 | tf_op jit(solution)/shard_map/attention_back/pallas_call | solution.py:28
  351.3 4.5 %grads_send.7.refs_6_ = bf16[16,32,768]{2,1,0:T(8,128)(2,1)} custom-call(s32[1,16]{1,0:T(1,128)} %get-tuple-element.185.refs_0_, s32[4,1]{1,0:T(4,128)} %call_exported.1.refs_1_, bf16[32,1,32,1024]{3,2,1,0:T(8,128)(2,1)} %bitcast.36, bf16[1024,256]{1,0:T(8,128)(2,1)} %get-tuple-element.136.refs_3_.refs_6_.refs_14_, ...), custom_call_target="tpu_custom_call" | custom-call | flops 1 | bytes 1 | tf_op jit(solution)/shard_map/grads_send/pallas_call | solution.py:28
  355.9 4.2 collective-permute-start.30
  361.5 3.7 halve.8
  366.4 4.8 %grads_keep.7 = (bf16[8,32,768]{2,1,0:T(8,128)(2,1)}, bf16[8,32,768]{2,1,0:T(8,128)(2,1)}) custom-call(s32[1,16]{1,0:T(1,128)} %get-tuple-element.186.refs_0_, s32[4,1]{1,0:T(4,128)} %call_exported.1.refs_1_, bf16[32,1,32,1024]{3,2,1,0:T(8,128)(2,1)} %bitcast.37, bf16[1024,256]{1,0:T(8,128)(2,1)} %get-tuple-element.136.refs_3_.refs_6_.refs_14_, ...), custom_call_target="tpu_custom_call" | custom-call | flops 1 | bytes 1 | tf_op jit(solution)/shard_map/grads_keep/pallas_call | solution.py:28
  372.8 1.9 collective-permute-start.49
  376.2 16.8 %finish.1 = (f32[1024,1024]{1,0:T(8,128)}, f32[8,16,128]{2,1,0:T(8,128)}, f32[8,16,128]{2,1,0:T(8,128)}, f32[8,16,128]{2,1,0:T(8,128)}, f32[8,16,128]{2,1,0:T(8,128)}) custom-call(s32[2,32]{1,0:T(2,128)} %pad_add_fusion.refs_0_, s32[32]{0:T(128)} %copy-done.27, bf16[1024,1024]{1,0:T(8,128)(2,1)} %refs_2_.1, f32[1024,1024]{1,0:T(8,128)} %get-tuple-element.112.refs_3_, ...), custom_call_target="tpu_custom_call" | custom-call | flops 1 | bytes 1 | tf_op jit(solution)/shard_map/finish/pallas_call | solution.py:28
  393.0 2.7 halve.9
  396.6 1.7 collective-permute-start.41
  398.7 1.8 collective-permute-start.37
  403.3 3.5 collective-permute-done.42.refs_5_
  406.8 5.4 %collective-permute-done.37.refs_1_ = bf16[2,32,2304]{2,1,0:T(8,128)(2,1)S(1)} collective-permute-done((bf16[2,32,2304]{2,1,0:T(8,128)(2,1)}, bf16[2,32,2304]{2,1,0:T(8,128)(2,1)S(1)}, u32[]{:S(2)}, u32[]{:S(2)}) %collective-permute-start.37) | collective-permute-done | bytes 294944 | tf_op jit(solution)/shard_map/ppermute | solution.py:236
  412.2 1.9 halve.10
  414.1 2.4 collective-permute-start.43
  417.4 2.9 collective-permute-start.46
  422.8 2.2 collective-permute-start.45
  428.8 3.3 collective-permute-done.47
  (207 shorter events, 56.3 us)
Async XLA Ops:
  2.3 13.6 %collective-permute-start = (bf16[1,32,2176]{2,1,0:T(8,128)(2,1)S(1)}, bf16[1,32,2176]{2,1,0:T(8,128)(2,1)S(1)}, u32[]{:S(2)}, u32[]{:S(2)}) collective-permute-start(bf16[1,32,2176]{2,1,0:T(8,128)(2,1)S(1)} %fusion.6.refs_0_), channel_id=1, source_target_pairs={{0,16},{1,17},{2,18},{3,19},{4,20},{5,21},{6,22},{7,23},{8,24},{9,... | collective-permute-start | bytes 417800 | tf_op jit(solution)/shard_map/ppermute | solution.py:141
  7.3 8.6 %collective-permute-start.1 = (bf16[1,32,1024]{2,1,0:T(8,128)(2,1)S(1)}, bf16[1,32,1024]{2,1,0:T(8,128)(2,1)S(1)}, u32[]{:S(2)}, u32[]{:S(2)}) collective-permute-start(bf16[1,32,1024]{2,1,0:T(8,128)(2,1)S(1)} %slice_bitcast_fusion.refs_2_), channel_id=1, source_target_pairs={{0,16},{1,17},{2,18},{3,19},{4,20},{5,21},{6,22},{7,23},{8,24},{9,... | collective-permute-start | bytes 196616 | tf_op jit(solution)/shard_map/ppermute | solution.py:141
  17.6 6.8 %collective-permute-start.2 = (bf16[2,32,2176]{2,1,0:T(8,128)(2,1)}, bf16[2,32,2176]{2,1,0:T(8,128)(2,1)S(1)}, u32[]{:S(2)}, u32[]{:S(2)}) collective-permute-start(bf16[2,32,2176]{2,1,0:T(8,128)(2,1)} %get-tuple-element.92.refs_0_.refs_2_), channel_id=1, source_target_pairs={{0,1},{1,0},{2,6},{3,7},{4,5},{5,4},{6,2},{7,3},{8,9},{9,8},{10,14... | collective-permute-start | bytes 835592 | tf_op jit(solution)/shard_map/ppermute | solution.py:141
  19.2 5.2 %collective-permute-start.3 = (bf16[2,32,1024]{2,1,0:T(8,128)(2,1)}, bf16[2,32,1024]{2,1,0:T(8,128)(2,1)S(1)}, u32[]{:S(2)}, u32[]{:S(2)}) collective-permute-start(bf16[2,32,1024]{2,1,0:T(8,128)(2,1)} %get-tuple-element.93.refs_2_), channel_id=1, source_target_pairs={{0,8},{1,9},{2,10},{3,11},{4,12},{5,13},{6,14},{7,15},{8,0},{9,1},... | collective-permute-start | bytes 393224 | tf_op jit(solution)/shard_map/ppermute | solution.py:141
  20.5 26.1 %collective-permute-start.12 = (bf16[1,32,6144]{2,1,0:T(8,128)(2,1)}, bf16[1,32,6144]{2,1,0:T(8,128)(2,1)S(1)}, u32[]{:S(2)}, u32[]{:S(2)}) collective-permute-start(bf16[1,32,6144]{2,1,0:T(8,128)(2,1)} %get-tuple-element.99), channel_id=1, source_target_pairs={{0,16},{1,17},{2,18},{3,19},{4,20},{5,21},{6,22},{7,23},{8,24},{9,... | collective-permute-start | bytes 1179656 | tf_op jit(solution)/shard_map/ppermute | solution.py:141
  26.3 14.0 %collective-permute-start.4 = (bf16[4,32,2176]{2,1,0:T(8,128)(2,1)}, bf16[4,32,2176]{2,1,0:T(8,128)(2,1)S(1)}, u32[]{:S(2)}, u32[]{:S(2)}) collective-permute-start(bf16[4,32,2176]{2,1,0:T(8,128)(2,1)} %get-tuple-element.94.refs_0_), channel_id=1, source_target_pairs={{0,4},{1,5},{2,10},{3,11},{4,0},{5,1},{6,14},{7,15},{8,12},{9,13},... | collective-permute-start | bytes 1671176 | tf_op jit(solution)/shard_map/ppermute | solution.py:141
  29.4 20.5 %collective-permute-start.14 = (bf16[1,32,3072]{2,1,0:T(8,128)(2,1)}, bf16[1,32,3072]{2,1,0:T(8,128)(2,1)S(1)}, u32[]{:S(2)}, u32[]{:S(2)}) collective-permute-start(bf16[1,32,3072]{2,1,0:T(8,128)(2,1)} %get-tuple-element.100), channel_id=1, source_target_pairs={{0,16},{1,17},{2,18},{3,19},{4,20},{5,21},{6,22},{7,23},{8,24},{9,... | collective-permute-start | bytes 589832 | tf_op jit(solution)/shard_map/ppermute | solution.py:141
  32.3 7.9 %collective-permute-start.5 = (bf16[4,32,1024]{2,1,0:T(8,128)(2,1)}, bf16[4,32,1024]{2,1,0:T(8,128)(2,1)S(1)}, u32[]{:S(2)}, u32[]{:S(2)}) collective-permute-start(bf16[4,32,1024]{2,1,0:T(8,128)(2,1)} %get-tuple-element.95.refs_2_), channel_id=1, source_target_pairs={{0,1},{1,0},{2,3},{3,2},{4,5},{5,4},{6,7},{7,6},{8,9},{9,8},{10,11... | collective-permute-start | bytes 786440 | tf_op jit(solution)/shard_map/ppermute | solution.py:141
  42.6 27.5 %collective-permute-start.6 = (bf16[8,32,2176]{2,1,0:T(8,128)(2,1)}, bf16[8,32,2176]{2,1,0:T(8,128)(2,1)S(1)}, u32[]{:S(2)}, u32[]{:S(2)}) collective-permute-start(bf16[8,32,2176]{2,1,0:T(8,128)(2,1)} %get-tuple-element.96.refs_2_.refs_17_), channel_id=1, source_target_pairs={{0,8},{1,9},{2,3},{3,2},{4,12},{5,13},{6,7},{7,6},{8,0},{9,1},{10,... | collective-permute-start | bytes 3342344 | tf_op jit(solution)/shard_map/ppermute | solution.py:141
  46.7 23.9 %collective-permute-start.13 = (bf16[2,32,6144]{2,1,0:T(8,128)(2,1)S(1)}, bf16[2,32,6144]{2,1,0:T(8,128)(2,1)S(1)}, u32[]{:S(2)}, u32[]{:S(2)}) collective-permute-start(bf16[2,32,6144]{2,1,0:T(8,128)(2,1)S(1)} %pad_maximum_fusion), channel_id=1, source_target_pairs={{0,1},{1,0},{2,6},{3,7},{4,5},{5,4},{6,2},{7,3},{8,9},{9,8},{10,14... | collective-permute-start | bytes 2359304 | tf_op jit(solution)/shard_map/ppermute | solution.py:141
  49.9 20.2 %collective-permute-start.15 = (bf16[2,32,3072]{2,1,0:T(8,128)(2,1)S(1)}, bf16[2,32,3072]{2,1,0:T(8,128)(2,1)S(1)}, u32[]{:S(2)}, u32[]{:S(2)}) collective-permute-start(bf16[2,32,3072]{2,1,0:T(8,128)(2,1)S(1)} %pad_maximum_fusion.2), channel_id=1, source_target_pairs={{0,8},{1,9},{2,10},{3,11},{4,12},{5,13},{6,14},{7,15},{8,0},{9,1},... | collective-permute-start | bytes 1179656 | tf_op jit(solution)/shard_map/ppermute | solution.py:141
  50.0 20.7 %collective-permute-start.9 = (bf16[8,32,1024]{2,1,0:T(8,128)(2,1)}, bf16[8,32,1024]{2,1,0:T(8,128)(2,1)S(1)}, u32[]{:S(2)}, u32[]{:S(2)}) collective-permute-start(bf16[8,32,1024]{2,1,0:T(8,128)(2,1)} %get-tuple-element.97.refs_6_.refs_21_), channel_id=1, source_target_pairs={{0,4},{1,5},{2,6},{3,7},{4,0},{5,1},{6,2},{7,3},{8,12},{9,13},{10,... | collective-permute-start | bytes 1572872 | tf_op jit(solution)/shard_map/ppermute | solution.py:141
  50.7 26.8 %collective-permute-start.7 = (bf16[8,32,2176]{2,1,0:T(8,128)(2,1)S(1)}, bf16[8,32,2176]{2,1,0:T(8,128)(2,1)}, u32[]{:S(2)}, u32[]{:S(2)}) collective-permute-start(bf16[8,32,2176]{2,1,0:T(8,128)(2,1)S(1)} %copy-done.13), channel_id=1, source_target_pairs={{0,2},{1,3},{2,0},{3,1},{4,6},{5,7},{6,4},{7,5},{8,10},{9,11},{10,... | collective-permute-start | bytes 3342344 | tf_op jit(solution)/shard_map/ppermute | solution.py:146
  70.1 5.2 %collective-permute-start.10 = (bf16[8,32,1024]{2,1,0:T(8,128)(2,1)}, bf16[8,32,1024]{2,1,0:T(8,128)(2,1)}, u32[]{:S(2)}, u32[]{:S(2)}) collective-permute-start(bf16[8,32,1024]{2,1,0:T(8,128)(2,1)} %get-tuple-element.97.refs_6_.refs_21_), channel_id=1, source_target_pairs={{0,2},{1,3},{2,0},{3,1},{4,6},{5,7},{6,4},{7,5},{8,10},{9,11},{10,... | collective-permute-start | bytes 1572872 | tf_op jit(solution)/shard_map/ppermute | solution.py:146
  70.1 7.3 %collective-permute-start.8 = (bf16[8,32,2176]{2,1,0:T(8,128)(2,1)S(1)}, bf16[8,32,2176]{2,1,0:T(8,128)(2,1)}, u32[]{:S(2)}, u32[]{:S(2)}) collective-permute-start(bf16[8,32,2176]{2,1,0:T(8,128)(2,1)S(1)} %collective-permute-done.6.refs_3_.refs_2_.refs_18_), channel_id=1, source_target_pairs={{0,2},{1,3},{2,0},{3,1},{4,6},{5,7},{6,4},{7,5},{8,10},{9,11},{10,... | collective-permute-start | bytes 3342344 | tf_op jit(solution)/shard_map/ppermute | solution.py:149
  73.6 21.7 %collective-permute-start.16 = (bf16[4,32,6144]{2,1,0:T(8,128)(2,1)S(1)}, bf16[4,32,6144]{2,1,0:T(8,128)(2,1)S(1)}, u32[]{:S(2)}, u32[]{:S(2)}) collective-permute-start(bf16[4,32,6144]{2,1,0:T(8,128)(2,1)S(1)} %constant_dynamic-update-slice_fusion.refs_0_), channel_id=1, source_target_pairs={{0,4},{1,5},{2,10},{3,11},{4,0},{5,1},{6,14},{7,15},{8,12},{9,13},... | collective-permute-start | bytes 4718600 | tf_op jit(solution)/shard_map/ppermute | solution.py:141
  75.3 19.9 %collective-permute-start.17 = (bf16[4,32,3072]{2,1,0:T(8,128)(2,1)S(1)}, bf16[4,32,3072]{2,1,0:T(8,128)(2,1)S(1)}, u32[]{:S(2)}, u32[]{:S(2)}) collective-permute-start(bf16[4,32,3072]{2,1,0:T(8,128)(2,1)S(1)} %constant_dynamic-update-slice_fusion.3.refs_2_), channel_id=1, source_target_pairs={{0,1},{1,0},{2,3},{3,2},{4,5},{5,4},{6,7},{7,6},{8,9},{9,8},{10,11... | collective-permute-start | bytes 2359304 | tf_op jit(solution)/shard_map/ppermute | solution.py:141
  99.2 37.5 %collective-permute-start.18 = (bf16[8,32,6144]{2,1,0:T(8,128)(2,1)}, bf16[8,32,6144]{2,1,0:T(8,128)(2,1)S(1)}, u32[]{:S(2)}, u32[]{:S(2)}) collective-permute-start(bf16[8,32,6144]{2,1,0:T(8,128)(2,1)} %get-tuple-element.104.refs_4_.refs_7_), channel_id=1, source_target_pairs={{0,8},{1,9},{2,3},{3,2},{4,12},{5,13},{6,7},{7,6},{8,0},{9,1},{10,... | collective-permute-start | bytes 9437192 | tf_op jit(solution)/shard_map/ppermute | solution.py:141
  100.3 36.3 %collective-permute-start.19 = (bf16[8,32,3072]{2,1,0:T(8,128)(2,1)}, bf16[8,32,3072]{2,1,0:T(8,128)(2,1)S(1)}, u32[]{:S(2)}, u32[]{:S(2)}) collective-permute-start(bf16[8,32,3072]{2,1,0:T(8,128)(2,1)} %get-tuple-element.105.refs_5_.refs_11_), channel_id=1, source_target_pairs={{0,4},{1,5},{2,6},{3,7},{4,0},{5,1},{6,2},{7,3},{8,12},{9,13},{10,... | collective-permute-start | bytes 4718600 | tf_op jit(solution)/shard_map/ppermute | solution.py:141
  101.5 47.2 %collective-permute-start.20 = (bf16[8,32,6144]{2,1,0:T(8,128)(2,1)}, bf16[8,32,6144]{2,1,0:T(8,128)(2,1)}, u32[]{:S(2)}, u32[]{:S(2)}) collective-permute-start(bf16[8,32,6144]{2,1,0:T(8,128)(2,1)} %get-tuple-element.104.refs_4_.refs_7_), channel_id=1, source_target_pairs={{0,2},{1,3},{2,0},{3,1},{4,6},{5,7},{6,4},{7,5},{8,10},{9,11},{10,... | collective-permute-start | bytes 9437192 | tf_op jit(solution)/shard_map/ppermute | solution.py:146
  138.7 10.5 %collective-permute-start.21 = (bf16[8,32,6144]{2,1,0:T(8,128)(2,1)}, bf16[8,32,6144]{2,1,0:T(8,128)(2,1)}, u32[]{:S(2)}, u32[]{:S(2)}) collective-permute-start(bf16[8,32,6144]{2,1,0:T(8,128)(2,1)} %get-tuple-element.109.refs_8_), channel_id=1, source_target_pairs={{0,2},{1,3},{2,0},{3,1},{4,6},{5,7},{6,4},{7,5},{8,10},{9,11},{10,... | collective-permute-start | bytes 9437192 | tf_op jit(solution)/shard_map/ppermute | solution.py:149
  138.7 10.0 %collective-permute-start.22 = (bf16[8,32,3072]{2,1,0:T(8,128)(2,1)}, bf16[8,32,3072]{2,1,0:T(8,128)(2,1)S(1)}, u32[]{:S(2)}, u32[]{:S(2)}) collective-permute-start(bf16[8,32,3072]{2,1,0:T(8,128)(2,1)} %get-tuple-element.105.refs_5_.refs_11_), channel_id=1, source_target_pairs={{0,2},{1,3},{2,0},{3,1},{4,6},{5,7},{6,4},{7,5},{8,10},{9,11},{10,... | collective-permute-start | bytes 4718600 | tf_op jit(solution)/shard_map/ppermute | solution.py:146
  139.2 10.0 %collective-permute-start.23 = (bf16[8,32,3072]{2,1,0:T(8,128)(2,1)}, bf16[8,32,3072]{2,1,0:T(8,128)(2,1)}, u32[]{:S(2)}, u32[]{:S(2)}) collective-permute-start(bf16[8,32,3072]{2,1,0:T(8,128)(2,1)} %get-tuple-element.110.refs_12_), channel_id=1, source_target_pairs={{0,2},{1,3},{2,0},{3,1},{4,6},{5,7},{6,4},{7,5},{8,10},{9,11},{10,... | collective-permute-start | bytes 4718600 | tf_op jit(solution)/shard_map/ppermute | solution.py:149
  236.0 13.3 %collective-permute-start.25 = (bf16[16,32,4096]{2,1,0:T(8,128)(2,1)}, bf16[16,32,4096]{2,1,0:T(8,128)(2,1)}, u32[]{:S(2)}, u32[]{:S(2)}) collective-permute-start(bf16[16,32,4096]{2,1,0:T(8,128)(2,1)} %grads_send.4.refs_6_), channel_id=1, source_target_pairs={{0,2},{1,3},{2,0},{3,1},{4,6},{5,7},{6,4},{7,5},{8,10},{9,11},{10,... | collective-permute-start | bytes 12582920 | tf_op jit(solution)/shard_map/ppermute | solution.py:279
  249.2 12.7 %collective-permute-start.24 = (bf16[16,32,5120]{2,1,0:T(8,128)(2,1)}, bf16[16,32,5120]{2,1,0:T(8,128)(2,1)}, u32[]{:S(2)}, u32[]{:S(2)}) collective-permute-start(bf16[16,32,5120]{2,1,0:T(8,128)(2,1)} %grads_send.5.refs_5_), channel_id=1, source_target_pairs={{0,2},{1,3},{2,0},{3,1},{4,6},{5,7},{6,4},{7,5},{8,10},{9,11},{10,... | collective-permute-start | bytes 15728648 | tf_op jit(solution)/shard_map/ppermute | solution.py:279
  260.7 30.5 %collective-permute-start.26 = (bf16[8,32,4096]{2,1,0:T(8,128)(2,1)}, bf16[8,32,4096]{2,1,0:T(8,128)(2,1)S(1)}, u32[]{:S(2)}, u32[]{:S(2)}) collective-permute-start(bf16[8,32,4096]{2,1,0:T(8,128)(2,1)} %get-tuple-element.121.refs_7_), channel_id=1, source_target_pairs={{0,1},{1,0},{2,6},{3,7},{4,5},{5,4},{6,2},{7,3},{8,9},{9,8},{10,14... | collective-permute-start | bytes 6291464 | tf_op jit(solution)/shard_map/ppermute | solution.py:236
  276.2 44.5 %collective-permute-start.29 = (bf16[8,32,5120]{2,1,0:T(8,128)(2,1)}, bf16[8,32,5120]{2,1,0:T(8,128)(2,1)S(1)}, u32[]{:S(2)}, u32[]{:S(2)}) collective-permute-start(bf16[8,32,5120]{2,1,0:T(8,128)(2,1)} %get-tuple-element.122.refs_7_), channel_id=1, source_target_pairs={{0,1},{1,0},{2,6},{3,7},{4,5},{5,4},{6,2},{7,3},{8,9},{9,8},{10,14... | collective-permute-start | bytes 7864328 | tf_op jit(solution)/shard_map/ppermute | solution.py:236
  294.4 26.3 %collective-permute-start.28 = (bf16[4,32,4096]{2,1,0:T(8,128)(2,1)}, bf16[4,32,4096]{2,1,0:T(8,128)(2,1)S(1)}, u32[]{:S(2)}, u32[]{:S(2)}) collective-permute-start(bf16[4,32,4096]{2,1,0:T(8,128)(2,1)} %get-tuple-element.127.refs_7_), channel_id=1, source_target_pairs={{0,4},{1,5},{2,10},{3,11},{4,0},{5,1},{6,14},{7,15},{8,12},{9,13},... | collective-permute-start | bytes 3145736 | tf_op jit(solution)/shard_map/ppermute | solution.py:236
  319.1 10.5 %collective-permute-start.27 = (bf16[16,32,2304]{2,1,0:T(8,128)(2,1)}, bf16[16,32,2304]{2,1,0:T(8,128)(2,1)}, u32[]{:S(2)}, u32[]{:S(2)}) collective-permute-start(bf16[16,32,2304]{2,1,0:T(8,128)(2,1)} %grads_send.6.refs_4_), channel_id=1, source_target_pairs={{0,2},{1,3},{2,0},{3,1},{4,6},{5,7},{6,4},{7,5},{8,10},{9,11},{10,... | collective-permute-start | bytes 7077896 | tf_op jit(solution)/shard_map/ppermute | solution.py:279
  328.1 32.0 %collective-permute-start.32 = (bf16[4,32,5120]{2,1,0:T(8,128)(2,1)}, bf16[4,32,5120]{2,1,0:T(8,128)(2,1)S(1)}, u32[]{:S(2)}, u32[]{:S(2)}) collective-permute-start(bf16[4,32,5120]{2,1,0:T(8,128)(2,1)} %get-tuple-element.141), channel_id=1, source_target_pairs={{0,4},{1,5},{2,10},{3,11},{4,0},{5,1},{6,14},{7,15},{8,12},{9,13},... | collective-permute-start | bytes 3932168 | tf_op jit(solution)/shard_map/ppermute | solution.py:236
  339.5 22.0 %collective-permute-start.33 = (bf16[8,32,2304]{2,1,0:T(8,128)(2,1)}, bf16[8,32,2304]{2,1,0:T(8,128)(2,1)S(1)}, u32[]{:S(2)}, u32[]{:S(2)}) collective-permute-start(bf16[8,32,2304]{2,1,0:T(8,128)(2,1)} %get-tuple-element.135.refs_7_), channel_id=1, source_target_pairs={{0,1},{1,0},{2,6},{3,7},{4,5},{5,4},{6,2},{7,3},{8,9},{9,8},{10,14... | collective-permute-start | bytes 3538952 | tf_op jit(solution)/shard_map/ppermute | solution.py:236
  340.6 19.5 %collective-permute-start.31 = (bf16[2,32,4096]{2,1,0:T(8,128)(2,1)S(1)}, bf16[2,32,4096]{2,1,0:T(8,128)(2,1)S(1)}, u32[]{:S(2)}, u32[]{:S(2)}) collective-permute-start(bf16[2,32,4096]{2,1,0:T(8,128)(2,1)S(1)} %copy-done.17), channel_id=1, source_target_pairs={{0,8},{1,9},{2,3},{3,2},{4,12},{5,13},{6,7},{7,6},{8,0},{9,1},{10,... | collective-permute-start | bytes 1572872 | tf_op jit(solution)/shard_map/ppermute | solution.py:236
  355.9 10.5 %collective-permute-start.30 = (bf16[16,32,768]{2,1,0:T(8,128)(2,1)}, bf16[16,32,768]{2,1,0:T(8,128)(2,1)}, u32[]{:S(2)}, u32[]{:S(2)}) collective-permute-start(bf16[16,32,768]{2,1,0:T(8,128)(2,1)} %grads_send.7.refs_6_), channel_id=1, source_target_pairs={{0,2},{1,3},{2,0},{3,1},{4,6},{5,7},{6,4},{7,5},{8,10},{9,11},{10,... | collective-permute-start | bytes 2359304 | tf_op jit(solution)/shard_map/ppermute | solution.py:279
  365.2 27.8 %collective-permute-start.34 = (bf16[2,32,5120]{2,1,0:T(8,128)(2,1)}, bf16[2,32,5120]{2,1,0:T(8,128)(2,1)S(1)}, u32[]{:S(2)}, u32[]{:S(2)}) collective-permute-start(bf16[2,32,5120]{2,1,0:T(8,128)(2,1)} %get-tuple-element.147), channel_id=1, source_target_pairs={{0,8},{1,9},{2,3},{3,2},{4,12},{5,13},{6,7},{7,6},{8,0},{9,1},{10,... | collective-permute-start | bytes 1966088 | tf_op jit(solution)/shard_map/ppermute | solution.py:236
  365.5 27.5 %collective-permute-start.35 = (bf16[4,32,2304]{2,1,0:T(8,128)(2,1)}, bf16[4,32,2304]{2,1,0:T(8,128)(2,1)S(1)}, u32[]{:S(2)}, u32[]{:S(2)}) collective-permute-start(bf16[4,32,2304]{2,1,0:T(8,128)(2,1)} %get-tuple-element.149), channel_id=1, source_target_pairs={{0,4},{1,5},{2,10},{3,11},{4,0},{5,1},{6,14},{7,15},{8,12},{9,13},... | collective-permute-start | bytes 1769480 | tf_op jit(solution)/shard_map/ppermute | solution.py:236
  371.2 21.8 %collective-permute-start.36 = (bf16[8,32,768]{2,1,0:T(8,128)(2,1)}, bf16[8,32,768]{2,1,0:T(8,128)(2,1)S(1)}, u32[]{:S(2)}, u32[]{:S(2)}) collective-permute-start(bf16[8,32,768]{2,1,0:T(8,128)(2,1)} %get-tuple-element.144.refs_25_), channel_id=1, source_target_pairs={{0,1},{1,0},{2,6},{3,7},{4,5},{5,4},{6,2},{7,3},{8,9},{9,8},{10,14... | collective-permute-start | bytes 1179656 | tf_op jit(solution)/shard_map/ppermute | solution.py:236
  372.8 25.5 %collective-permute-start.49 = (bf16[1,32,4096]{2,1,0:T(8,128)(2,1)S(1)}, bf16[1,32,4096]{2,1,0:T(8,128)(2,1)S(1)}, u32[]{:S(2)}, u32[]{:S(2)}) collective-permute-start(bf16[1,32,4096]{2,1,0:T(8,128)(2,1)S(1)} %copy-done.19), channel_id=1, source_target_pairs={{0,16},{1,17},{2,18},{3,19},{4,20},{5,21},{6,22},{7,23},{8,24},{9,... | collective-permute-start | bytes 786440 | tf_op jit(solution)/shard_map/ppermute | solution.py:236
  395.7 4.8 %collective-permute-start.39 = (f32[8,16,128]{2,1,0:T(8,128)}, f32[8,16,128]{2,1,0:T(8,128)S(1)}, u32[]{:S(2)}, u32[]{:S(2)}) collective-permute-start(f32[8,16,128]{2,1,0:T(8,128)} %get-tuple-element.160), channel_id=1, source_target_pairs={{0,1},{1,0},{2,6},{3,7},{4,5},{5,4},{6,2},{7,3},{8,9},{9,8},{10,14... | collective-permute-start | bytes 196616 | tf_op jit(solution)/shard_map/ppermute | solution.py:1093
  396.6 5.5 %collective-permute-start.40 = (f32[8,16,128]{2,1,0:T(8,128)}, f32[8,16,128]{2,1,0:T(8,128)S(1)}, u32[]{:S(2)}, u32[]{:S(2)}) collective-permute-start(f32[8,16,128]{2,1,0:T(8,128)} %get-tuple-element.161), channel_id=1, source_target_pairs={{0,2},{1,3},{2,0},{3,1},{4,6},{5,7},{6,4},{7,5},{8,10},{9,11},{10,... | collective-permute-start | bytes 196616 | tf_op jit(solution)/shard_map/ppermute | solution.py:1093
  396.6 5.5 %collective-permute-start.41 = (f32[8,16,128]{2,1,0:T(8,128)}, f32[8,16,128]{2,1,0:T(8,128)S(1)}, u32[]{:S(2)}, u32[]{:S(2)}) collective-permute-start(f32[8,16,128]{2,1,0:T(8,128)} %get-tuple-element.162), channel_id=1, source_target_pairs={{0,6},{1,7},{2,1},{3,0},{4,2},{5,3},{6,5},{7,4},{8,14},{9,15},{10,... | collective-permute-start | bytes 196616 | tf_op jit(solution)/shard_map/ppermute | solution.py:1093
  398.4 26.7 %collective-permute-start.48 = (bf16[1,32,5120]{2,1,0:T(8,128)(2,1)}, bf16[1,32,5120]{2,1,0:T(8,128)(2,1)S(1)}, u32[]{:S(2)}, u32[]{:S(2)}) collective-permute-start(bf16[1,32,5120]{2,1,0:T(8,128)(2,1)} %get-tuple-element.159.refs_3_.refs_6_), channel_id=1, source_target_pairs={{0,16},{1,17},{2,18},{3,19},{4,20},{5,21},{6,22},{7,23},{8,24},{9,... | collective-permute-start | bytes 983048 | tf_op jit(solution)/shard_map/ppermute | solution.py:236
  398.7 13.5 %collective-permute-start.37 = (bf16[2,32,2304]{2,1,0:T(8,128)(2,1)}, bf16[2,32,2304]{2,1,0:T(8,128)(2,1)S(1)}, u32[]{:S(2)}, u32[]{:S(2)}) collective-permute-start(bf16[2,32,2304]{2,1,0:T(8,128)(2,1)} %get-tuple-element.152), channel_id=1, source_target_pairs={{0,8},{1,9},{2,3},{3,2},{4,12},{5,13},{6,7},{7,6},{8,0},{9,1},{10,... | collective-permute-start | bytes 884744 | tf_op jit(solution)/shard_map/ppermute | solution.py:236
  400.6 6.2 %collective-permute-start.38 = (bf16[4,32,768]{2,1,0:T(8,128)(2,1)}, bf16[4,32,768]{2,1,0:T(8,128)(2,1)S(1)}, u32[]{:S(2)}, u32[]{:S(2)}) collective-permute-start(bf16[4,32,768]{2,1,0:T(8,128)(2,1)} %get-tuple-element.154), channel_id=1, source_target_pairs={{0,4},{1,5},{2,10},{3,11},{4,0},{5,1},{6,14},{7,15},{8,12},{9,13},... | collective-permute-start | bytes 589832 | tf_op jit(solution)/shard_map/ppermute | solution.py:236
  414.1 7.2 %collective-permute-start.43 = (bf16[2,32,768]{2,1,0:T(8,128)(2,1)}, bf16[2,32,768]{2,1,0:T(8,128)(2,1)S(1)}, u32[]{:S(2)}, u32[]{:S(2)}) collective-permute-start(bf16[2,32,768]{2,1,0:T(8,128)(2,1)} %get-tuple-element.164), channel_id=1, source_target_pairs={{0,8},{1,9},{2,3},{3,2},{4,12},{5,13},{6,7},{7,6},{8,0},{9,1},{10,... | collective-permute-start | bytes 294920 | tf_op jit(solution)/shard_map/ppermute | solution.py:236
  416.5 4.7 %collective-permute-start.44 = (f32[2,16,128]{2,1,0:T(8,128)}, f32[2,16,128]{2,1,0:T(8,128)S(1)}, u32[]{:S(2)}, u32[]{:S(2)}) collective-permute-start(f32[2,16,128]{2,1,0:T(8,128)} %get-tuple-element.166), channel_id=1, source_target_pairs={{0,8},{1,9},{2,3},{3,2},{4,12},{5,13},{6,7},{7,6},{8,0},{9,1},{10,... | collective-permute-start | bytes 49160 | tf_op jit(solution)/shard_map/ppermute | solution.py:236
  417.4 11.3 %collective-permute-start.46 = (bf16[1,32,2304]{2,1,0:T(8,128)(2,1)}, bf16[1,32,2304]{2,1,0:T(8,128)(2,1)S(1)}, u32[]{:S(2)}, u32[]{:S(2)}) collective-permute-start(bf16[1,32,2304]{2,1,0:T(8,128)(2,1)} %get-tuple-element.167.refs_4_), channel_id=1, source_target_pairs={{0,16},{1,17},{2,18},{3,19},{4,20},{5,21},{6,22},{7,23},{8,24},{9,... | collective-permute-start | bytes 442376 | tf_op jit(solution)/shard_map/ppermute | solution.py:236
  422.8 4.8 %collective-permute-start.45 = (f32[1,16,128]{2,1,0:T(8,128)}, f32[1,16,128]{2,1,0:T(8,128)S(1)}, u32[]{:S(2)}, u32[]{:S(2)}) collective-permute-start(f32[1,16,128]{2,1,0:T(8,128)} %get-tuple-element.169), channel_id=1, source_target_pairs={{0,16},{1,17},{2,18},{3,19},{4,20},{5,21},{6,22},{7,23},{8,24},{9,... | collective-permute-start | bytes 24584 | tf_op jit(solution)/shard_map/ppermute | solution.py:236
  426.6 5.5 %collective-permute-start.47 = (bf16[1,32,768]{2,1,0:T(8,128)(2,1)S(1)}, bf16[1,32,768]{2,1,0:T(8,128)(2,1)S(1)}, u32[]{:S(2)}, u32[]{:S(2)}) collective-permute-start(bf16[1,32,768]{2,1,0:T(8,128)(2,1)S(1)} %copy-done.37), channel_id=1, source_target_pairs={{0,16},{1,17},{2,18},{3,19},{4,20},{5,21},{6,22},{7,23},{8,24},{9,... | collective-permute-start | bytes 147464 | tf_op jit(solution)/shard_map/ppermute | solution.py:236
  (40 other events, 356.1 us)

commit v4 on v3

--- a/solution.py
+++ b/solution.py
@@ -1086,7 +1086,7 @@
         n_hid,
         done,
     )
-    done = step_all([fc1_sum, sum_a, sum_b], [grad_tokens])
+    done = step_all([sum_a, sum_b], [grad_tokens])
     ways_out = (plan.pairs(0, 0, False), plan.core_pairs(), plan.corner_pairs(0))
     vec_all = vec_parts[0]
     for one, pairs_of in zip(relay(vec_parts[1:], done), ways_out):
@@ -1094,7 +1094,7 @@
     vec_sum = Scatter(plan, 0, None, None)
     vec_sum.at = 1
     vec_sum.send(vec_all[half // 4 :], vec_all[: half // 4])
-    done = step_all([sum_a, sum_b, vec_sum], done)
+    done = step_all([fc1_sum, sum_a, sum_b, vec_sum], done)
     step_all([sum_b, vec_sum], done)
     sent_vec = vec_sum.total()
     sent_a, sent_b = sum_a.total(), sum_b.total()

time: 441 us -> 456 us (1.034)
  waiting for transfers between devices: 76.3 us -> 92.4 us
    ppermute x19, waiting for transfers between devices: 16.5 us -> 32.7 us  [send(): lax.ppermute(going, AXES, self.plan.pairs(self.part, self.at, False))]
  transfers between devices with their start and end apart: 50 -> 50, of which waited for: 19 -> 19; matrix products, arithmetic and copies ran while one was open for 4% -> 4% of each run, Pallas kernels for 42% -> 39%
where the time goes in v4:
time: 456 us; the launch traced here: 448 us
  Pallas kernels  273 us (60%)
  waiting for transfers between devices  92.4 us (20%)
  starting transfers between devices  51.4 us (11%)
  local copies, waits for them, and re-layouts  23.3 us (5%)
  other arithmetic  6.43 us (1%)
    pallas_call x29, Pallas kernels, launch(): pl.pallas_call(body, grid_spec=pltpu.PrefetchScalarGridSpec(num_scalar_pr...  273 us
    ppermute x16, waiting for transfers between devices, step(): lax.ppermute(h, AXES, self.plan.pairs(part, self.at, True))  51.7 us
    ppermute x19, waiting for transfers between devices, send(): lax.ppermute(going, AXES, self.plan.pairs(self.part, self.at, False))  32.7 us
    ppermute x19, starting transfers between devices, send(): lax.ppermute(going, AXES, self.plan.pairs(self.part, self.at, False))  21.5 us
    ppermute x16, starting transfers between devices, step(): lax.ppermute(h, AXES, self.plan.pairs(part, self.at, True))  20.8 us
    unnamed x88, local copies, waits for them, and re-layouts  12.1 us
  transfers between devices with their start and end apart: 50, of which 19 were waited for; matrix products, arithmetic and copies ran while one was open for 4% of the time, Pallas kernels for 39%

profile of v4, /device:TPU:0, one launch (start us, length us, event | category | flops | bytes accessed | tf_op | source)
XLA Modules:
  0.0 448.4 jit_solution(14338681016849638632)
XLA Ops:
  2.3 4.1 collective-permute-start
  8.3 1.7 maximum_bitcast_fusion.refs_0_
  10.0 5.9 %collective-permute-done.1.refs_3_ = bf16[1,32,1024]{2,1,0:T(8,128)(2,1)S(1)} collective-permute-done((bf16[1,32,1024]{2,1,0:T(8,128)(2,1)S(1)}, bf16[1,32,1024]{2,1,0:T(8,128)(2,1)S(1)}, u32[]{:S(2)}, u32[]{:S(2)}) %collective-permute-start.1) | collective-permute-done | bytes 65568 | tf_op jit(solution)/shard_map/ppermute | solution.py:141
  15.9 1.7 join.4
  20.5 3.4 collective-permute-start.12
  24.4 1.9 join.5
  26.3 2.1 collective-permute-start.4
  29.4 3.0 collective-permute-start.14
  33.7 6.6 %collective-permute-done.5.refs_3_ = bf16[4,32,1024]{2,1,0:T(8,128)(2,1)S(1)} collective-permute-done((bf16[4,32,1024]{2,1,0:T(8,128)(2,1)}, bf16[4,32,1024]{2,1,0:T(8,128)(2,1)S(1)}, u32[]{:S(2)}, u32[]{:S(2)}) %collective-permute-start.5) | collective-permute-done | bytes 262176 | tf_op jit(solution)/shard_map/ppermute | solution.py:141
  40.3 2.4 join.6
  43.0 3.6 collective-permute-done.12
  47.5 2.4 collective-permute-done.14
  50.7 19.4 %collective-permute-done.15.refs_1_ = bf16[2,32,3072]{2,1,0:T(8,128)(2,1)S(1)} collective-permute-done((bf16[2,32,3072]{2,1,0:T(8,128)(2,1)S(1)}, bf16[2,32,3072]{2,1,0:T(8,128)(2,1)S(1)}, u32[]{:S(2)}, u32[]{:S(2)}) %collective-permute-start.15) | collective-permute-done | bytes 393248 | tf_op jit(solution)/shard_map/ppermute | solution.py:141
  78.3 15.1 %project.1 = (bf16[1024,3072]{1,0:T(8,128)(2,1)}, bf16[1024,1024]{1,0:T(8,128)(2,1)}, f32[16,1024]{1,0:T(8,128)}, f32[16,4096]{1,0:T(8,128)}) custom-call(s32[2,32]{1,0:T(2,128)} %pad_add_fusion.refs_0_, bf16[1024,1024]{1,0:T(8,128)(2,1)} %refs_2_.1, bf16[8,32,2176]{2,1,0:T(8,128)(2,1)} %get-tuple-element.96.refs_2_.refs_17_, ...), custom_call_target="tpu_custom_call" | custom-call | flops 6442450944 | bytes 18874368 | tf_op jit(solution)/shard_map/project/pallas_call | solution.py:28
  93.4 1.9 collective-permute-done.17.refs_3_
  95.3 3.9 join.7
  102.1 23.1 %attention.1 = (f32[1024,1024]{1,0:T(8,128)}, f32[8,2,1024]{2,1,0:T(2,128)}) custom-call(s32[1]{0:T(128)S(6)} %copy.71.refs_0_, bf16[1024,3072]{1,0:T(8,128)(2,1)} %get-tuple-element.98.refs_1_.refs_2_.refs_3_, bf16[1024,3072]{1,0:T(8,128)(2,1)} %get-tuple-element.98.refs_1_.refs_2_.refs_3_, bf16[1024,3072]{1,0:T(8,128)(2,1)} %get-tuple-element.98.refs_1_.refs_2_.refs_3_, ...), custom_call_target="tpu_custom_call" | custom-call | flops 12884901888 | bytes 10485760 | tf_op jit(solution)/shard_map/attention/pallas_call | solution.py:28
  125.2 11.4 %collective-permute-done.19.refs_1_ = bf16[8,32,3072]{2,1,0:T(8,128)(2,1)S(1)} collective-permute-done((bf16[8,32,3072]{2,1,0:T(8,128)(2,1)}, bf16[8,32,3072]{2,1,0:T(8,128)(2,1)S(1)}, u32[]{:S(2)}, u32[]{:S(2)}) %collective-permute-start.19) | collective-permute-done | bytes 1572896 | tf_op jit(solution)/shard_map/ppermute | solution.py:141
  141.2 7.5 %collective-permute-done.22.refs_13_ = bf16[8,32,3072]{2,1,0:T(8,128)(2,1)S(1)} collective-permute-done((bf16[8,32,3072]{2,1,0:T(8,128)(2,1)}, bf16[8,32,3072]{2,1,0:T(8,128)(2,1)S(1)}, u32[]{:S(2)}, u32[]{:S(2)}) %collective-permute-start.22) | collective-permute-done | bytes 1572896 | tf_op jit(solution)/shard_map/ppermute | solution.py:146
  149.9 76.0 %middle.1 = (bf16[1024,1024]{1,0:T(8,128)(2,1)}, bf16[1024,1024]{1,0:T(8,128)(2,1)}, bf16[1024,1024]{1,0:T(8,128)(2,1)}, bf16[4096,1024]{1,0:T(8,128)(2,1)}, bf1...) custom-call(s32[2,32]{1,0:T(2,128)} %pad_add_fusion.refs_0_, ...), custom_call_target="tpu_custom_call" | custom-call | flops 38654705664 | bytes 60817408 | tf_op jit(solution)/shard_map/middle/pallas_call | solution.py:28
  225.9 10.2 %grads_send.4.refs_6_ = bf16[16,32,4096]{2,1,0:T(8,128)(2,1)} custom-call(s32[1,16]{1,0:T(1,128)} %get-tuple-element.185.refs_0_, s32[2,4]{1,0:T(2,128)} %constant.65.clone.refs_1_, bf16[32,4,32,1024]{3,2,1,0:T(8,128)(2,1)} %bitcast.38, bf16[1024,1024]{1,0:T(8,128)(2,1)} %refs_3_.5), custom_call_target="tpu_custom_call" | custom-call | flops 1 | bytes 1 | tf_op jit(solution)/shard_map/grads_send/pallas_call | solution.py:28
  236.4 12.8 %grads_send.5.refs_5_ = bf16[16,32,5120]{2,1,0:T(8,128)(2,1)} custom-call(s32[1,16]{1,0:T(1,128)} %get-tuple-element.185.refs_0_, s32[4,5]{1,0:T(4,128)} %constant.66.clone.refs_1_, bf16[32,1,32,1024]{3,2,1,0:T(8,128)(2,1)} %bitcast.42, bf16[32,1,32,1024]{3,2,1,0:T(8,128)(2,1)} %bitcast.40, bf16[1024,4096]{1,0:T(8,128)(2,1)} %get-tuple-element.118.refs_4_, ...), custom_call_target="tpu_custom_call" | custom-call | flops 999999995904 | bytes 1 | tf_op jit(solution)/shard_map/grads_send/pallas_call | solution.py:28
  249.3 11.4 %grads_keep.4 = (bf16[8,32,4096]{2,1,0:T(8,128)(2,1)}, bf16[8,32,4096]{2,1,0:T(8,128)(2,1)}) custom-call(s32[1,16]{1,0:T(1,128)} %get-tuple-element.186.refs_0_, s32[2,4]{1,0:T(2,128)} %constant.65.clone.refs_1_, bf16[32,4,32,1024]{3,2,1,0:T(8,128)(2,1)} %bitcast.39, bf16[1024,1024]{1,0:T(8,128)(2,1)} %refs_3_.5, ...), custom_call_target="tpu_custom_call" | custom-call | flops 999999995904 | bytes 1 | tf_op jit(solution)/shard_map/grads_keep/pallas_call | solution.py:28
  261.9 14.3 %grads_keep.5 = (bf16[8,32,5120]{2,1,0:T(8,128)(2,1)}, bf16[8,32,5120]{2,1,0:T(8,128)(2,1)}) custom-call(s32[1,16]{1,0:T(1,128)} %get-tuple-element.186.refs_0_, s32[4,5]{1,0:T(4,128)} %constant.66.clone.refs_1_, bf16[32,1,32,1024]{3,2,1,0:T(8,128)(2,1)} %bitcast.43, bf16[32,1,32,1024]{3,2,1,0:T(8,128)(2,1)} %bitcast.41, ...), custom_call_target="tpu_custom_call" | custom-call | flops 1 | bytes 1 | tf_op jit(solution)/shard_map/grads_keep/pallas_call | solution.py:28
  277.1 14.1 %attention_back.3 = (bf16[1024,384]{1,0:T(8,128)(2,1)}, bf16[1024,384]{1,0:T(8,128)(2,1)}, bf16[1024,384]{1,0:T(8,128)(2,1)}) custom-call(s32[1]{0:T(128)S(6)} %copy.71.refs_0_, bf16[1024,3072]{1,0:T(8,128)(2,1)} %get-tuple-element.98.refs_1_.refs_2_.refs_3_, bf16[1024,3072]{1,0:T(8,128)(2,1)} %get-tuple-element.98.refs_1_.refs_2_.refs_3_, ...), custom_call_target="tpu_custom_call" | custom-call | flops 1 | bytes 1 | tf_op jit(solution)/shard_map/attention_back/pallas_call | solution.py:28
  291.2 3.1 halve.6
  295.9 13.9 %attention_back.4 = (bf16[1024,384]{1,0:T(8,128)(2,1)}, bf16[1024,384]{1,0:T(8,128)(2,1)}, bf16[1024,384]{1,0:T(8,128)(2,1)}) custom-call(s32[1]{0:T(128)S(6)} %copy.71.refs_0_, bf16[1024,3072]{1,0:T(8,128)(2,1)} %get-tuple-element.98.refs_1_.refs_2_.refs_3_, bf16[1024,3072]{1,0:T(8,128)(2,1)} %get-tuple-element.98.refs_1_.refs_2_.refs_3_, ...), custom_call_target="tpu_custom_call" | custom-call | flops 1 | bytes 1 | tf_op jit(solution)/shard_map/attention_back/pallas_call | solution.py:28
  310.5 8.8 %grads_send.6.refs_4_ = bf16[16,32,2304]{2,1,0:T(8,128)(2,1)} custom-call(s32[1,16]{1,0:T(1,128)} %get-tuple-element.185.refs_0_, s32[7,2]{1,0:T(8,128)} %call_exported.0.refs_1_, bf16[32,1,32,1024]{3,2,1,0:T(8,128)(2,1)} %bitcast.34, bf16[1024,384]{1,0:T(8,128)(2,1)} %get-tuple-element.123.refs_2_.refs_3_.refs_8_, ...), custom_call_target="tpu_custom_call" | custom-call | flops 1 | bytes 1 | tf_op jit(solution)/shard_map/grads_send/pallas_call | solution.py:28
  322.2 1.7 copy-done.1
  324.0 4.1 halve.7
  329.6 10.0 %grads_keep.6 = (bf16[8,32,2304]{2,1,0:T(8,128)(2,1)}, bf16[8,32,2304]{2,1,0:T(8,128)(2,1)}) custom-call(s32[1,16]{1,0:T(1,128)} %get-tuple-element.186.refs_0_, s32[7,2]{1,0:T(8,128)} %call_exported.0.refs_1_, bf16[32,1,32,1024]{3,2,1,0:T(8,128)(2,1)} %bitcast.35, bf16[1024,384]{1,0:T(8,128)(2,1)} %get-tuple-element.123.refs_2_.refs_3_.refs_8_, ...), custom_call_target="tpu_custom_call" | custom-call | flops 1 | bytes 1 | tf_op jit(solution)/shard_map/grads_keep/pallas_call | solution.py:28
  340.8 10.0 %attention_back.5 = (bf16[1024,256]{1,0:T(8,128)(2,1)}, bf16[1024,256]{1,0:T(8,128)(2,1)}, bf16[1024,256]{1,0:T(8,128)(2,1)}) custom-call(s32[1]{0:T(128)S(6)} %copy.71.refs_0_, bf16[1024,3072]{1,0:T(8,128)(2,1)} %get-tuple-element.98.refs_1_.refs_2_.refs_3_, bf16[1024,3072]{1,0:T(8,128)(2,1)} %get-tuple-element.98.refs_1_.refs_2_.refs_3_, ...), custom_call_target="tpu_custom_call" | custom-call | flops 1 | bytes 1 | tf_op jit(solution)/shard_map/attention_back/pallas_call | solution.py:28
  351.4 4.5 %grads_send.7.refs_6_ = bf16[16,32,768]{2,1,0:T(8,128)(2,1)} custom-call(s32[1,16]{1,0:T(1,128)} %get-tuple-element.185.refs_0_, s32[4,1]{1,0:T(4,128)} %call_exported.1.refs_1_, bf16[32,1,32,1024]{3,2,1,0:T(8,128)(2,1)} %bitcast.36, bf16[1024,256]{1,0:T(8,128)(2,1)} %get-tuple-element.136.refs_3_.refs_6_.refs_14_, ...), custom_call_target="tpu_custom_call" | custom-call | flops 1 | bytes 1 | tf_op jit(solution)/shard_map/grads_send/pallas_call | solution.py:28
  356.0 4.2 collective-permute-start.30
  361.6 3.6 halve.8
  365.8 4.7 %grads_keep.7 = (bf16[8,32,768]{2,1,0:T(8,128)(2,1)}, bf16[8,32,768]{2,1,0:T(8,128)(2,1)}) custom-call(s32[1,16]{1,0:T(1,128)} %get-tuple-element.186.refs_0_, s32[4,1]{1,0:T(4,128)} %call_exported.1.refs_1_, bf16[32,1,32,1024]{3,2,1,0:T(8,128)(2,1)} %bitcast.37, bf16[1024,256]{1,0:T(8,128)(2,1)} %get-tuple-element.136.refs_3_.refs_6_.refs_14_, ...), custom_call_target="tpu_custom_call" | custom-call | flops 1 | bytes 1 | tf_op jit(solution)/shard_map/grads_keep/pallas_call | solution.py:28
  373.2 16.8 %finish.1 = (f32[1024,1024]{1,0:T(8,128)}, f32[8,16,128]{2,1,0:T(8,128)}, f32[8,16,128]{2,1,0:T(8,128)}, f32[8,16,128]{2,1,0:T(8,128)}, f32[8,16,128]{2,1,0:T(8,128)}) custom-call(s32[2,32]{1,0:T(2,128)} %pad_add_fusion.refs_0_, s32[32]{0:T(128)} %copy-done.27, bf16[1024,1024]{1,0:T(8,128)(2,1)} %refs_2_.1, f32[1024,1024]{1,0:T(8,128)} %get-tuple-element.112.refs_3_, ...), custom_call_target="tpu_custom_call" | custom-call | flops 1 | bytes 1 | tf_op jit(solution)/shard_map/finish/pallas_call | solution.py:28
  390.0 2.3 halve.9
  396.1 1.8 collective-permute-start.34
  401.2 8.1 %collective-permute-done.49 = bf16[1,32,4096]{2,1,0:T(8,128)(2,1)S(1)} collective-permute-done((bf16[1,32,4096]{2,1,0:T(8,128)(2,1)S(1)}, bf16[1,32,4096]{2,1,0:T(8,128)(2,1)S(1)}, u32[]{:S(2)}, u32[]{:S(2)}) %collective-permute-start.49) | collective-permute-done | bytes 262176 | tf_op jit(solution)/shard_map/ppermute | solution.py:236
  409.4 4.7 %collective-permute-done.34.refs_1_ = bf16[2,32,5120]{2,1,0:T(8,128)(2,1)S(1)} collective-permute-done((bf16[2,32,5120]{2,1,0:T(8,128)(2,1)S(1)}, bf16[2,32,5120]{2,1,0:T(8,128)(2,1)S(1)}, u32[]{:S(2)}, u32[]{:S(2)}) %collective-permute-start.34) | collective-permute-done | bytes 655392 | tf_op jit(solution)/shard_map/ppermute | solution.py:236
  414.1 3.2 collective-permute-done.37.refs_3_
  417.2 2.4 halve.10
  419.8 1.9 collective-permute-start.44
  421.7 3.8 collective-permute-done.44.refs_3_
  428.4 2.4 collective-permute-start.48
  431.3 2.4 collective-permute-start.47
  435.6 9.5 %collective-permute-done.46 = bf16[1,32,2304]{2,1,0:T(8,128)(2,1)S(1)} collective-permute-done((bf16[1,32,2304]{2,1,0:T(8,128)(2,1)S(1)}, bf16[1,32,2304]{2,1,0:T(8,128)(2,1)S(1)}, u32[]{:S(2)}, u32[]{:S(2)}) %collective-permute-start.46) | collective-permute-done | bytes 147488 | tf_op jit(solution)/shard_map/ppermute | solution.py:236
  (207 shorter events, 58.5 us)
Async XLA Ops:
  2.3 13.6 %collective-permute-start = (bf16[1,32,2176]{2,1,0:T(8,128)(2,1)S(1)}, bf16[1,32,2176]{2,1,0:T(8,128)(2,1)S(1)}, u32[]{:S(2)}, u32[]{:S(2)}) collective-permute-start(bf16[1,32,2176]{2,1,0:T(8,128)(2,1)S(1)} %fusion.6.refs_0_), channel_id=1, source_target_pairs={{0,16},{1,17},{2,18},{3,19},{4,20},{5,21},{6,22},{7,23},{8,24},{9,... | collective-permute-start | bytes 417800 | tf_op jit(solution)/shard_map/ppermute | solution.py:141
  7.3 8.6 %collective-permute-start.1 = (bf16[1,32,1024]{2,1,0:T(8,128)(2,1)S(1)}, bf16[1,32,1024]{2,1,0:T(8,128)(2,1)S(1)}, u32[]{:S(2)}, u32[]{:S(2)}) collective-permute-start(bf16[1,32,1024]{2,1,0:T(8,128)(2,1)S(1)} %slice_bitcast_fusion.refs_2_), channel_id=1, source_target_pairs={{0,16},{1,17},{2,18},{3,19},{4,20},{5,21},{6,22},{7,23},{8,24},{9,... | collective-permute-start | bytes 196616 | tf_op jit(solution)/shard_map/ppermute | solution.py:141
  17.6 6.8 %collective-permute-start.2 = (bf16[2,32,2176]{2,1,0:T(8,128)(2,1)}, bf16[2,32,2176]{2,1,0:T(8,128)(2,1)S(1)}, u32[]{:S(2)}, u32[]{:S(2)}) collective-permute-start(bf16[2,32,2176]{2,1,0:T(8,128)(2,1)} %get-tuple-element.92.refs_0_.refs_2_), channel_id=1, source_target_pairs={{0,1},{1,0},{2,6},{3,7},{4,5},{5,4},{6,2},{7,3},{8,9},{9,8},{10,14... | collective-permute-start | bytes 835592 | tf_op jit(solution)/shard_map/ppermute | solution.py:141
  20.5 26.1 %collective-permute-start.12 = (bf16[1,32,6144]{2,1,0:T(8,128)(2,1)}, bf16[1,32,6144]{2,1,0:T(8,128)(2,1)S(1)}, u32[]{:S(2)}, u32[]{:S(2)}) collective-permute-start(bf16[1,32,6144]{2,1,0:T(8,128)(2,1)} %get-tuple-element.99), channel_id=1, source_target_pairs={{0,16},{1,17},{2,18},{3,19},{4,20},{5,21},{6,22},{7,23},{8,24},{9,... | collective-permute-start | bytes 1179656 | tf_op jit(solution)/shard_map/ppermute | solution.py:141
  26.3 14.0 %collective-permute-start.4 = (bf16[4,32,2176]{2,1,0:T(8,128)(2,1)}, bf16[4,32,2176]{2,1,0:T(8,128)(2,1)S(1)}, u32[]{:S(2)}, u32[]{:S(2)}) collective-permute-start(bf16[4,32,2176]{2,1,0:T(8,128)(2,1)} %get-tuple-element.94.refs_0_), channel_id=1, source_target_pairs={{0,4},{1,5},{2,10},{3,11},{4,0},{5,1},{6,14},{7,15},{8,12},{9,13},... | collective-permute-start | bytes 1671176 | tf_op jit(solution)/shard_map/ppermute | solution.py:141
  29.4 20.5 %collective-permute-start.14 = (bf16[1,32,3072]{2,1,0:T(8,128)(2,1)}, bf16[1,32,3072]{2,1,0:T(8,128)(2,1)S(1)}, u32[]{:S(2)}, u32[]{:S(2)}) collective-permute-start(bf16[1,32,3072]{2,1,0:T(8,128)(2,1)} %get-tuple-element.100), channel_id=1, source_target_pairs={{0,16},{1,17},{2,18},{3,19},{4,20},{5,21},{6,22},{7,23},{8,24},{9,... | collective-permute-start | bytes 589832 | tf_op jit(solution)/shard_map/ppermute | solution.py:141
  32.3 7.9 %collective-permute-start.5 = (bf16[4,32,1024]{2,1,0:T(8,128)(2,1)}, bf16[4,32,1024]{2,1,0:T(8,128)(2,1)S(1)}, u32[]{:S(2)}, u32[]{:S(2)}) collective-permute-start(bf16[4,32,1024]{2,1,0:T(8,128)(2,1)} %get-tuple-element.95.refs_2_), channel_id=1, source_target_pairs={{0,1},{1,0},{2,3},{3,2},{4,5},{5,4},{6,7},{7,6},{8,9},{9,8},{10,11... | collective-permute-start | bytes 786440 | tf_op jit(solution)/shard_map/ppermute | solution.py:141
  42.6 27.5 %collective-permute-start.6 = (bf16[8,32,2176]{2,1,0:T(8,128)(2,1)}, bf16[8,32,2176]{2,1,0:T(8,128)(2,1)S(1)}, u32[]{:S(2)}, u32[]{:S(2)}) collective-permute-start(bf16[8,32,2176]{2,1,0:T(8,128)(2,1)} %get-tuple-element.96.refs_2_.refs_17_), channel_id=1, source_target_pairs={{0,8},{1,9},{2,3},{3,2},{4,12},{5,13},{6,7},{7,6},{8,0},{9,1},{10,... | collective-permute-start | bytes 3342344 | tf_op jit(solution)/shard_map/ppermute | solution.py:141
  46.7 23.9 %collective-permute-start.13 = (bf16[2,32,6144]{2,1,0:T(8,128)(2,1)S(1)}, bf16[2,32,6144]{2,1,0:T(8,128)(2,1)S(1)}, u32[]{:S(2)}, u32[]{:S(2)}) collective-permute-start(bf16[2,32,6144]{2,1,0:T(8,128)(2,1)S(1)} %pad_maximum_fusion), channel_id=1, source_target_pairs={{0,1},{1,0},{2,6},{3,7},{4,5},{5,4},{6,2},{7,3},{8,9},{9,8},{10,14... | collective-permute-start | bytes 2359304 | tf_op jit(solution)/shard_map/ppermute | solution.py:141
  49.9 20.2 %collective-permute-start.15 = (bf16[2,32,3072]{2,1,0:T(8,128)(2,1)S(1)}, bf16[2,32,3072]{2,1,0:T(8,128)(2,1)S(1)}, u32[]{:S(2)}, u32[]{:S(2)}) collective-permute-start(bf16[2,32,3072]{2,1,0:T(8,128)(2,1)S(1)} %pad_maximum_fusion.2), channel_id=1, source_target_pairs={{0,8},{1,9},{2,10},{3,11},{4,12},{5,13},{6,14},{7,15},{8,0},{9,1},... | collective-permute-start | bytes 1179656 | tf_op jit(solution)/shard_map/ppermute | solution.py:141
  50.0 20.7 %collective-permute-start.9 = (bf16[8,32,1024]{2,1,0:T(8,128)(2,1)}, bf16[8,32,1024]{2,1,0:T(8,128)(2,1)S(1)}, u32[]{:S(2)}, u32[]{:S(2)}) collective-permute-start(bf16[8,32,1024]{2,1,0:T(8,128)(2,1)} %get-tuple-element.97.refs_6_.refs_21_), channel_id=1, source_target_pairs={{0,4},{1,5},{2,6},{3,7},{4,0},{5,1},{6,2},{7,3},{8,12},{9,13},{10,... | collective-permute-start | bytes 1572872 | tf_op jit(solution)/shard_map/ppermute | solution.py:141
  50.7 26.8 %collective-permute-start.7 = (bf16[8,32,2176]{2,1,0:T(8,128)(2,1)S(1)}, bf16[8,32,2176]{2,1,0:T(8,128)(2,1)}, u32[]{:S(2)}, u32[]{:S(2)}) collective-permute-start(bf16[8,32,2176]{2,1,0:T(8,128)(2,1)S(1)} %copy-done.13), channel_id=1, source_target_pairs={{0,2},{1,3},{2,0},{3,1},{4,6},{5,7},{6,4},{7,5},{8,10},{9,11},{10,... | collective-permute-start | bytes 3342344 | tf_op jit(solution)/shard_map/ppermute | solution.py:146
  70.1 5.2 %collective-permute-start.10 = (bf16[8,32,1024]{2,1,0:T(8,128)(2,1)}, bf16[8,32,1024]{2,1,0:T(8,128)(2,1)}, u32[]{:S(2)}, u32[]{:S(2)}) collective-permute-start(bf16[8,32,1024]{2,1,0:T(8,128)(2,1)} %get-tuple-element.97.refs_6_.refs_21_), channel_id=1, source_target_pairs={{0,2},{1,3},{2,0},{3,1},{4,6},{5,7},{6,4},{7,5},{8,10},{9,11},{10,... | collective-permute-start | bytes 1572872 | tf_op jit(solution)/shard_map/ppermute | solution.py:146
  70.1 7.3 %collective-permute-start.8 = (bf16[8,32,2176]{2,1,0:T(8,128)(2,1)S(1)}, bf16[8,32,2176]{2,1,0:T(8,128)(2,1)}, u32[]{:S(2)}, u32[]{:S(2)}) collective-permute-start(bf16[8,32,2176]{2,1,0:T(8,128)(2,1)S(1)} %collective-permute-done.6.refs_3_.refs_2_.refs_18_), channel_id=1, source_target_pairs={{0,2},{1,3},{2,0},{3,1},{4,6},{5,7},{6,4},{7,5},{8,10},{9,11},{10,... | collective-permute-start | bytes 3342344 | tf_op jit(solution)/shard_map/ppermute | solution.py:149
  73.6 21.7 %collective-permute-start.16 = (bf16[4,32,6144]{2,1,0:T(8,128)(2,1)S(1)}, bf16[4,32,6144]{2,1,0:T(8,128)(2,1)S(1)}, u32[]{:S(2)}, u32[]{:S(2)}) collective-permute-start(bf16[4,32,6144]{2,1,0:T(8,128)(2,1)S(1)} %constant_dynamic-update-slice_fusion.refs_0_), channel_id=1, source_target_pairs={{0,4},{1,5},{2,10},{3,11},{4,0},{5,1},{6,14},{7,15},{8,12},{9,13},... | collective-permute-start | bytes 4718600 | tf_op jit(solution)/shard_map/ppermute | solution.py:141
  75.3 19.9 %collective-permute-start.17 = (bf16[4,32,3072]{2,1,0:T(8,128)(2,1)S(1)}, bf16[4,32,3072]{2,1,0:T(8,128)(2,1)S(1)}, u32[]{:S(2)}, u32[]{:S(2)}) collective-permute-start(bf16[4,32,3072]{2,1,0:T(8,128)(2,1)S(1)} %constant_dynamic-update-slice_fusion.3.refs_2_), channel_id=1, source_target_pairs={{0,1},{1,0},{2,3},{3,2},{4,5},{5,4},{6,7},{7,6},{8,9},{9,8},{10,11... | collective-permute-start | bytes 2359304 | tf_op jit(solution)/shard_map/ppermute | solution.py:141
  99.2 37.5 %collective-permute-start.18 = (bf16[8,32,6144]{2,1,0:T(8,128)(2,1)}, bf16[8,32,6144]{2,1,0:T(8,128)(2,1)S(1)}, u32[]{:S(2)}, u32[]{:S(2)}) collective-permute-start(bf16[8,32,6144]{2,1,0:T(8,128)(2,1)} %get-tuple-element.104.refs_4_.refs_7_), channel_id=1, source_target_pairs={{0,8},{1,9},{2,3},{3,2},{4,12},{5,13},{6,7},{7,6},{8,0},{9,1},{10,... | collective-permute-start | bytes 9437192 | tf_op jit(solution)/shard_map/ppermute | solution.py:141
  100.3 36.3 %collective-permute-start.19 = (bf16[8,32,3072]{2,1,0:T(8,128)(2,1)}, bf16[8,32,3072]{2,1,0:T(8,128)(2,1)S(1)}, u32[]{:S(2)}, u32[]{:S(2)}) collective-permute-start(bf16[8,32,3072]{2,1,0:T(8,128)(2,1)} %get-tuple-element.105.refs_5_.refs_11_), channel_id=1, source_target_pairs={{0,4},{1,5},{2,6},{3,7},{4,0},{5,1},{6,2},{7,3},{8,12},{9,13},{10,... | collective-permute-start | bytes 4718600 | tf_op jit(solution)/shard_map/ppermute | solution.py:141
  101.5 47.2 %collective-permute-start.20 = (bf16[8,32,6144]{2,1,0:T(8,128)(2,1)}, bf16[8,32,6144]{2,1,0:T(8,128)(2,1)}, u32[]{:S(2)}, u32[]{:S(2)}) collective-permute-start(bf16[8,32,6144]{2,1,0:T(8,128)(2,1)} %get-tuple-element.104.refs_4_.refs_7_), channel_id=1, source_target_pairs={{0,2},{1,3},{2,0},{3,1},{4,6},{5,7},{6,4},{7,5},{8,10},{9,11},{10,... | collective-permute-start | bytes 9437192 | tf_op jit(solution)/shard_map/ppermute | solution.py:146
  138.7 10.5 %collective-permute-start.21 = (bf16[8,32,6144]{2,1,0:T(8,128)(2,1)}, bf16[8,32,6144]{2,1,0:T(8,128)(2,1)}, u32[]{:S(2)}, u32[]{:S(2)}) collective-permute-start(bf16[8,32,6144]{2,1,0:T(8,128)(2,1)} %get-tuple-element.109.refs_8_), channel_id=1, source_target_pairs={{0,2},{1,3},{2,0},{3,1},{4,6},{5,7},{6,4},{7,5},{8,10},{9,11},{10,... | collective-permute-start | bytes 9437192 | tf_op jit(solution)/shard_map/ppermute | solution.py:149
  138.7 10.0 %collective-permute-start.22 = (bf16[8,32,3072]{2,1,0:T(8,128)(2,1)}, bf16[8,32,3072]{2,1,0:T(8,128)(2,1)S(1)}, u32[]{:S(2)}, u32[]{:S(2)}) collective-permute-start(bf16[8,32,3072]{2,1,0:T(8,128)(2,1)} %get-tuple-element.105.refs_5_.refs_11_), channel_id=1, source_target_pairs={{0,2},{1,3},{2,0},{3,1},{4,6},{5,7},{6,4},{7,5},{8,10},{9,11},{10,... | collective-permute-start | bytes 4718600 | tf_op jit(solution)/shard_map/ppermute | solution.py:146
  139.2 10.0 %collective-permute-start.23 = (bf16[8,32,3072]{2,1,0:T(8,128)(2,1)}, bf16[8,32,3072]{2,1,0:T(8,128)(2,1)}, u32[]{:S(2)}, u32[]{:S(2)}) collective-permute-start(bf16[8,32,3072]{2,1,0:T(8,128)(2,1)} %get-tuple-element.110.refs_12_), channel_id=1, source_target_pairs={{0,2},{1,3},{2,0},{3,1},{4,6},{5,7},{6,4},{7,5},{8,10},{9,11},{10,... | collective-permute-start | bytes 4718600 | tf_op jit(solution)/shard_map/ppermute | solution.py:149
  236.0 13.3 %collective-permute-start.25 = (bf16[16,32,4096]{2,1,0:T(8,128)(2,1)}, bf16[16,32,4096]{2,1,0:T(8,128)(2,1)}, u32[]{:S(2)}, u32[]{:S(2)}) collective-permute-start(bf16[16,32,4096]{2,1,0:T(8,128)(2,1)} %grads_send.4.refs_6_), channel_id=1, source_target_pairs={{0,2},{1,3},{2,0},{3,1},{4,6},{5,7},{6,4},{7,5},{8,10},{9,11},{10,... | collective-permute-start | bytes 12582920 | tf_op jit(solution)/shard_map/ppermute | solution.py:279
  249.2 12.7 %collective-permute-start.24 = (bf16[16,32,5120]{2,1,0:T(8,128)(2,1)}, bf16[16,32,5120]{2,1,0:T(8,128)(2,1)}, u32[]{:S(2)}, u32[]{:S(2)}) collective-permute-start(bf16[16,32,5120]{2,1,0:T(8,128)(2,1)} %grads_send.5.refs_5_), channel_id=1, source_target_pairs={{0,2},{1,3},{2,0},{3,1},{4,6},{5,7},{6,4},{7,5},{8,10},{9,11},{10,... | collective-permute-start | bytes 15728648 | tf_op jit(solution)/shard_map/ppermute | solution.py:279
  260.7 30.5 %collective-permute-start.26 = (bf16[8,32,4096]{2,1,0:T(8,128)(2,1)}, bf16[8,32,4096]{2,1,0:T(8,128)(2,1)S(1)}, u32[]{:S(2)}, u32[]{:S(2)}) collective-permute-start(bf16[8,32,4096]{2,1,0:T(8,128)(2,1)} %get-tuple-element.121.refs_7_), channel_id=1, source_target_pairs={{0,1},{1,0},{2,6},{3,7},{4,5},{5,4},{6,2},{7,3},{8,9},{9,8},{10,14... | collective-permute-start | bytes 6291464 | tf_op jit(solution)/shard_map/ppermute | solution.py:236
  276.2 44.5 %collective-permute-start.29 = (bf16[8,32,5120]{2,1,0:T(8,128)(2,1)}, bf16[8,32,5120]{2,1,0:T(8,128)(2,1)S(1)}, u32[]{:S(2)}, u32[]{:S(2)}) collective-permute-start(bf16[8,32,5120]{2,1,0:T(8,128)(2,1)} %get-tuple-element.122.refs_7_), channel_id=1, source_target_pairs={{0,1},{1,0},{2,6},{3,7},{4,5},{5,4},{6,2},{7,3},{8,9},{9,8},{10,14... | collective-permute-start | bytes 7864328 | tf_op jit(solution)/shard_map/ppermute | solution.py:236
  294.4 26.3 %collective-permute-start.28 = (bf16[4,32,4096]{2,1,0:T(8,128)(2,1)}, bf16[4,32,4096]{2,1,0:T(8,128)(2,1)S(1)}, u32[]{:S(2)}, u32[]{:S(2)}) collective-permute-start(bf16[4,32,4096]{2,1,0:T(8,128)(2,1)} %get-tuple-element.127.refs_7_), channel_id=1, source_target_pairs={{0,4},{1,5},{2,10},{3,11},{4,0},{5,1},{6,14},{7,15},{8,12},{9,13},... | collective-permute-start | bytes 3145736 | tf_op jit(solution)/shard_map/ppermute | solution.py:236
  319.3 10.3 %collective-permute-start.27 = (bf16[16,32,2304]{2,1,0:T(8,128)(2,1)}, bf16[16,32,2304]{2,1,0:T(8,128)(2,1)}, u32[]{:S(2)}, u32[]{:S(2)}) collective-permute-start(bf16[16,32,2304]{2,1,0:T(8,128)(2,1)} %grads_send.6.refs_4_), channel_id=1, source_target_pairs={{0,2},{1,3},{2,0},{3,1},{4,6},{5,7},{6,4},{7,5},{8,10},{9,11},{10,... | collective-permute-start | bytes 7077896 | tf_op jit(solution)/shard_map/ppermute | solution.py:279
  328.1 32.1 %collective-permute-start.32 = (bf16[4,32,5120]{2,1,0:T(8,128)(2,1)}, bf16[4,32,5120]{2,1,0:T(8,128)(2,1)S(1)}, u32[]{:S(2)}, u32[]{:S(2)}) collective-permute-start(bf16[4,32,5120]{2,1,0:T(8,128)(2,1)} %get-tuple-element.141), channel_id=1, source_target_pairs={{0,4},{1,5},{2,10},{3,11},{4,0},{5,1},{6,14},{7,15},{8,12},{9,13},... | collective-permute-start | bytes 3932168 | tf_op jit(solution)/shard_map/ppermute | solution.py:236
  339.6 22.0 %collective-permute-start.33 = (bf16[8,32,2304]{2,1,0:T(8,128)(2,1)}, bf16[8,32,2304]{2,1,0:T(8,128)(2,1)S(1)}, u32[]{:S(2)}, u32[]{:S(2)}) collective-permute-start(bf16[8,32,2304]{2,1,0:T(8,128)(2,1)} %get-tuple-element.135.refs_7_), channel_id=1, source_target_pairs={{0,1},{1,0},{2,6},{3,7},{4,5},{5,4},{6,2},{7,3},{8,9},{9,8},{10,14... | collective-permute-start | bytes 3538952 | tf_op jit(solution)/shard_map/ppermute | solution.py:236
  340.7 19.5 %collective-permute-start.31 = (bf16[2,32,4096]{2,1,0:T(8,128)(2,1)S(1)}, bf16[2,32,4096]{2,1,0:T(8,128)(2,1)S(1)}, u32[]{:S(2)}, u32[]{:S(2)}) collective-permute-start(bf16[2,32,4096]{2,1,0:T(8,128)(2,1)S(1)} %copy-done.17), channel_id=1, source_target_pairs={{0,8},{1,9},{2,3},{3,2},{4,12},{5,13},{6,7},{7,6},{8,0},{9,1},{10,... | collective-permute-start | bytes 1572872 | tf_op jit(solution)/shard_map/ppermute | solution.py:236
  356.0 9.8 %collective-permute-start.30 = (bf16[16,32,768]{2,1,0:T(8,128)(2,1)}, bf16[16,32,768]{2,1,0:T(8,128)(2,1)}, u32[]{:S(2)}, u32[]{:S(2)}) collective-permute-start(bf16[16,32,768]{2,1,0:T(8,128)(2,1)} %grads_send.7.refs_6_), channel_id=1, source_target_pairs={{0,2},{1,3},{2,0},{3,1},{4,6},{5,7},{6,4},{7,5},{8,10},{9,11},{10,... | collective-permute-start | bytes 2359304 | tf_op jit(solution)/shard_map/ppermute | solution.py:279
  365.3 24.7 %collective-permute-start.35 = (bf16[4,32,2304]{2,1,0:T(8,128)(2,1)}, bf16[4,32,2304]{2,1,0:T(8,128)(2,1)S(1)}, u32[]{:S(2)}, u32[]{:S(2)}) collective-permute-start(bf16[4,32,2304]{2,1,0:T(8,128)(2,1)} %get-tuple-element.149), channel_id=1, source_target_pairs={{0,4},{1,5},{2,10},{3,11},{4,0},{5,1},{6,14},{7,15},{8,12},{9,13},... | collective-permute-start | bytes 1769480 | tf_op jit(solution)/shard_map/ppermute | solution.py:236
  370.5 19.5 %collective-permute-start.36 = (bf16[8,32,768]{2,1,0:T(8,128)(2,1)}, bf16[8,32,768]{2,1,0:T(8,128)(2,1)S(1)}, u32[]{:S(2)}, u32[]{:S(2)}) collective-permute-start(bf16[8,32,768]{2,1,0:T(8,128)(2,1)} %get-tuple-element.144.refs_25_), channel_id=1, source_target_pairs={{0,1},{1,0},{2,6},{3,7},{4,5},{5,4},{6,2},{7,3},{8,9},{9,8},{10,14... | collective-permute-start | bytes 1179656 | tf_op jit(solution)/shard_map/ppermute | solution.py:236
  392.3 5.5 %collective-permute-start.39 = (f32[8,16,128]{2,1,0:T(8,128)}, f32[8,16,128]{2,1,0:T(8,128)S(1)}, u32[]{:S(2)}, u32[]{:S(2)}) collective-permute-start(f32[8,16,128]{2,1,0:T(8,128)} %get-tuple-element.159), channel_id=1, source_target_pairs={{0,1},{1,0},{2,6},{3,7},{4,5},{5,4},{6,2},{7,3},{8,9},{9,8},{10,14... | collective-permute-start | bytes 196616 | tf_op jit(solution)/shard_map/ppermute | solution.py:1093
  393.2 5.3 %collective-permute-start.40 = (f32[8,16,128]{2,1,0:T(8,128)}, f32[8,16,128]{2,1,0:T(8,128)S(1)}, u32[]{:S(2)}, u32[]{:S(2)}) collective-permute-start(f32[8,16,128]{2,1,0:T(8,128)} %get-tuple-element.160), channel_id=1, source_target_pairs={{0,2},{1,3},{2,0},{3,1},{4,6},{5,7},{6,4},{7,5},{8,10},{9,11},{10,... | collective-permute-start | bytes 196616 | tf_op jit(solution)/shard_map/ppermute | solution.py:1093
  393.2 5.7 %collective-permute-start.41 = (f32[8,16,128]{2,1,0:T(8,128)}, f32[8,16,128]{2,1,0:T(8,128)S(1)}, u32[]{:S(2)}, u32[]{:S(2)}) collective-permute-start(f32[8,16,128]{2,1,0:T(8,128)} %get-tuple-element.161), channel_id=1, source_target_pairs={{0,6},{1,7},{2,1},{3,0},{4,2},{5,3},{6,5},{7,4},{8,14},{9,15},{10,... | collective-permute-start | bytes 196616 | tf_op jit(solution)/shard_map/ppermute | solution.py:1093
  394.9 14.4 %collective-permute-start.49 = (bf16[1,32,4096]{2,1,0:T(8,128)(2,1)S(1)}, bf16[1,32,4096]{2,1,0:T(8,128)(2,1)S(1)}, u32[]{:S(2)}, u32[]{:S(2)}) collective-permute-start(bf16[1,32,4096]{2,1,0:T(8,128)(2,1)S(1)} %copy-done.20), channel_id=1, source_target_pairs={{0,16},{1,17},{2,18},{3,19},{4,20},{5,21},{6,22},{7,23},{8,24},{9,... | collective-permute-start | bytes 786440 | tf_op jit(solution)/shard_map/ppermute | solution.py:236
  396.1 18.0 %collective-permute-start.34 = (bf16[2,32,5120]{2,1,0:T(8,128)(2,1)S(1)}, bf16[2,32,5120]{2,1,0:T(8,128)(2,1)S(1)}, u32[]{:S(2)}, u32[]{:S(2)}) collective-permute-start(bf16[2,32,5120]{2,1,0:T(8,128)(2,1)S(1)} %copy-done.36), channel_id=1, source_target_pairs={{0,8},{1,9},{2,3},{3,2},{4,12},{5,13},{6,7},{7,6},{8,0},{9,1},{10,... | collective-permute-start | bytes 1966088 | tf_op jit(solution)/shard_map/ppermute | solution.py:236
  397.8 19.4 %collective-permute-start.37 = (bf16[2,32,2304]{2,1,0:T(8,128)(2,1)}, bf16[2,32,2304]{2,1,0:T(8,128)(2,1)S(1)}, u32[]{:S(2)}, u32[]{:S(2)}) collective-permute-start(bf16[2,32,2304]{2,1,0:T(8,128)(2,1)} %get-tuple-element.152.refs_3_.refs_8_), channel_id=1, source_target_pairs={{0,8},{1,9},{2,3},{3,2},{4,12},{5,13},{6,7},{7,6},{8,0},{9,1},{10,... | collective-permute-start | bytes 884744 | tf_op jit(solution)/shard_map/ppermute | solution.py:236
  398.5 15.6 %collective-permute-start.38 = (bf16[4,32,768]{2,1,0:T(8,128)(2,1)}, bf16[4,32,768]{2,1,0:T(8,128)(2,1)S(1)}, u32[]{:S(2)}, u32[]{:S(2)}) collective-permute-start(bf16[4,32,768]{2,1,0:T(8,128)(2,1)} %get-tuple-element.154), channel_id=1, source_target_pairs={{0,4},{1,5},{2,10},{3,11},{4,0},{5,1},{6,14},{7,15},{8,12},{9,13},... | collective-permute-start | bytes 589832 | tf_op jit(solution)/shard_map/ppermute | solution.py:236
  399.6 14.5 %collective-permute-start.42 = (f32[4,16,128]{2,1,0:T(8,128)S(1)}, f32[4,16,128]{2,1,0:T(8,128)S(1)}, u32[]{:S(2)}, u32[]{:S(2)}) collective-permute-start(f32[4,16,128]{2,1,0:T(8,128)S(1)} %get-tuple-element.183), channel_id=1, source_target_pairs={{0,4},{1,5},{2,10},{3,11},{4,0},{5,1},{6,14},{7,15},{8,12},{9,13},... | collective-permute-start | bytes 98312 | tf_op jit(solution)/shard_map/ppermute | solution.py:236
  419.6 5.9 %collective-permute-start.43 = (bf16[2,32,768]{2,1,0:T(8,128)(2,1)}, bf16[2,32,768]{2,1,0:T(8,128)(2,1)S(1)}, u32[]{:S(2)}, u32[]{:S(2)}) collective-permute-start(bf16[2,32,768]{2,1,0:T(8,128)(2,1)} %get-tuple-element.163), channel_id=1, source_target_pairs={{0,8},{1,9},{2,3},{3,2},{4,12},{5,13},{6,7},{7,6},{8,0},{9,1},{10,... | collective-permute-start | bytes 294920 | tf_op jit(solution)/shard_map/ppermute | solution.py:236
  419.8 5.7 %collective-permute-start.44 = (f32[2,16,128]{2,1,0:T(8,128)}, f32[2,16,128]{2,1,0:T(8,128)S(1)}, u32[]{:S(2)}, u32[]{:S(2)}) collective-permute-start(f32[2,16,128]{2,1,0:T(8,128)} %get-tuple-element.165), channel_id=1, source_target_pairs={{0,8},{1,9},{2,3},{3,2},{4,12},{5,13},{6,7},{7,6},{8,0},{9,1},{10,... | collective-permute-start | bytes 49160 | tf_op jit(solution)/shard_map/ppermute | solution.py:236
  427.1 6.7 %collective-permute-start.45 = (f32[1,16,128]{2,1,0:T(8,128)}, f32[1,16,128]{2,1,0:T(8,128)S(1)}, u32[]{:S(2)}, u32[]{:S(2)}) collective-permute-start(f32[1,16,128]{2,1,0:T(8,128)} %get-tuple-element.168), channel_id=1, source_target_pairs={{0,16},{1,17},{2,18},{3,19},{4,20},{5,21},{6,22},{7,23},{8,24},{9,... | collective-permute-start | bytes 24584 | tf_op jit(solution)/shard_map/ppermute | solution.py:236
  428.4 18.1 %collective-permute-start.48 = (bf16[1,32,5120]{2,1,0:T(8,128)(2,1)S(1)}, bf16[1,32,5120]{2,1,0:T(8,128)(2,1)S(1)}, u32[]{:S(2)}, u32[]{:S(2)}) collective-permute-start(bf16[1,32,5120]{2,1,0:T(8,128)(2,1)S(1)} %copy-done.19), channel_id=1, source_target_pairs={{0,16},{1,17},{2,18},{3,19},{4,20},{5,21},{6,22},{7,23},{8,24},{9,... | collective-permute-start | bytes 983048 | tf_op jit(solution)/shard_map/ppermute | solution.py:236
  430.8 14.2 %collective-permute-start.46 = (bf16[1,32,2304]{2,1,0:T(8,128)(2,1)S(1)}, bf16[1,32,2304]{2,1,0:T(8,128)(2,1)S(1)}, u32[]{:S(2)}, u32[]{:S(2)}) collective-permute-start(bf16[1,32,2304]{2,1,0:T(8,128)(2,1)S(1)} %copy-done.37), channel_id=1, source_target_pairs={{0,16},{1,17},{2,18},{3,19},{4,20},{5,21},{6,22},{7,23},{8,24},{9,... | collective-permute-start | bytes 442376 | tf_op jit(solution)/shard_map/ppermute | solution.py:236
  431.3 14.3 %collective-permute-start.47 = (bf16[1,32,768]{2,1,0:T(8,128)(2,1)}, bf16[1,32,768]{2,1,0:T(8,128)(2,1)S(1)}, u32[]{:S(2)}, u32[]{:S(2)}) collective-permute-start(bf16[1,32,768]{2,1,0:T(8,128)(2,1)} %get-tuple-element.172), channel_id=1, source_target_pairs={{0,16},{1,17},{2,18},{3,19},{4,20},{5,21},{6,22},{7,23},{8,24},{9,... | collective-permute-start | bytes 147464 | tf_op jit(solution)/shard_map/ppermute | solution.py:236
  (40 other events, 402.4 us)
